TPU v7x, 128 devices: a whole 4x4x4 slice. The times are simulated.
128 devices in a mesh: pipe: 4 (over y), expert: 32 (over z, x, core).
Axes of the slice: x: 4, y: 4, z: 4, core: 2. Of those that a mesh axis runs over, the one named last changes fastest.
Arguments:
- acts: bfloat16 [4, 4096, 3072], P('pipe', 'expert'), may hold values from -6 to 6
- hid_grad: bfloat16 [4, 4096, 2, 8192], P('pipe', 'expert'), may hold values from -6 to 6
- routes: int32 [4, 4096, 2], P('pipe', 'expert'), may hold values from 0 to 7, all different within a row; in each aligned block of 128 rows (0 to 127, 128 to 255, ..., all dimensions but the last counted through in order) at most 64 rows name the same one
- probs: float32 [4, 4096, 2], P('pipe', 'expert'), may hold values from 0.1 to 0.9
- w_gate: bfloat16 [4, 32, 3072, 2048], P('pipe', 'expert'), may hold values from -0.109375 to 0.109375
Outputs:
- in_grad: bfloat16 [4, 4096, 3072], P('pipe', 'expert')
Inputs may be any that keep to these rules, and one draw needn't show every extreme that they name: `routes`: each token names 2 different experts. Among the 128 tokens of one device in one section, no expert is named more than 64 times, and in every draw some device names some expert exactly 64 times.
All inputs are finite; a program needn't handle non-finite values.
Results may differ from a plain program's by a relative error of at most 0.013.
Values may be sent and summed in bfloat16 or wider, within the bound.
No kernel may reach another device: no remote copies, remote signals or barrier semaphores. Data moves between devices by JAX's collectives and lax.ppermute only.
A program may use at most 192 MiB of HBM per device.

v0:
```python
import jax
import jax.numpy as jnp
from jax import lax
from jax.experimental import pallas as pl
from jax.experimental.pallas import tpu as pltpu
from jax.sharding import Mesh, PartitionSpec as P

EXPERTS = 8
TOP = 2
SLOTS = 64
PLANE = ("z", "xp", "p", "core")
DEVICES = 32
SHARE = SLOTS // 2
BACK = [((i + 1) % 4, i) for i in range(4)]
COLUMN_PARTS = 2
VMEM = 56 * 1024 * 1024


def exchange(block):
    return lax.all_to_all(block, PLANE, split_axis=0, concat_axis=0, tiled=True)


def derivative(gate_pre):
    squash = jax.nn.sigmoid(gate_pre)
    return (squash * (1.0 + gate_pre * (1.0 - squash))).astype(jnp.bfloat16)


def bf16_dot(a, b, dims):
    return lax.dot_general(a, b, (dims, ((), ())), preferred_element_type=jnp.float32)


def place_kernel(target_ref, grads_ref, out_ref):
    tokens, top, columns = grads_ref.shape
    places = lax.broadcasted_iota(jnp.int32, (EXPERTS * SLOTS, tokens * top), 0)
    hit = jnp.where(places == target_ref[...], 1.0, 0.0).astype(jnp.bfloat16)
    grads = grads_ref[...].reshape(tokens * top, columns)
    placed = jnp.dot(hit, grads, preferred_element_type=jnp.float32).astype(jnp.bfloat16)
    out_ref[:, 0] = placed.reshape(EXPERTS, 2, SHARE, columns)


def place(target, grads):
    tokens, top, width = grads.shape
    pairs, hidden = tokens * top, width // 2
    columns = 1024
    steps = hidden // columns
    out = pl.pallas_call(
        place_kernel,
        grid=(2, steps),
        in_specs=[
            pl.BlockSpec((1, pairs), lambda p, j: (0, 0)),
            pl.BlockSpec((tokens, top, columns), lambda p, j: (0, 0, p * steps + j)),
        ],
        out_specs=pl.BlockSpec((EXPERTS, 1, 2, SHARE, columns), lambda p, j: (0, p, 0, 0, j)),
        out_shape=jax.ShapeDtypeStruct((EXPERTS, 2, 2, SHARE, hidden), jnp.bfloat16),
        compiler_params=pltpu.CompilerParams(vmem_limit_bytes=VMEM),
        cost_estimate=pl.CostEstimate(
            flops=4 * EXPERTS * SLOTS * pairs * hidden,
            bytes_accessed=4 * (EXPERTS * SLOTS + pairs) * hidden,
            transcendentals=0,
        ),
        name="place_grads",
    )(target.reshape(1, pairs), grads)
    return out.reshape(DEVICES, SHARE, hidden)


SOURCES = 4


def pick_kernel(base_ref, target_ref, tokens_ref, out_ref):
    n_tokens = tokens_ref.shape[1]
    wanted = base_ref[0] + lax.broadcasted_iota(jnp.int32, (SHARE, n_tokens), 0)
    for i in range(SOURCES):
        hit = (wanted == target_ref[i, 0:1]) | (wanted == target_ref[i, 1:2])
        hit = jnp.where(hit, 1.0, 0.0).astype(jnp.bfloat16)
        rows = jnp.dot(hit, tokens_ref[i], preferred_element_type=jnp.float32)
        out_ref[i] = rows.astype(jnp.bfloat16)


def pick(base, targets, tokens):
    sources, n_tokens, width = tokens.shape
    return pl.pallas_call(
        pick_kernel,
        grid=(sources // SOURCES,),
        in_specs=[
            pl.BlockSpec(memory_space=pltpu.SMEM),
            pl.BlockSpec((SOURCES, TOP, n_tokens), lambda i: (i, 0, 0)),
            pl.BlockSpec((SOURCES, n_tokens, width), lambda i: (i, 0, 0)),
        ],
        out_specs=pl.BlockSpec((SOURCES, SHARE, width), lambda i: (i, 0, 0)),
        out_shape=jax.ShapeDtypeStruct((sources, SHARE, width), jnp.bfloat16),
        compiler_params=pltpu.CompilerParams(vmem_limit_bytes=VMEM),
        cost_estimate=pl.CostEstimate(
            flops=2 * sources * SHARE * n_tokens * width,
            bytes_accessed=2 * sources * (SHARE + n_tokens) * width,
            transcendentals=0,
        ),
        name="pick_rows",
    )(base.reshape(1), targets, tokens)


DEEP = 1024


def term_kernel(g0, g1, s0, s1, w0, w1, out_ref, gate, total):
    j, k = pl.program_id(0), pl.program_id(1)

    @pl.when(j == 0)
    def _():
        for half, (g, s) in enumerate(((g0, s0), (g1, s1))):
            product = g[...].astype(jnp.float32) * s[...].astype(jnp.float32)
            gate[2 * k + half] = product.astype(jnp.bfloat16)

    def part(half, w):
        return bf16_dot(gate[2 * k + half], w[...], ((1,), (1,)))

    @pl.when(k == 0)
    def _():
        total[...] = part(0, w0) + part(1, w1)

    @pl.when(k == 1)
    def _():
        out_ref[...] = (total[...] + part(0, w0) + part(1, w1)).astype(jnp.bfloat16)


def terms(grads, slopes, weights, first, columns):
    rows, hidden = grads[0].shape
    wide = 768
    steps, offset = columns // wide, first // wide
    side = pl.BlockSpec((rows, DEEP), lambda j, k: (0, jnp.where(j == 0, k, 1)))
    weight = pl.BlockSpec((wide, DEEP), lambda j, k: (offset + j, k))
    return pl.pallas_call(
        term_kernel,
        grid=(steps, hidden // DEEP),
        in_specs=[side] * 4 + [weight] * 2,
        out_specs=pl.BlockSpec((rows, wide), lambda j, k: (0, j)),
        out_shape=jax.ShapeDtypeStruct((rows, columns), jnp.bfloat16),
        scratch_shapes=[
            pltpu.VMEM((4, rows, DEEP), jnp.bfloat16),
            pltpu.VMEM((rows, wide), jnp.float32),
        ],
        compiler_params=pltpu.CompilerParams(vmem_limit_bytes=VMEM),
        cost_estimate=pl.CostEstimate(
            flops=4 * rows * hidden * columns,
            bytes_accessed=8 * rows * hidden + 4 * hidden * columns + 2 * rows * columns,
            transcendentals=0,
        ),
        name="terms",
    )(*grads, *slopes, *weights)


def local(acts, hid_grad, routes, probs, w_gate):
    tokens = acts[0]
    n_tokens, width = tokens.shape
    mine = w_gate[0, 0]
    hidden = mine.shape[1]
    core = lax.axis_index("core")
    expert = lax.axis_index("z") * 2 + lax.axis_index("xp")

    halves = []
    for h in range(2):
        pieces = [hid_grad[0][:, :, f * hidden : (f + 1) * hidden] for f in (h, 2 + h)]
        halves.append(lax.ppermute(jnp.concatenate(pieces, axis=2), "pipe", BACK))
    gathered = lax.all_gather(tokens, PLANE, axis=0)
    other = lax.ppermute(mine, "core", [(0, 1), (1, 0)])

    flat_expert = routes[0].reshape(-1)
    pairs = flat_expert.shape[0]
    number = jnp.arange(pairs, dtype=jnp.int32)
    earlier = (flat_expert[:, None] == flat_expert[None, :]) & (number[None, :] < number[:, None])
    slot = jnp.sum(earlier.astype(jnp.int32), axis=1)
    target = flat_expert * SLOTS + slot
    by_token = target.reshape(n_tokens, TOP)
    targets = lax.all_gather(by_token.T, PLANE, axis=0)

    received = []
    for h in range(2):
        received.append(exchange(place(target, halves[h])).reshape(DEVICES * SHARE, hidden))

    gathered, received[0] = lax.optimization_barrier((gathered, received[0]))
    weights = (jnp.where(core == 0, mine, other), jnp.where(core == 0, other, mine))
    rows = pick(expert * SLOTS + core * SHARE, targets, gathered).reshape(DEVICES * SHARE, width)
    slopes = [
        lax.optimization_barrier(derivative(bf16_dot(rows, w, ((1,), (0,))))) for w in weights
    ]

    places = jnp.arange(EXPERTS * SLOTS, dtype=jnp.int32).reshape(EXPERTS, 1, SLOTS)
    places = jnp.broadcast_to(places, (EXPERTS, 2, SLOTS)).reshape(-1)
    hit = [by_token[:, k, None] == places[None, :] for k in range(TOP)]
    mix = sum(jnp.where(hit[k], probs[0][:, k, None], 0.0) for k in range(TOP))
    high = lax.reduce_precision(mix, 8, 7)
    mix = jnp.concatenate([high, mix - high]).astype(jnp.bfloat16)

    columns = width // COLUMN_PARTS
    parts = []
    for j in range(COLUMN_PARTS):
        term = terms(received, slopes, weights, j * columns, columns)
        returned = exchange(term.reshape(DEVICES, SHARE, columns)).reshape(-1, columns)
        both = bf16_dot(mix, returned, ((1,), (0,)))
        summed = (both[:n_tokens] + both[n_tokens:]).astype(jnp.bfloat16)
        parts.append(lax.ppermute(summed, "pipe", BACK))
    return jnp.concatenate(parts, axis=1)[None]


def solution(mesh):
    fine = Mesh(mesh.devices.reshape(4, 4, 2, 2, 2), ("pipe",) + PLANE)
    placed = (
        P("pipe", PLANE, None),
        P("pipe", PLANE, None, None),
        P("pipe", PLANE, None),
        P("pipe", PLANE, None),
        P("pipe", PLANE, None, None),
    )
    return jax.shard_map(
        local, mesh=fine, in_specs=placed, out_specs=P("pipe", PLANE, None), check_vma=False
    )
```

profile of v0, /device:TPU:24, one launch (start us, length us, event | category | flops | bytes accessed | tf_op | source)
XLA Modules:
  0.0 383.8 jit_solution(13365039128664414619)
XLA Ops:
  6.5 0.7 all-gather.4.cloned.1.call-update
  7.4 4.6 %fusion.8 = (bf16[128,2,2048]{2,1,0:T(2,128)(2,1)S(1)}, bf16[128,2,2048]{2,1,0:T(2,128)(2,1)S(1)}, bf16[128,2,2048]{2,1,0:T(2,128)(2,1)S(1)}, bf16[128,2,2048]{2,1,0:T(2,128)(2,1)S(1)}) fusion(bf16[128,2,8192]{2,1,0:T(2,128)(2,1)} %bitcast.41), kind=kLoop, calls=%fused_computation.30 | loop fusion | bytes 8388608 | tf_op jit(solution)/shard_map/slice | solution.py:161
  12.0 3.9 %pad_maximum_fusion = bf16[128,2,4096]{2,1,0:T(2,128)(2,1)} fusion(bf16[128,2,2048]{2,1,0:T(2,128)(2,1)S(1)} %get-tuple-element.15, bf16[128,2,2048]{2,1,0:T(2,128)(2,1)S(1)} %get-tuple-element.16), kind=kLoop, calls=%fused_computation.4 | loop fusion | flops 4194304 | bytes 4194304 | tf_op jit(solution)/shard_map/concatenate | solution.py:162
  15.9 0.7 collective-permute-start
  16.6 2.6 pad_maximum_fusion.1
  19.2 0.5 collective-permute-start.1
  20.1 0.2 convert_reduce_fusion
  20.3 0.6 add.51.target_ref
  20.9 45.0 %collective-permute-done.grads_ref = bf16[128,2,4096]{2,1,0:T(2,128)(2,1)} collective-permute-done((bf16[128,2,4096]{2,1,0:T(2,128)(2,1)}, bf16[128,2,4096]{2,1,0:T(2,128)(2,1)}, u32[]{:S(2)}, u32[]{:S(2)}) %collective-permute-start) | collective-permute-done | bytes 2097184 | tf_op jit(solution)/shard_map/ppermute | solution.py:162
  65.8 5.3 %place_grads.2 = bf16[8,2,2,32,2048]{4,3,2,1,0:T(8,128)(2,1)} custom-call(s32[1,256]{1,0:T(1,128)} %add.51.target_ref, bf16[128,2,4096]{2,1,0:T(2,128)(2,1)} %collective-permute-done.grads_ref), custom_call_target="tpu_custom_call" | custom-call | flops 1073741824 | bytes 6291456 | tf_op jit(solution)/shard_map/place_grads/pallas_call | solution.py:46
  71.1 8.1 %all-to-all-start = ((bf16[32,32,2048]{2,1,0:T(8,128)(2,1)}), bf16[32,32,2048]{2,1,0:T(8,128)(2,1)}, u32[]{:S(2)}, u32[]{:S(2)}) async-start(bf16[32,32,2048]{2,1,0:T(8,128)(2,1)} %bitcast.33), calls=%async_computation | async-start | bytes 8388608 | tf_op jit(solution)/shard_map/all_to_all | solution.py:20
  79.5 85.1 %all-gather.1.target_ref = s32[32,2,128]{2,1,0:T(2,128)} all-gather(s32[1,2,128]{2,1,0:T(2,128)S(1)} %copy.17), channel_id=2, replica_groups=mesh['pipe'=4,'z'=4,'xp'=2,'p'=2,'core'=2] {'z','xp','p','core'}, dimensions={0}, use_global_device_ids=true | all-gather | bytes 33792 | tf_op jit(solution)/shard_map/all_gather | solution.py:173
  164.6 5.1 %place_grads.3 = bf16[8,2,2,32,2048]{4,3,2,1,0:T(8,128)(2,1)} custom-call(s32[1,256]{1,0:T(1,128)} %add.51.target_ref, bf16[128,2,4096]{2,1,0:T(2,128)(2,1)} %collective-permute-done.1.grads_ref), custom_call_target="tpu_custom_call" | custom-call | flops 1073741824 | bytes 6291456 | tf_op jit(solution)/shard_map/place_grads/pallas_call | solution.py:46
  169.6 16.9 %broadcast_select_fusion = (bf16[3072,2048]{1,0:T(8,128)(2,1)}, bf16[3072,2048]{1,0:T(8,128)(2,1)}) fusion(bf16[3072,2048]{1,0:T(8,128)(2,1)} %collective-permute-done.2, pred[]{:T(512)S(6)} %eq.65, bf16[1,1,3072,2048]{3,2,1,0:T(8,128)(2,1)} %param.9), kind=kLoop, calls=%fused_computation | loop fusion | flops 12582912 | bytes 50331648 | tf_op jit(solution)/shard_map/jit(_where)/select_n | solution.py:180
  186.6 7.1 %all-to-all-start.1 = ((bf16[32,32,2048]{2,1,0:T(8,128)(2,1)}), bf16[32,32,2048]{2,1,0:T(8,128)(2,1)}, u32[]{:S(2)}, u32[]{:S(2)}) async-start(bf16[32,32,2048]{2,1,0:T(8,128)(2,1)} %bitcast.34), calls=%async_computation.1 | async-start | bytes 8388608 | tf_op jit(solution)/shard_map/all_to_all | solution.py:20
  193.8 13.8 %pick_rows.1 = bf16[32,32,3072]{2,1,0:T(8,128)(2,1)} custom-call(s32[1]{0:T(128)} %bitcast.10.base_ref, s32[32,2,128]{2,1,0:T(2,128)} %all-gather.1.target_ref, bf16[32,128,3072]{2,1,0:T(8,128)(2,1)} %all-gather.4.cloned.1.call-done.tokens_ref), custom_call_target="tpu_custom_call" | custom-call | flops 805306368 | bytes 31457280 | tf_op jit(solution)/shard_map/pick_rows/pallas_call | solution.py:81
  207.6 20.9 %multiply_convert_fusion.1.s0 = bf16[1024,2048]{1,0:T(8,128)(2,1)} fusion(bf16[1024,3072]{1,0:T(8,128)(2,1)} %bitcast.39, bf16[3072,2048]{1,0:T(8,128)(2,1)} %get-tuple-element.12.w0), kind=kOutput, calls=%fused_computation.3 | convolution fusion | flops 12901679104 | bytes 23068672 | tf_op jit(solution)/shard_map/dot_general | solution.py:29
  228.5 16.2 %multiply_convert_fusion.s1 = bf16[1024,2048]{1,0:T(8,128)(2,1)} fusion(bf16[1024,3072]{1,0:T(8,128)(2,1)S(1)} %bitcast.40, bf16[3072,2048]{1,0:T(8,128)(2,1)S(1)} %bitcast.38), kind=kOutput, calls=%fused_computation.2 | convolution fusion | flops 12901679104 | bytes 23068672 | tf_op jit(solution)/shard_map/dot_general | solution.py:29
  244.7 2.5 all-to-all-done.1
  247.2 21.7 %terms.2 = bf16[1024,1536]{1,0:T(8,128)(2,1)} custom-call(bf16[1024,2048]{1,0:T(8,128)(2,1)} %bitcast.7.g0, bf16[1024,2048]{1,0:T(8,128)(2,1)} %bitcast.9.g1, bf16[1024,2048]{1,0:T(8,128)(2,1)} %multiply_convert_fusion.1.s0, bf16[1024,2048]{1,0:T(8,128)(2,1)} %multiply_convert_fusion.s1, bf16[3072,2048]{1,0:T(8,128)(2,1)} %get-tuple-element.12.w0, ...), custom_call_target="tpu_custom_call" | custom-call | flops 12884901888 | bytes 32505856 | tf_op jit(solution)/shard_map/terms/pallas_call | solution.py:131
  268.9 5.3 %all-to-all-start.2 = ((bf16[32,32,1536]{2,1,0:T(8,128)(2,1)}), bf16[32,32,1536]{2,1,0:T(8,128)(2,1)S(1)}, u32[]{:S(2)}, u32[]{:S(2)}) async-start(bf16[32,32,1536]{2,1,0:T(8,128)(2,1)} %bitcast.43), calls=%async_computation.2 | async-start | bytes 6291456 | tf_op jit(solution)/shard_map/all_to_all | solution.py:20
  274.2 21.5 %terms.3 = bf16[1024,1536]{1,0:T(8,128)(2,1)} custom-call(bf16[1024,2048]{1,0:T(8,128)(2,1)} %bitcast.7.g0, bf16[1024,2048]{1,0:T(8,128)(2,1)} %bitcast.9.g1, bf16[1024,2048]{1,0:T(8,128)(2,1)} %multiply_convert_fusion.1.s0, bf16[1024,2048]{1,0:T(8,128)(2,1)} %multiply_convert_fusion.s1, bf16[3072,2048]{1,0:T(8,128)(2,1)} %get-tuple-element.12.w0, ...), custom_call_target="tpu_custom_call" | custom-call | flops 12884901888 | bytes 32505856 | tf_op jit(solution)/shard_map/terms/pallas_call | solution.py:131
  295.7 20.2 %all-to-all-done.2 = bf16[32,32,1536]{2,1,0:T(8,128)(2,1)S(1)} async-done(((bf16[32,32,1536]{2,1,0:T(8,128)(2,1)}), bf16[32,32,1536]{2,1,0:T(8,128)(2,1)S(1)}, u32[]{:S(2)}, u32[]{:S(2)}) %all-to-all-start.2) | async-done | bytes 3145760 | tf_op jit(solution)/shard_map/all_to_all | solution.py:20
  315.9 4.8 %all-to-all-start.3 = ((bf16[32,32,1536]{2,1,0:T(8,128)(2,1)}), bf16[32,32,1536]{2,1,0:T(8,128)(2,1)}, u32[]{:S(2)}, u32[]{:S(2)}) async-start(bf16[32,32,1536]{2,1,0:T(8,128)(2,1)} %bitcast.42), calls=%async_computation.3 | async-start | bytes 6291456 | tf_op jit(solution)/shard_map/all_to_all | solution.py:20
  321.1 0.2 reduce-precision_convert_fusion
  321.3 1.0 fusion.4
  322.4 0.7 collective-permute-start.3
  323.1 39.4 %all-to-all-done.3 = bf16[32,32,1536]{2,1,0:T(8,128)(2,1)} async-done(((bf16[32,32,1536]{2,1,0:T(8,128)(2,1)}), bf16[32,32,1536]{2,1,0:T(8,128)(2,1)}, u32[]{:S(2)}, u32[]{:S(2)}) %all-to-all-start.3) | async-done | bytes 3145760 | tf_op jit(solution)/shard_map/all_to_all | solution.py:20
  362.5 3.0 fusion.3
  365.6 0.7 collective-permute-start.4
  366.3 9.2 %collective-permute-done.4 = bf16[128,1536]{1,0:T(8,128)(2,1)S(1)} collective-permute-done((bf16[128,1536]{1,0:T(8,128)(2,1)S(1)}, bf16[128,1536]{1,0:T(8,128)(2,1)S(1)}, u32[]{:S(2)}, u32[]{:S(2)}) %collective-permute-start.4) | collective-permute-done | bytes 393248 | tf_op jit(solution)/shard_map/ppermute | solution.py:200
  375.5 1.0 maximum_bitcast_fusion
  (36 shorter events, 1.2 us)
Async XLA Ops:
  6.5 187.2 %all-gather.4.cloned.1.call-start = ((), (), s32[]{:S(2)}) async-start(), calls=%async_computation.4 | async-start | bytes 25952256 | tf_op jit(solution)/shard_map/all_gather | solution.py:163
  7.3 162.4 %collective-permute-start.2 = (bf16[3072,2048]{1,0:T(8,128)(2,1)}, bf16[3072,2048]{1,0:T(8,128)(2,1)}, u32[]{:S(2)}, u32[]{:S(2)}) collective-permute-start(bf16[3072,2048]{1,0:T(8,128)(2,1)} %bitcast.36), channel_id=1, source_target_pairs={{0,1},{1,0},{2,3},{3,2},{4,5},{5,4},{6,7},{7,6},{8,9},{9,8},{10,11... | collective-permute-start | bytes 37748744 | tf_op jit(solution)/shard_map/ppermute | solution.py:164
  12.0 7.7 %copy-start.2 = (s32[1,128,2]{1,2,0:T(2,128)S(1)}, s32[1,128,2]{1,2,0:T(2,128)}, u32[]{:S(2)}) copy-start(s32[1,128,2]{1,2,0:T(2,128)} %param.7) | copy-start | bytes 3076
  15.9 49.9 %collective-permute-start = (bf16[128,2,4096]{2,1,0:T(2,128)(2,1)}, bf16[128,2,4096]{2,1,0:T(2,128)(2,1)}, u32[]{:S(2)}, u32[]{:S(2)}) collective-permute-start(bf16[128,2,4096]{2,1,0:T(2,128)(2,1)} %pad_maximum_fusion), channel_id=1, source_target_pairs={{32,0},{64,32},{96,64},{0,96},{33,1},{65,33},{97,65},{1,97},{34,2}... | collective-permute-start | bytes 6291464 | tf_op jit(solution)/shard_map/ppermute | solution.py:162
  19.2 145.4 %collective-permute-start.1 = (bf16[128,2,4096]{2,1,0:T(2,128)(2,1)S(1)}, bf16[128,2,4096]{2,1,0:T(2,128)(2,1)}, u32[]{:S(2)}, u32[]{:S(2)}) collective-permute-start(bf16[128,2,4096]{2,1,0:T(2,128)(2,1)S(1)} %pad_maximum_fusion.1), channel_id=1, source_target_pairs={{32,0},{64,32},{96,64},{0,96},{33,1},{65,33},{97,65},{1,97},{34,2}... | collective-permute-start | bytes 6291464 | tf_op jit(solution)/shard_map/ppermute | solution.py:162
  71.1 115.5 %all-to-all-start = ((bf16[32,32,2048]{2,1,0:T(8,128)(2,1)}), bf16[32,32,2048]{2,1,0:T(8,128)(2,1)}, u32[]{:S(2)}, u32[]{:S(2)}) async-start(bf16[32,32,2048]{2,1,0:T(8,128)(2,1)} %bitcast.33), calls=%async_computation | async-start | bytes 8388608 | tf_op jit(solution)/shard_map/all_to_all | solution.py:20
  186.6 60.6 %all-to-all-start.1 = ((bf16[32,32,2048]{2,1,0:T(8,128)(2,1)}), bf16[32,32,2048]{2,1,0:T(8,128)(2,1)}, u32[]{:S(2)}, u32[]{:S(2)}) async-start(bf16[32,32,2048]{2,1,0:T(8,128)(2,1)} %bitcast.34), calls=%async_computation.1 | async-start | bytes 8388608 | tf_op jit(solution)/shard_map/all_to_all | solution.py:20
  193.8 34.7 %slice-start = ((s8[12582912]{0:T(1024)(128)(4,1)}), s8[4194304]{0:T(1024)(128)(4,1)S(1)}, s32[]{:S(2)}) async-start(s8[12582912]{0:T(1024)(128)(4,1)} %bitcast.37), calls=%async_computation.5 | async-start | bytes 8388608
  207.6 20.9 %slice-start.1 = ((s8[12582912]{0:T(1024)(128)(4,1)}), s8[4194304]{0:T(1024)(128)(4,1)S(1)}, s32[]{:S(2)}) async-start(s8[12582912]{0:T(1024)(128)(4,1)} %bitcast.37), calls=%async_computation.6 | async-start | bytes 8388608
  207.6 20.9 %slice-start.2 = ((s8[12582912]{0:T(1024)(128)(4,1)}), s8[4194304]{0:T(1024)(128)(4,1)S(1)}, s32[]{:S(2)}) async-start(s8[12582912]{0:T(1024)(128)(4,1)} %bitcast.37), calls=%async_computation.7 | async-start | bytes 8388608
  207.6 20.9 %copy-start = (bf16[32,32,3072]{2,1,0:T(8,128)(2,1)S(1)}, bf16[32,32,3072]{2,1,0:T(8,128)(2,1)}, u32[]{:S(2)}) copy-start(bf16[32,32,3072]{2,1,0:T(8,128)(2,1)} %pick_rows.1) | copy-start | bytes 18874372
  268.9 47.0 %all-to-all-start.2 = ((bf16[32,32,1536]{2,1,0:T(8,128)(2,1)}), bf16[32,32,1536]{2,1,0:T(8,128)(2,1)S(1)}, u32[]{:S(2)}, u32[]{:S(2)}) async-start(bf16[32,32,1536]{2,1,0:T(8,128)(2,1)} %bitcast.43), calls=%async_computation.2 | async-start | bytes 6291456 | tf_op jit(solution)/shard_map/all_to_all | solution.py:20
  295.7 25.4 %copy-start.3 = (f32[1,128,2]{1,2,0:T(2,128)S(1)}, f32[1,128,2]{1,2,0:T(2,128)}, u32[]{:S(2)}) copy-start(f32[1,128,2]{1,2,0:T(2,128)} %param.8) | copy-start | bytes 3076
  315.9 46.6 %all-to-all-start.3 = ((bf16[32,32,1536]{2,1,0:T(8,128)(2,1)}), bf16[32,32,1536]{2,1,0:T(8,128)(2,1)}, u32[]{:S(2)}, u32[]{:S(2)}) async-start(bf16[32,32,1536]{2,1,0:T(8,128)(2,1)} %bitcast.42), calls=%async_computation.3 | async-start | bytes 6291456 | tf_op jit(solution)/shard_map/all_to_all | solution.py:20
  321.3 1.1 copy-start.1
  322.4 43.9 %collective-permute-start.3 = (bf16[128,1536]{1,0:T(8,128)(2,1)S(1)}, bf16[128,1536]{1,0:T(8,128)(2,1)S(1)}, u32[]{:S(2)}, u32[]{:S(2)}) collective-permute-start(bf16[128,1536]{1,0:T(8,128)(2,1)S(1)} %fusion.1), channel_id=1, source_target_pairs={{32,0},{64,32},{96,64},{0,96},{33,1},{65,33},{97,65},{1,97},{34,2}... | collective-permute-start | bytes 1179656 | tf_op jit(solution)/shard_map/ppermute | solution.py:200
  365.6 10.0 %collective-permute-start.4 = (bf16[128,1536]{1,0:T(8,128)(2,1)S(1)}, bf16[128,1536]{1,0:T(8,128)(2,1)S(1)}, u32[]{:S(2)}, u32[]{:S(2)}) collective-permute-start(bf16[128,1536]{1,0:T(8,128)(2,1)S(1)} %fusion), channel_id=1, source_target_pairs={{32,0},{64,32},{96,64},{0,96},{33,1},{65,33},{97,65},{1,97},{34,2}... | collective-permute-start | bytes 1179656 | tf_op jit(solution)/shard_map/ppermute | solution.py:200
Sparse Core Ops, SparseCore 0:
  9.6 136.9 all-gather.3
where the time goes:
time: 391 us; the launch traced here: 384 us
  waiting for transfers between devices  117 us (30%)
  blocking collectives  85.1 us (22%)
  Pallas kernels  67.3 us (17%)
  matrix products  41 us (10%)
  starting transfers between devices  28.2 us (7%)
  other arithmetic  25.5 us (7%)
  between operations  14.1 us (4%)
  local copies, waits for them, and re-layouts  5.5 us (1%)
    all_gather x1, blocking collectives, local(): targets = lax.all_gather(by_token.T, PLANE, axis=0)  85.1 us
    all_to_all x4, waiting for transfers between devices, exchange(): return lax.all_to_all(block, PLANE, split_axis=0, concat_axis=0, tiled=True)  62.2 us
    ppermute x2, waiting for transfers between devices, local(): halves.append(lax.ppermute(jnp.concatenate(pieces, axis=2), 'pipe', BACK))  45 us
    pallas_call x2, Pallas kernels, terms(): pl.pallas_call(term_kernel, grid=(steps, hidden // DEEP), in_specs=[side]...  43.2 us
    dot_general x4, matrix products, bf16_dot(): lax.dot_general(a, b, (dims, ((), ())), preferred_element_type=jnp.float32)  41 us
    all_to_all x4, starting transfers between devices, exchange(): return lax.all_to_all(block, PLANE, split_axis=0, concat_axis=0, tiled=True)  25.4 us
    select_n x1, other arithmetic, local(): jnp.where(core == 0, other, mine)  16.9 us
    pallas_call x1, Pallas kernels, pick(): pl.pallas_call(pick_kernel, grid=(sources // SOURCES,), in_specs=[pl.Bloc...  13.8 us
  transfers between devices with their start and end apart: 10, of which 5 were waited for; matrix products, arithmetic and copies ran while one was open for 18% of the time, Pallas kernels for 12%

commit v1 on v0

--- a/solution.py
+++ b/solution.py
@@ -1,3 +1,5 @@
+import functools
+
 import jax
 import jax.numpy as jnp
 from jax import lax
@@ -18,6 +20,10 @@
 
 def exchange(block):
     return lax.all_to_all(block, PLANE, split_axis=0, concat_axis=0, tiled=True)
+
+
+def after(*values):
+    return lax.optimization_barrier(values if len(values) > 1 else values[0])
 
 
 def derivative(gate_pre):
@@ -67,13 +73,19 @@
 
 
 def pick_kernel(base_ref, target_ref, tokens_ref, out_ref):
-    n_tokens = tokens_ref.shape[1]
-    wanted = base_ref[0] + lax.broadcasted_iota(jnp.int32, (SHARE, n_tokens), 0)
-    for i in range(SOURCES):
-        hit = (wanted == target_ref[i, 0:1]) | (wanted == target_ref[i, 1:2])
-        hit = jnp.where(hit, 1.0, 0.0).astype(jnp.bfloat16)
-        rows = jnp.dot(hit, tokens_ref[i], preferred_element_type=jnp.float32)
-        out_ref[i] = rows.astype(jnp.bfloat16)
+    n_tokens, width = tokens_ref.shape[1:]
+    shape = (2 * SHARE, n_tokens)
+    row = lax.broadcasted_iota(jnp.int32, shape, 0)
+    wanted = base_ref[0] + lax.rem(row, SHARE)
+    for i in range(0, SOURCES, 2):
+        hits = []
+        for n in range(2):
+            hit = (wanted == target_ref[i + n, 0:1]) | (wanted == target_ref[i + n, 1:2])
+            hit = hit & (row // SHARE == n)
+            hits.append(jnp.where(hit, 1.0, 0.0).astype(jnp.bfloat16))
+        both = tokens_ref[i : i + 2].reshape(2 * n_tokens, width)
+        rows = jnp.dot(jnp.concatenate(hits, axis=1), both, preferred_element_type=jnp.float32)
+        out_ref[i : i + 2] = rows.astype(jnp.bfloat16).reshape(2, SHARE, width)
 
 
 def pick(base, targets, tokens):
@@ -98,54 +110,89 @@
     )(base.reshape(1), targets, tokens)
 
 
-DEEP = 1024
-
-
-def term_kernel(g0, g1, s0, s1, w0, w1, out_ref, gate, total):
+def copy_kernel(in_ref, out_ref):
+    out_ref[...] = in_ref[...]
+
+
+def cut(grads, h):
+    tokens, top, width = grads.shape
+    columns = width // 8
+    return pl.pallas_call(
+        copy_kernel,
+        grid=(2, 2),
+        in_specs=[
+            pl.BlockSpec((tokens, top, columns), lambda p, j: (0, 0, (2 * p + h) * 2 + j)),
+        ],
+        out_specs=pl.BlockSpec((tokens, top, columns), lambda p, j: (0, 0, 2 * p + j)),
+        out_shape=jax.ShapeDtypeStruct((tokens, top, width // 2), grads.dtype),
+        compiler_params=pltpu.CompilerParams(vmem_limit_bytes=VMEM),
+        cost_estimate=pl.CostEstimate(
+            flops=0, bytes_accessed=2 * tokens * top * width, transcendentals=0
+        ),
+        name="cut_grads",
+    )(grads)
+
+
+DEEP = 512
+WIDE = 768
+
+
+def term_kernel(n, based, *refs):
+    grads, slopes, weights = refs[:n], refs[n : 2 * n], refs[2 * n : 3 * n]
+    out_ref, gate, total = refs[-3:]
     j, k = pl.program_id(0), pl.program_id(1)
 
     @pl.when(j == 0)
     def _():
-        for half, (g, s) in enumerate(((g0, s0), (g1, s1))):
-            product = g[...].astype(jnp.float32) * s[...].astype(jnp.float32)
-            gate[2 * k + half] = product.astype(jnp.bfloat16)
-
-    def part(half, w):
-        return bf16_dot(gate[2 * k + half], w[...], ((1,), (1,)))
+        for i in range(n):
+            product = grads[i][...].astype(jnp.float32) * slopes[i][...].astype(jnp.float32)
+            gate[n * k + i] = product.astype(jnp.bfloat16)
+
+    def step():
+        return sum(bf16_dot(gate[n * k + i], weights[i][...], ((1,), (1,))) for i in range(n))
+
+    last = pl.num_programs(1) - 1
 
     @pl.when(k == 0)
     def _():
-        total[...] = part(0, w0) + part(1, w1)
-
-    @pl.when(k == 1)
-    def _():
-        out_ref[...] = (total[...] + part(0, w0) + part(1, w1)).astype(jnp.bfloat16)
-
-
-def terms(grads, slopes, weights, first, columns):
+        total[...] = step() + refs[3 * n][...] if based else step()
+
+    @pl.when((k > 0) & (k < last))
+    def _():
+        total[...] += step()
+
+    @pl.when(k == last)
+    def _():
+        out_ref[...] = (total[...] + step()).astype(out_ref.dtype)
+
+
+def terms(grads, slopes, weights, first, columns, base=None, dtype=jnp.bfloat16):
+    n = len(grads)
     rows, hidden = grads[0].shape
-    wide = 768
-    steps, offset = columns // wide, first // wide
-    side = pl.BlockSpec((rows, DEEP), lambda j, k: (0, jnp.where(j == 0, k, 1)))
-    weight = pl.BlockSpec((wide, DEEP), lambda j, k: (offset + j, k))
+    steps, offset, depth = columns // WIDE, first // WIDE, hidden // DEEP
+    side = pl.BlockSpec((rows, DEEP), lambda j, k: (0, jnp.where(j == 0, k, depth - 1)))
+    weight = pl.BlockSpec((WIDE, DEEP), lambda j, k: (offset + j, k))
+    column = pl.BlockSpec((rows, WIDE), lambda j, k: (0, j))
+    behind = pl.BlockSpec((rows, WIDE), lambda j, k: (0, offset + j))
+    based = base is not None
     return pl.pallas_call(
-        term_kernel,
-        grid=(steps, hidden // DEEP),
-        in_specs=[side] * 4 + [weight] * 2,
-        out_specs=pl.BlockSpec((rows, wide), lambda j, k: (0, j)),
-        out_shape=jax.ShapeDtypeStruct((rows, columns), jnp.bfloat16),
+        functools.partial(term_kernel, n, based),
+        grid=(steps, depth),
+        in_specs=[side] * (2 * n) + [weight] * n + [behind] * based,
+        out_specs=column,
+        out_shape=jax.ShapeDtypeStruct((rows, columns), dtype),
         scratch_shapes=[
-            pltpu.VMEM((4, rows, DEEP), jnp.bfloat16),
-            pltpu.VMEM((rows, wide), jnp.float32),
-        ],
-        compiler_params=pltpu.CompilerParams(vmem_limit_bytes=VMEM),
-        cost_estimate=pl.CostEstimate(
-            flops=4 * rows * hidden * columns,
-            bytes_accessed=8 * rows * hidden + 4 * hidden * columns + 2 * rows * columns,
+            pltpu.VMEM((n * depth, rows, DEEP), jnp.bfloat16),
+            pltpu.VMEM((rows, WIDE), jnp.float32),
+        ],
+        compiler_params=pltpu.CompilerParams(vmem_limit_bytes=VMEM),
+        cost_estimate=pl.CostEstimate(
+            flops=2 * n * rows * hidden * columns,
+            bytes_accessed=2 * n * hidden * (2 * rows + columns) + 4 * rows * columns,
             transcendentals=0,
         ),
         name="terms",
-    )(*grads, *slopes, *weights)
+    )(*grads, *slopes, *weights, *([base] if based else []))
 
 
 def local(acts, hid_grad, routes, probs, w_gate):
@@ -156,10 +203,7 @@
     core = lax.axis_index("core")
     expert = lax.axis_index("z") * 2 + lax.axis_index("xp")
 
-    halves = []
-    for h in range(2):
-        pieces = [hid_grad[0][:, :, f * hidden : (f + 1) * hidden] for f in (h, 2 + h)]
-        halves.append(lax.ppermute(jnp.concatenate(pieces, axis=2), "pipe", BACK))
+    halves = [lax.ppermute(cut(hid_grad[0], h), "pipe", BACK) for h in range(2)]
     gathered = lax.all_gather(tokens, PLANE, axis=0)
     other = lax.ppermute(mine, "core", [(0, 1), (1, 0)])
 
@@ -170,18 +214,22 @@
     slot = jnp.sum(earlier.astype(jnp.int32), axis=1)
     target = flat_expert * SLOTS + slot
     by_token = target.reshape(n_tokens, TOP)
-    targets = lax.all_gather(by_token.T, PLANE, axis=0)
-
-    received = []
-    for h in range(2):
-        received.append(exchange(place(target, halves[h])).reshape(DEVICES * SHARE, hidden))
-
-    gathered, received[0] = lax.optimization_barrier((gathered, received[0]))
-    weights = (jnp.where(core == 0, mine, other), jnp.where(core == 0, other, mine))
+    targets = exchange(jnp.broadcast_to(by_token.T[None], (DEVICES, TOP, n_tokens)))
+
+    target, targets = after(target, targets)
+    first = exchange(place(target, halves[0])).reshape(DEVICES * SHARE, hidden)
+    lower = jnp.where(core == 0, mine, other)
+    upper = jnp.where(core == 0, other, mine)
+    target, lower, upper = after(target, lower, upper)
+    second = exchange(place(target, halves[1])).reshape(DEVICES * SHARE, hidden)
+
+    gathered, first = after(gathered, first)
     rows = pick(expert * SLOTS + core * SHARE, targets, gathered).reshape(DEVICES * SHARE, width)
-    slopes = [
-        lax.optimization_barrier(derivative(bf16_dot(rows, w, ((1,), (0,))))) for w in weights
-    ]
+    columns = width // COLUMN_PARTS
+    slope_0 = after(derivative(bf16_dot(rows, lower, ((1,), (0,)))))
+    early = terms([first], [slope_0], [lower], 0, width, dtype=jnp.float32)
+    rows, early = after(rows, early)
+    slope_1 = after(derivative(bf16_dot(rows, upper, ((1,), (0,)))))
 
     places = jnp.arange(EXPERTS * SLOTS, dtype=jnp.int32).reshape(EXPERTS, 1, SLOTS)
     places = jnp.broadcast_to(places, (EXPERTS, 2, SLOTS)).reshape(-1)
@@ -190,10 +238,9 @@
     high = lax.reduce_precision(mix, 8, 7)
     mix = jnp.concatenate([high, mix - high]).astype(jnp.bfloat16)
 
-    columns = width // COLUMN_PARTS
     parts = []
     for j in range(COLUMN_PARTS):
-        term = terms(received, slopes, weights, j * columns, columns)
+        term = terms([second], [slope_1], [upper], j * columns, columns, base=early)
         returned = exchange(term.reshape(DEVICES, SHARE, columns)).reshape(-1, columns)
         both = bf16_dot(mix, returned, ((1,), (0,)))
         summed = (both[:n_tokens] + both[n_tokens:]).astype(jnp.bfloat16)

time: 391 us -> 366 us (0.936); the launches traced: 384 us -> 364 us
  blocking collectives: 85.1 us -> 0 us
  waiting for transfers between devices: 117 us -> 161 us
  Pallas kernels: 67.3 us -> 87 us
  starting transfers between devices: 28.2 us -> 36.2 us
  other arithmetic: 25.5 us -> 19.1 us
    all_gather x1 -> x0, blocking collectives: 85.1 us -> none  [local(): targets = lax.all_gather(by_token.T, PLANE, axis=0)]
    all_to_all x4 -> x5, waiting for transfers between devices: 62.2 us -> 87.2 us  [exchange(): return lax.all_to_all(block, PLANE, split_axis=0, concat_axis=0, tiled=True)]
    pallas_call x2 -> x5, Pallas kernels: 43.2 us -> 62.6 us  [the longest x3 54.7 us: terms(): pl.pallas_call(functools.partial(term_kernel, n, based), grid=(steps, dep...]
    ppermute x2, waiting for transfers between devices: 45 us -> 63.9 us  [local(): halves = [lax.ppermute(cut(hid_grad[0], h), 'pipe', BACK) for h in range(2)]]
    all_to_all x4 -> x5, starting transfers between devices: 25.4 us -> 33.6 us  [exchange(): return lax.all_to_all(block, PLANE, split_axis=0, concat_axis=0, tiled=True)]
    concatenate x2 -> x0, other arithmetic: 6.43 us -> none  [local(): halves.append(lax.ppermute(jnp.concatenate(pieces, axis=2), 'pipe', BACK))]
    slice x1 -> x0, local copies, waits for them, and re-layouts: 4.63 us -> none  [local(): hid_grad[0][:, :, f * hidden:(f + 1) * hidden]]
  transfers between devices with their start and end apart: 10 -> 11, of which waited for: 5 -> 7; matrix products, arithmetic and copies ran while one was open for 18% -> 17% of each run, Pallas kernels for 12% -> 20%
where the time goes in v1:
time: 366 us; the launch traced here: 364 us
  waiting for transfers between devices  161 us (44%)
  Pallas kernels  87 us (24%)
  matrix products  43.7 us (12%)
  starting transfers between devices  36.2 us (10%)
  other arithmetic  19.1 us (5%)
  between operations  13.6 us (4%)
  local copies, waits for them, and re-layouts  4.03 us (1%)
    all_to_all x5, waiting for transfers between devices, exchange(): return lax.all_to_all(block, PLANE, split_axis=0, concat_axis=0, tiled=True)  87.2 us
    ppermute x2, waiting for transfers between devices, local(): halves = [lax.ppermute(cut(hid_grad[0], h), 'pipe', BACK) for h in range(2)]  63.9 us
    pallas_call x3, Pallas kernels, terms(): pl.pallas_call(functools.partial(term_kernel, n, based), grid=(steps, dep...  54.7 us
    dot_general x4, matrix products, bf16_dot(): lax.dot_general(a, b, (dims, ((), ())), preferred_element_type=jnp.float32)  43.7 us
    all_to_all x5, starting transfers between devices, exchange(): return lax.all_to_all(block, PLANE, split_axis=0, concat_axis=0, tiled=True)  33.6 us
    select_n x1, other arithmetic, local(): upper = jnp.where(core == 0, other, mine)  17 us
    pallas_call x1, Pallas kernels, pick(): pl.pallas_call(pick_kernel, grid=(sources // SOURCES,), in_specs=[pl.Bloc...  14 us
    pallas_call x2, Pallas kernels, place(): pl.pallas_call(place_kernel, grid=(2, steps), in_specs=[pl.BlockSpec((1,...  10.4 us
  transfers between devices with their start and end apart: 11, of which 7 were waited for; matrix products, arithmetic and copies ran while one was open for 17% of the time, Pallas kernels for 20%

profile of v1, /device:TPU:24, one launch (start us, length us, event | category | flops | bytes accessed | tf_op | source)
XLA Modules:
  0.0 364.4 jit_solution(17763019511674326886)
XLA Ops:
  6.5 0.7 all-gather.2.cloned.1.call-update
  7.4 3.9 %cut_grads.3 = bf16[128,2,4096]{2,1,0:T(2,128)(2,1)} custom-call(bf16[128,2,8192]{2,1,0:T(2,128)(2,1)} %bitcast.32), custom_call_target="tpu_custom_call" | custom-call | bytes 4194304 | tf_op jit(solution)/shard_map/cut_grads/pallas_call | solution.py:120
  11.2 0.7 collective-permute-start.2
  13.3 8.2 %all-to-all-start = ((s32[32,2,128]{2,1,0:T(2,128)}), s32[32,2,128]{2,1,0:T(2,128)S(1)}, u32[]{:S(2)}, u32[]{:S(2)}) async-start(s32[32,2,128]{2,1,0:T(2,128)} %broadcast_in_dim.46), calls=%async_computation | async-start | bytes 65536 | tf_op jit(solution)/shard_map/all_to_all | solution.py:22
  22.1 6.8 %all-to-all-done.target_ref = s32[32,2,128]{2,1,0:T(2,128)S(1)} async-done(((s32[32,2,128]{2,1,0:T(2,128)}), s32[32,2,128]{2,1,0:T(2,128)S(1)}, u32[]{:S(2)}, u32[]{:S(2)}) %all-to-all-start) | async-done | bytes 32800 | tf_op jit(solution)/shard_map/all_to_all | solution.py:22
  28.9 31.8 %collective-permute-done.2.grads_ref = bf16[128,2,4096]{2,1,0:T(2,128)(2,1)S(1)} collective-permute-done((bf16[128,2,4096]{2,1,0:T(2,128)(2,1)}, bf16[128,2,4096]{2,1,0:T(2,128)(2,1)S(1)}, u32[]{:S(2)}, u32[]{:S(2)}) %collective-permute-start.2) | collective-permute-done | bytes 2097184 | tf_op jit(solution)/shard_map/ppermute | solution.py:206
  60.7 1.3 copy-done.3
  62.0 5.3 %place_grads.3 = bf16[8,2,2,32,2048]{4,3,2,1,0:T(8,128)(2,1)} custom-call(s32[1,256]{1,0:T(1,128)} %bitcast.43, bf16[128,2,4096]{2,1,0:T(2,128)(2,1)} %copy-done.3), custom_call_target="tpu_custom_call" | custom-call | flops 1073741824 | bytes 6291456 | tf_op jit(solution)/shard_map/place_grads/pallas_call | solution.py:52
  67.3 8.1 %all-to-all-start.2 = ((bf16[32,32,2048]{2,1,0:T(8,128)(2,1)}), bf16[32,32,2048]{2,1,0:T(8,128)(2,1)}, u32[]{:S(2)}, u32[]{:S(2)}) async-start(bf16[32,32,2048]{2,1,0:T(8,128)(2,1)} %bitcast.34), calls=%async_computation.2 | async-start | bytes 8388608 | tf_op jit(solution)/shard_map/all_to_all | solution.py:22
  75.4 4.0 %cut_grads.2 = bf16[128,2,4096]{2,1,0:T(2,128)(2,1)} custom-call(bf16[128,2,8192]{2,1,0:T(2,128)(2,1)} %bitcast.33), custom_call_target="tpu_custom_call" | custom-call | bytes 4194304 | tf_op jit(solution)/shard_map/cut_grads/pallas_call | solution.py:120
  79.4 17.0 %broadcast_select_fusion = (bf16[3072,2048]{1,0:T(8,128)(2,1)}, bf16[3072,2048]{1,0:T(8,128)(2,1)}) fusion(bf16[3072,2048]{1,0:T(8,128)(2,1)} %collective-permute-done, pred[]{:T(512)S(6)} %eq.65, bf16[1,1,3072,2048]{3,2,1,0:T(8,128)(2,1)} %param.9), kind=kLoop, calls=%fused_computation | loop fusion | flops 12582912 | bytes 50331648 | tf_op jit(solution)/shard_map/jit(_where)/select_n | solution.py:222
  96.4 32.2 %collective-permute-done.1.grads_ref = bf16[128,2,4096]{2,1,0:T(2,128)(2,1)S(1)} collective-permute-done((bf16[128,2,4096]{2,1,0:T(2,128)(2,1)}, bf16[128,2,4096]{2,1,0:T(2,128)(2,1)S(1)}, u32[]{:S(2)}, u32[]{:S(2)}) %collective-permute-start.1) | collective-permute-done | bytes 2097184 | tf_op jit(solution)/shard_map/ppermute | solution.py:206
  128.6 1.3 copy-done.2
  129.9 5.1 %place_grads.2 = bf16[8,2,2,32,2048]{4,3,2,1,0:T(8,128)(2,1)} custom-call(s32[1,256]{1,0:T(1,128)} %bitcast.44, bf16[128,2,4096]{2,1,0:T(2,128)(2,1)} %copy-done.2), custom_call_target="tpu_custom_call" | custom-call | flops 1073741824 | bytes 6291456 | tf_op jit(solution)/shard_map/place_grads/pallas_call | solution.py:52
  134.9 14.6 %all-to-all-done.2 = bf16[32,32,2048]{2,1,0:T(8,128)(2,1)} async-done(((bf16[32,32,2048]{2,1,0:T(8,128)(2,1)}), bf16[32,32,2048]{2,1,0:T(8,128)(2,1)}, u32[]{:S(2)}, u32[]{:S(2)}) %all-to-all-start.2) | async-done | bytes 4194336 | tf_op jit(solution)/shard_map/all_to_all | solution.py:22
  149.6 5.1 %all-to-all-start.1 = ((bf16[32,32,2048]{2,1,0:T(8,128)(2,1)}), bf16[32,32,2048]{2,1,0:T(8,128)(2,1)}, u32[]{:S(2)}, u32[]{:S(2)}) async-start(bf16[32,32,2048]{2,1,0:T(8,128)(2,1)} %bitcast.35), calls=%async_computation.1 | async-start | bytes 8388608 | tf_op jit(solution)/shard_map/all_to_all | solution.py:22
  154.7 14.0 %pick_rows.1 = bf16[32,32,3072]{2,1,0:T(8,128)(2,1)} custom-call(s32[1]{0:T(128)} %bitcast.10.base_ref, s32[32,2,128]{2,1,0:T(2,128)} %copy-done.4, bf16[32,128,3072]{2,1,0:T(8,128)(2,1)} %all-gather.2.cloned.1.call-done.tokens_ref), custom_call_target="tpu_custom_call" | custom-call | flops 805306368 | bytes 31457280 | tf_op jit(solution)/shard_map/pick_rows/pallas_call | solution.py:93
  168.7 20.8 %multiply_convert_fusion.1.refs_1_ = bf16[1024,2048]{1,0:T(8,128)(2,1)} fusion(bf16[1024,3072]{1,0:T(8,128)(2,1)} %bitcast.40, bf16[3072,2048]{1,0:T(8,128)(2,1)} %get-tuple-element.19.refs_2_), kind=kOutput, calls=%fused_computation.3 | convolution fusion | flops 12901679104 | bytes 23068672 | tf_op jit(solution)/shard_map/dot_general | solution.py:35
  189.5 24.8 %terms.3.refs_3_ = f32[1024,3072]{1,0:T(8,128)} custom-call(bf16[1024,2048]{1,0:T(8,128)(2,1)} %bitcast.13.refs_0_, bf16[1024,2048]{1,0:T(8,128)(2,1)} %multiply_convert_fusion.1.refs_1_, bf16[3072,2048]{1,0:T(8,128)(2,1)} %get-tuple-element.19.refs_2_), custom_call_target="tpu_custom_call" | custom-call | flops 12884901888 | bytes 33554432 | tf_op jit(solution)/shard_map/terms/pallas_call | solution.py:178
  214.2 19.0 %multiply_convert_fusion.refs_1_ = bf16[1024,2048]{1,0:T(8,128)(2,1)} fusion(bf16[1024,3072]{1,0:T(8,128)(2,1)S(1)} %bitcast.41, bf16[3072,2048]{1,0:T(8,128)(2,1)} %get-tuple-element.21.refs_2_), kind=kOutput, calls=%fused_computation.2 | convolution fusion | flops 12901679104 | bytes 23068672 | tf_op jit(solution)/shard_map/dot_general | solution.py:35
  233.2 15.0 %terms.4 = bf16[1024,1536]{1,0:T(8,128)(2,1)} custom-call(bf16[1024,2048]{1,0:T(8,128)(2,1)} %bitcast.9.refs_0_, bf16[1024,2048]{1,0:T(8,128)(2,1)} %multiply_convert_fusion.refs_1_, bf16[3072,2048]{1,0:T(8,128)(2,1)} %get-tuple-element.21.refs_2_, f32[1024,3072]{1,0:T(8,128)} %terms.3.refs_3_), custom_call_target="tpu_custom_call" | custom-call | flops 6442450944 | bytes 20971520 | tf_op jit(solution)/shard_map/terms/pallas_call | solution.py:178
  248.2 7.1 %all-to-all-start.3 = ((bf16[32,32,1536]{2,1,0:T(8,128)(2,1)}), bf16[32,32,1536]{2,1,0:T(8,128)(2,1)S(1)}, u32[]{:S(2)}, u32[]{:S(2)}) async-start(bf16[32,32,1536]{2,1,0:T(8,128)(2,1)} %bitcast.37), calls=%async_computation.3 | async-start | bytes 6291456 | tf_op jit(solution)/shard_map/all_to_all | solution.py:22
  255.3 15.0 %terms.5 = bf16[1024,1536]{1,0:T(8,128)(2,1)} custom-call(bf16[1024,2048]{1,0:T(8,128)(2,1)} %bitcast.9.refs_0_, bf16[1024,2048]{1,0:T(8,128)(2,1)} %multiply_convert_fusion.refs_1_, bf16[3072,2048]{1,0:T(8,128)(2,1)} %get-tuple-element.21.refs_2_, f32[1024,3072]{1,0:T(8,128)} %terms.3.refs_3_), custom_call_target="tpu_custom_call" | custom-call | flops 6442450944 | bytes 20971520 | tf_op jit(solution)/shard_map/terms/pallas_call | solution.py:178
  270.3 26.8 %all-to-all-done.3 = bf16[32,32,1536]{2,1,0:T(8,128)(2,1)S(1)} async-done(((bf16[32,32,1536]{2,1,0:T(8,128)(2,1)}), bf16[32,32,1536]{2,1,0:T(8,128)(2,1)S(1)}, u32[]{:S(2)}, u32[]{:S(2)}) %all-to-all-start.3) | async-done | bytes 3145760 | tf_op jit(solution)/shard_map/all_to_all | solution.py:22
  297.1 5.1 %all-to-all-start.4 = ((bf16[32,32,1536]{2,1,0:T(8,128)(2,1)}), bf16[32,32,1536]{2,1,0:T(8,128)(2,1)}, u32[]{:S(2)}, u32[]{:S(2)}) async-start(bf16[32,32,1536]{2,1,0:T(8,128)(2,1)} %bitcast.36), calls=%async_computation.4 | async-start | bytes 6291456 | tf_op jit(solution)/shard_map/all_to_all | solution.py:22
  302.7 1.0 fusion.4
  303.8 0.9 collective-permute-start.3
  304.7 39.0 %all-to-all-done.4 = bf16[32,32,1536]{2,1,0:T(8,128)(2,1)} async-done(((bf16[32,32,1536]{2,1,0:T(8,128)(2,1)}), bf16[32,32,1536]{2,1,0:T(8,128)(2,1)}, u32[]{:S(2)}, u32[]{:S(2)}) %all-to-all-start.4) | async-done | bytes 3145760 | tf_op jit(solution)/shard_map/all_to_all | solution.py:22
  343.7 3.0 fusion.3
  346.8 0.9 collective-permute-start.4
  347.7 8.9 %collective-permute-done.4 = bf16[128,1536]{1,0:T(8,128)(2,1)S(1)} collective-permute-done((bf16[128,1536]{1,0:T(8,128)(2,1)S(1)}, bf16[128,1536]{1,0:T(8,128)(2,1)S(1)}, u32[]{:S(2)}, u32[]{:S(2)}) %collective-permute-start.4) | collective-permute-done | bytes 393248 | tf_op jit(solution)/shard_map/ppermute | solution.py:247
  356.6 1.0 maximum_bitcast_fusion
  (35 shorter events, 2.7 us)
Async XLA Ops:
  6.5 5.5 %copy-start.5 = (s32[1,128,2]{1,2,0:T(2,128)S(1)}, s32[1,128,2]{1,2,0:T(2,128)}, u32[]{:S(2)}) copy-start(s32[1,128,2]{1,2,0:T(2,128)} %param.7) | copy-start | bytes 3076
  6.5 148.1 %all-gather.2.cloned.1.call-start = ((), (), s32[]{:S(2)}) async-start(), calls=%async_computation.5 | async-start | bytes 25952256 | tf_op jit(solution)/shard_map/all_gather | solution.py:207
  7.3 72.1 %collective-permute-start = (bf16[3072,2048]{1,0:T(8,128)(2,1)}, bf16[3072,2048]{1,0:T(8,128)(2,1)}, u32[]{:S(2)}, u32[]{:S(2)}) collective-permute-start(bf16[3072,2048]{1,0:T(8,128)(2,1)} %bitcast.39), channel_id=1, source_target_pairs={{0,1},{1,0},{2,3},{3,2},{4,5},{5,4},{6,7},{7,6},{8,9},{9,8},{10,11... | collective-permute-start | bytes 37748744 | tf_op jit(solution)/shard_map/ppermute | solution.py:208
  11.2 49.4 %collective-permute-start.2 = (bf16[128,2,4096]{2,1,0:T(2,128)(2,1)}, bf16[128,2,4096]{2,1,0:T(2,128)(2,1)S(1)}, u32[]{:S(2)}, u32[]{:S(2)}) collective-permute-start(bf16[128,2,4096]{2,1,0:T(2,128)(2,1)} %cut_grads.3), channel_id=1, source_target_pairs={{32,0},{64,32},{96,64},{0,96},{33,1},{65,33},{97,65},{1,97},{34,2}... | collective-permute-start | bytes 6291464 | tf_op jit(solution)/shard_map/ppermute | solution.py:206
  13.3 15.6 %all-to-all-start = ((s32[32,2,128]{2,1,0:T(2,128)}), s32[32,2,128]{2,1,0:T(2,128)S(1)}, u32[]{:S(2)}, u32[]{:S(2)}) async-start(s32[32,2,128]{2,1,0:T(2,128)} %broadcast_in_dim.46), calls=%async_computation | async-start | bytes 65536 | tf_op jit(solution)/shard_map/all_to_all | solution.py:22
  28.9 67.5 %copy-start.4 = (s32[32,2,128]{2,1,0:T(2,128)}, s32[32,2,128]{2,1,0:T(2,128)S(1)}, u32[]{:S(2)}) copy-start(s32[32,2,128]{2,1,0:T(2,128)S(1)} %all-to-all-done.target_ref) | copy-start | bytes 98308
  60.7 1.3 copy-start.3
  67.3 82.3 %all-to-all-start.2 = ((bf16[32,32,2048]{2,1,0:T(8,128)(2,1)}), bf16[32,32,2048]{2,1,0:T(8,128)(2,1)}, u32[]{:S(2)}, u32[]{:S(2)}) async-start(bf16[32,32,2048]{2,1,0:T(8,128)(2,1)} %bitcast.34), calls=%async_computation.2 | async-start | bytes 8388608 | tf_op jit(solution)/shard_map/all_to_all | solution.py:22
  79.4 49.2 %collective-permute-start.1 = (bf16[128,2,4096]{2,1,0:T(2,128)(2,1)}, bf16[128,2,4096]{2,1,0:T(2,128)(2,1)S(1)}, u32[]{:S(2)}, u32[]{:S(2)}) collective-permute-start(bf16[128,2,4096]{2,1,0:T(2,128)(2,1)} %cut_grads.2), channel_id=1, source_target_pairs={{32,0},{64,32},{96,64},{0,96},{33,1},{65,33},{97,65},{1,97},{34,2}... | collective-permute-start | bytes 6291464 | tf_op jit(solution)/shard_map/ppermute | solution.py:206
  128.5 1.3 copy-start.2
  149.6 83.6 %all-to-all-start.1 = ((bf16[32,32,2048]{2,1,0:T(8,128)(2,1)}), bf16[32,32,2048]{2,1,0:T(8,128)(2,1)}, u32[]{:S(2)}, u32[]{:S(2)}) async-start(bf16[32,32,2048]{2,1,0:T(8,128)(2,1)} %bitcast.35), calls=%async_computation.1 | async-start | bytes 8388608 | tf_op jit(solution)/shard_map/all_to_all | solution.py:22
  189.5 24.8 %copy-start = (bf16[32,32,3072]{2,1,0:T(8,128)(2,1)S(1)}, bf16[32,32,3072]{2,1,0:T(8,128)(2,1)}, u32[]{:S(2)}) copy-start(bf16[32,32,3072]{2,1,0:T(8,128)(2,1)} %pick_rows.1) | copy-start | bytes 18874372
  248.2 48.9 %all-to-all-start.3 = ((bf16[32,32,1536]{2,1,0:T(8,128)(2,1)}), bf16[32,32,1536]{2,1,0:T(8,128)(2,1)S(1)}, u32[]{:S(2)}, u32[]{:S(2)}) async-start(bf16[32,32,1536]{2,1,0:T(8,128)(2,1)} %bitcast.37), calls=%async_computation.3 | async-start | bytes 6291456 | tf_op jit(solution)/shard_map/all_to_all | solution.py:22
  270.3 32.2 %copy-start.6 = (f32[1,128,2]{1,2,0:T(2,128)S(1)}, f32[1,128,2]{1,2,0:T(2,128)}, u32[]{:S(2)}) copy-start(f32[1,128,2]{1,2,0:T(2,128)} %param.8) | copy-start | bytes 3076
  297.1 46.6 %all-to-all-start.4 = ((bf16[32,32,1536]{2,1,0:T(8,128)(2,1)}), bf16[32,32,1536]{2,1,0:T(8,128)(2,1)}, u32[]{:S(2)}, u32[]{:S(2)}) async-start(bf16[32,32,1536]{2,1,0:T(8,128)(2,1)} %bitcast.36), calls=%async_computation.4 | async-start | bytes 6291456 | tf_op jit(solution)/shard_map/all_to_all | solution.py:22
  302.7 1.1 copy-start.1
  303.8 43.9 %collective-permute-start.3 = (bf16[128,1536]{1,0:T(8,128)(2,1)S(1)}, bf16[128,1536]{1,0:T(8,128)(2,1)S(1)}, u32[]{:S(2)}, u32[]{:S(2)}) collective-permute-start(bf16[128,1536]{1,0:T(8,128)(2,1)S(1)} %fusion.1), channel_id=1, source_target_pairs={{32,0},{64,32},{96,64},{0,96},{33,1},{65,33},{97,65},{1,97},{34,2}... | collective-permute-start | bytes 1179656 | tf_op jit(solution)/shard_map/ppermute | solution.py:247
  346.8 9.8 %collective-permute-start.4 = (bf16[128,1536]{1,0:T(8,128)(2,1)S(1)}, bf16[128,1536]{1,0:T(8,128)(2,1)S(1)}, u32[]{:S(2)}, u32[]{:S(2)}) collective-permute-start(bf16[128,1536]{1,0:T(8,128)(2,1)S(1)} %fusion), channel_id=1, source_target_pairs={{32,0},{64,32},{96,64},{0,96},{33,1},{65,33},{97,65},{1,97},{34,2}... | collective-permute-start | bytes 1179656 | tf_op jit(solution)/shard_map/ppermute | solution.py:247
Sparse Core Ops, SparseCore 0:
  9.6 137.2 all-gather.1

commit v2 on v1

--- a/solution.py
+++ b/solution.py
@@ -69,33 +69,38 @@
     return out.reshape(DEVICES, SHARE, hidden)
 
 
-SOURCES = 4
-
-
-def pick_kernel(base_ref, target_ref, tokens_ref, out_ref):
+SOURCES = 8
+
+
+def pick_kernel(number_ref, tokens_ref, out_ref):
     n_tokens, width = tokens_ref.shape[1:]
-    shape = (2 * SHARE, n_tokens)
-    row = lax.broadcasted_iota(jnp.int32, shape, 0)
-    wanted = base_ref[0] + lax.rem(row, SHARE)
+    token = lax.broadcasted_iota(jnp.int32, (SHARE, n_tokens), 1) + 1
+    nothing = jnp.zeros((SHARE, n_tokens), jnp.bfloat16)
     for i in range(0, SOURCES, 2):
-        hits = []
-        for n in range(2):
-            hit = (wanted == target_ref[i + n, 0:1]) | (wanted == target_ref[i + n, 1:2])
-            hit = hit & (row // SHARE == n)
-            hits.append(jnp.where(hit, 1.0, 0.0).astype(jnp.bfloat16))
+        hits = [
+            jnp.where(number_ref[i + n].astype(jnp.float32) == token.astype(jnp.float32), 1.0, 0.0)
+            for n in range(2)
+        ]
+        hits = [hit.astype(jnp.bfloat16) for hit in hits]
+        pair = jnp.concatenate(
+            [
+                jnp.concatenate([hits[0], nothing], axis=1),
+                jnp.concatenate([nothing, hits[1]], axis=1),
+            ],
+            axis=0,
+        )
         both = tokens_ref[i : i + 2].reshape(2 * n_tokens, width)
-        rows = jnp.dot(jnp.concatenate(hits, axis=1), both, preferred_element_type=jnp.float32)
+        rows = jnp.dot(pair, both, preferred_element_type=jnp.float32)
         out_ref[i : i + 2] = rows.astype(jnp.bfloat16).reshape(2, SHARE, width)
 
 
-def pick(base, targets, tokens):
+def pick(numbers, tokens):
     sources, n_tokens, width = tokens.shape
     return pl.pallas_call(
         pick_kernel,
         grid=(sources // SOURCES,),
         in_specs=[
-            pl.BlockSpec(memory_space=pltpu.SMEM),
-            pl.BlockSpec((SOURCES, TOP, n_tokens), lambda i: (i, 0, 0)),
+            pl.BlockSpec((SOURCES, SHARE, n_tokens), lambda i: (i, 0, 0)),
             pl.BlockSpec((SOURCES, n_tokens, width), lambda i: (i, 0, 0)),
         ],
         out_specs=pl.BlockSpec((SOURCES, SHARE, width), lambda i: (i, 0, 0)),
@@ -107,7 +112,7 @@
             transcendentals=0,
         ),
         name="pick_rows",
-    )(base.reshape(1), targets, tokens)
+    )(numbers, tokens)
 
 
 def copy_kernel(in_ref, out_ref):
@@ -201,11 +206,10 @@
     mine = w_gate[0, 0]
     hidden = mine.shape[1]
     core = lax.axis_index("core")
-    expert = lax.axis_index("z") * 2 + lax.axis_index("xp")
-
-    halves = [lax.ppermute(cut(hid_grad[0], h), "pipe", BACK) for h in range(2)]
-    gathered = lax.all_gather(tokens, PLANE, axis=0)
-    other = lax.ppermute(mine, "core", [(0, 1), (1, 0)])
+    rows_here = DEVICES * SHARE
+
+    sent_width = width // 2
+    gathered = lax.all_gather(tokens[:, sent_width:], PLANE, axis=0)
 
     flat_expert = routes[0].reshape(-1)
     pairs = flat_expert.shape[0]
@@ -214,25 +218,40 @@
     slot = jnp.sum(earlier.astype(jnp.int32), axis=1)
     target = flat_expert * SLOTS + slot
     by_token = target.reshape(n_tokens, TOP)
-    targets = exchange(jnp.broadcast_to(by_token.T[None], (DEVICES, TOP, n_tokens)))
-
-    target, targets = after(target, targets)
-    first = exchange(place(target, halves[0])).reshape(DEVICES * SHARE, hidden)
+
+    places = jnp.arange(EXPERTS * SLOTS, dtype=jnp.int32).reshape(EXPERTS, 1, SLOTS)
+    places = jnp.broadcast_to(places, (EXPERTS, 2, SLOTS)).reshape(-1)
+    row_hit = [places[:, None] == by_token[None, :, k] for k in range(TOP)]
+    place_token = (row_hit[0] | row_hit[1]).astype(jnp.bfloat16)
+    numbered = jnp.broadcast_to(
+        jnp.arange(1, n_tokens + 1, dtype=jnp.int32)[:, None], (n_tokens, n_tokens)
+    ).astype(jnp.bfloat16)
+    sent = jnp.concatenate([tokens[:, :sent_width], numbered], axis=1)
+    sent = bf16_dot(place_token, sent, ((1,), (0,))).astype(jnp.bfloat16)
+    got = exchange(sent.reshape(DEVICES, SHARE, sent_width + n_tokens))
+    rows_0 = got[:, :, :sent_width].reshape(rows_here, sent_width)
+    numbers = got[:, :, sent_width:]
+
+    pieces = [cut(hid_grad[0], h) for h in range(2)]
+    halves = [lax.ppermute(piece, "pipe", BACK) for piece in pieces]
+    other = lax.ppermute(mine, "core", [(0, 1), (1, 0)])
     lower = jnp.where(core == 0, mine, other)
     upper = jnp.where(core == 0, other, mine)
-    target, lower, upper = after(target, lower, upper)
-    second = exchange(place(target, halves[1])).reshape(DEVICES * SHARE, hidden)
-
-    gathered, first = after(gathered, first)
-    rows = pick(expert * SLOTS + core * SHARE, targets, gathered).reshape(DEVICES * SHARE, width)
+
+    first = exchange(place(target, halves[0])).reshape(rows_here, hidden)
+    below = [
+        after(bf16_dot(rows_0, w[:sent_width], ((1,), (0,)))) for w in (lower, upper)
+    ]
+    target, below[0], below[1] = after(target, below[0], below[1])
+    second = exchange(place(target, halves[1])).reshape(rows_here, hidden)
+
+    rows_1 = pick(numbers, gathered).reshape(rows_here, width - sent_width)
+    slope_0 = after(derivative(below[0] + bf16_dot(rows_1, lower[sent_width:], ((1,), (0,)))))
+    early = terms([first], [slope_0], [lower], 0, width, dtype=jnp.float32)
+    rows_1, early = after(rows_1, early)
+    slope_1 = after(derivative(below[1] + bf16_dot(rows_1, upper[sent_width:], ((1,), (0,)))))
+
     columns = width // COLUMN_PARTS
-    slope_0 = after(derivative(bf16_dot(rows, lower, ((1,), (0,)))))
-    early = terms([first], [slope_0], [lower], 0, width, dtype=jnp.float32)
-    rows, early = after(rows, early)
-    slope_1 = after(derivative(bf16_dot(rows, upper, ((1,), (0,)))))
-
-    places = jnp.arange(EXPERTS * SLOTS, dtype=jnp.int32).reshape(EXPERTS, 1, SLOTS)
-    places = jnp.broadcast_to(places, (EXPERTS, 2, SLOTS)).reshape(-1)
     hit = [by_token[:, k, None] == places[None, :] for k in range(TOP)]
     mix = sum(jnp.where(hit[k], probs[0][:, k, None], 0.0) for k in range(TOP))
     high = lax.reduce_precision(mix, 8, 7)

time: 366 us -> 361 us (0.986)
  matrix products: 43.7 us -> 53.1 us
  Pallas kernels: 87 us -> 80.1 us
  other arithmetic: 19.1 us -> 12.4 us
    all_gather x1, waiting for transfers between devices: 0.02 us -> 24.9 us  [local(): gathered = lax.all_gather(tokens[:, sent_width:], PLANE, axis=0)]
    ppermute x2, waiting for transfers between devices: 63.9 us -> 44.2 us  [local(): halves = [lax.ppermute(piece, 'pipe', BACK) for piece in pieces]]
    dot_general x4 -> x7, matrix products: 43.7 us -> 53.1 us  [bf16_dot(): lax.dot_general(a, b, (dims, ((), ())), preferred_element_type=jnp.float32)]
    select_n x1, other arithmetic: 17 us -> 9.74 us  [local(): upper = jnp.where(core == 0, other, mine)]
    pallas_call x1, Pallas kernels: 14 us -> 7.63 us  [pick(): pl.pallas_call(pick_kernel, grid=(sources // SOURCES,), in_specs=[pl.Bloc...]
    all_to_all x5, waiting for transfers between devices: 87.2 us -> 81 us  [exchange(): return lax.all_to_all(block, PLANE, split_axis=0, concat_axis=0, tiled=True)]
  transfers between devices with their start and end apart: 11 -> 11, of which waited for: 7 -> 7; matrix products, arithmetic and copies ran while one was open for 17% -> 19% of each run, Pallas kernels for 20% -> 18%
where the time goes in v2:
time: 361 us; the launch traced here: 360 us
  waiting for transfers between devices  159 us (44%)
  Pallas kernels  80.1 us (22%)
  matrix products  53.1 us (15%)
  starting transfers between devices  35.7 us (10%)
  between operations  13.6 us (4%)
  other arithmetic  12.4 us (3%)
  local copies, waits for them, and re-layouts  6.01 us (2%)
    all_to_all x5, waiting for transfers between devices, exchange(): return lax.all_to_all(block, PLANE, split_axis=0, concat_axis=0, tiled=True)  81 us
    pallas_call x3, Pallas kernels, terms(): pl.pallas_call(functools.partial(term_kernel, n, based), grid=(steps, dep...  54.5 us
    dot_general x7, matrix products, bf16_dot(): lax.dot_general(a, b, (dims, ((), ())), preferred_element_type=jnp.float32)  53.1 us
    ppermute x2, waiting for transfers between devices, local(): halves = [lax.ppermute(piece, 'pipe', BACK) for piece in pieces]  44.2 us
    all_to_all x5, starting transfers between devices, exchange(): return lax.all_to_all(block, PLANE, split_axis=0, concat_axis=0, tiled=True)  32.6 us
    all_gather x1, waiting for transfers between devices, local(): gathered = lax.all_gather(tokens[:, sent_width:], PLANE, axis=0)  24.9 us
    pallas_call x2, Pallas kernels, place(): pl.pallas_call(place_kernel, grid=(2, steps), in_specs=[pl.BlockSpec((1,...  10.2 us
    select_n x1, other arithmetic, local(): upper = jnp.where(core == 0, other, mine)  9.74 us
  transfers between devices with their start and end apart: 11, of which 7 were waited for; matrix products, arithmetic and copies ran while one was open for 19% of the time, Pallas kernels for 18%

profile of v2, /device:TPU:24, one launch (start us, length us, event | category | flops | bytes accessed | tf_op | source)
XLA Modules:
  0.0 360.0 jit_solution(3627870684451006892)
XLA Ops:
  6.5 1.9 fusion.30
  10.2 2.9 convolution_convert_fusion
  13.1 8.3 %all-to-all-start = ((bf16[32,32,1664]{2,1,0:T(8,128)(2,1)}), bf16[32,32,1664]{2,1,0:T(8,128)(2,1)S(1)}, u32[]{:S(2)}, u32[]{:S(2)}) async-start(bf16[32,32,1664]{2,1,0:T(8,128)(2,1)} %bitcast.38), calls=%async_computation | async-start | bytes 6815744 | tf_op jit(solution)/shard_map/all_to_all | solution.py:22
  21.4 3.9 %cut_grads.3 = bf16[128,2,4096]{2,1,0:T(2,128)(2,1)} custom-call(bf16[128,2,8192]{2,1,0:T(2,128)(2,1)} %bitcast.34), custom_call_target="tpu_custom_call" | custom-call | bytes 4194304 | tf_op jit(solution)/shard_map/cut_grads/pallas_call | solution.py:125
  26.0 3.9 %cut_grads.2 = bf16[128,2,4096]{2,1,0:T(2,128)(2,1)} custom-call(bf16[128,2,8192]{2,1,0:T(2,128)(2,1)} %bitcast.35), custom_call_target="tpu_custom_call" | custom-call | bytes 4194304 | tf_op jit(solution)/shard_map/cut_grads/pallas_call | solution.py:125
  31.6 43.6 %collective-permute-done.2.grads_ref = bf16[128,2,4096]{2,1,0:T(2,128)(2,1)} collective-permute-done((bf16[128,2,4096]{2,1,0:T(2,128)(2,1)}, bf16[128,2,4096]{2,1,0:T(2,128)(2,1)}, u32[]{:S(2)}, u32[]{:S(2)}) %collective-permute-start.2) | collective-permute-done | bytes 2097184 | tf_op jit(solution)/shard_map/ppermute | solution.py:236
  75.2 5.1 %place_grads.3 = bf16[8,2,2,32,2048]{4,3,2,1,0:T(8,128)(2,1)} custom-call(s32[1,256]{1,0:T(1,128)} %add.66.target_ref, bf16[128,2,4096]{2,1,0:T(2,128)(2,1)} %collective-permute-done.2.grads_ref), custom_call_target="tpu_custom_call" | custom-call | flops 1073741824 | bytes 6291456 | tf_op jit(solution)/shard_map/place_grads/pallas_call | solution.py:52
  80.3 7.7 %all-to-all-start.2 = ((bf16[32,32,2048]{2,1,0:T(8,128)(2,1)}), bf16[32,32,2048]{2,1,0:T(8,128)(2,1)}, u32[]{:S(2)}, u32[]{:S(2)}) async-start(bf16[32,32,2048]{2,1,0:T(8,128)(2,1)} %bitcast.36), calls=%async_computation.2 | async-start | bytes 8388608 | tf_op jit(solution)/shard_map/all_to_all | solution.py:22
  89.2 9.7 %broadcast_select_fusion = (bf16[3072,2048]{1,0:T(8,128)(2,1)S(1)}, bf16[3072,2048]{1,0:T(8,128)(2,1)S(1)}) fusion(bf16[3072,2048]{1,0:T(8,128)(2,1)} %collective-permute-done, pred[]{:T(512)S(6)} %eq.100, bf16[1,1,3072,2048]{3,2,1,0:T(8,128)(2,1)} %param.9), kind=kLoop, calls=%fused_computation | loop fusion | flops 12582912 | bytes 50331648 | tf_op jit(solution)/shard_map/jit(_where)/select_n | solution.py:239
  99.0 9.7 %fusion.4 = f32[1024,2048]{1,0:T(8,128)} fusion(bf16[1024,1536]{1,0:T(8,128)(2,1)S(1)} %bitcast.44, bf16[3072,2048]{1,0:T(8,128)(2,1)S(1)} %get-tuple-element.17.refs_2_), kind=kOutput, calls=%fused_computation.8 | convolution fusion | flops 6442450944 | bytes 17825792 | tf_op jit(solution)/shard_map/dot_general | solution.py:35
  108.7 1.4 copy-done.1
  110.1 8.8 %fusion.6 = f32[1024,2048]{1,0:T(8,128)} fusion(bf16[1024,1536]{1,0:T(8,128)(2,1)S(1)} %bitcast.45, bf16[3072,2048]{1,0:T(8,128)(2,1)S(1)} %get-tuple-element.18.refs_2_), kind=kOutput, calls=%fused_computation.10 | convolution fusion | flops 6442450944 | bytes 17825792 | tf_op jit(solution)/shard_map/dot_general | solution.py:35
  119.5 5.1 %place_grads.2 = bf16[8,2,2,32,2048]{4,3,2,1,0:T(8,128)(2,1)} custom-call(s32[1,256]{1,0:T(1,128)} %bitcast.50, bf16[128,2,4096]{2,1,0:T(2,128)(2,1)} %collective-permute-done.1.grads_ref), custom_call_target="tpu_custom_call" | custom-call | flops 1073741824 | bytes 6291456 | tf_op jit(solution)/shard_map/place_grads/pallas_call | solution.py:52
  124.6 24.9 %all-gather.3.cloned.1.call-done = bf16[4096,1536]{1,0:T(8,128)(2,1)} async-done(((bf16[128,1536]{1,0:T(8,128)(2,1)}), bf16[4096,1536]{1,0:T(8,128)(2,1)}) %all-gather.3.cloned.1.call-update) | async-done | bytes 12582928 | tf_op jit(solution)/shard_map/all_gather | solution.py:212
  149.5 7.6 %pick_rows.1 = bf16[32,32,1536]{2,1,0:T(8,128)(2,1)} custom-call(bf16[32,32,128]{2,1,0:T(8,128)(2,1)} %slice.72.number_ref, bf16[32,128,1536]{2,1,0:T(8,128)(2,1)} %bitcast.42), custom_call_target="tpu_custom_call" | custom-call | flops 402653184 | bytes 15728640 | tf_op jit(solution)/shard_map/pick_rows/pallas_call | solution.py:99
  157.1 13.9 %multiply_convert_fusion.1.refs_1_ = bf16[1024,2048]{1,0:T(8,128)(2,1)} fusion(f32[1024,2048]{1,0:T(8,128)} %fusion.6, bf16[1024,1536]{1,0:T(8,128)(2,1)} %bitcast.46, bf16[3072,2048]{1,0:T(8,128)(2,1)} %copy-done.1), kind=kOutput, calls=%fused_computation.3 | convolution fusion | flops 6461325312 | bytes 22020096 | tf_op jit(solution)/shard_map/dot_general | solution.py:35
  171.0 7.5 %all-to-all-start.1 = ((bf16[32,32,2048]{2,1,0:T(8,128)(2,1)}), bf16[32,32,2048]{2,1,0:T(8,128)(2,1)}, u32[]{:S(2)}, u32[]{:S(2)}) async-start(bf16[32,32,2048]{2,1,0:T(8,128)(2,1)} %bitcast.37), calls=%async_computation.1 | async-start | bytes 8388608 | tf_op jit(solution)/shard_map/all_to_all | solution.py:22
  178.5 24.4 %terms.3.refs_3_ = f32[1024,3072]{1,0:T(8,128)} custom-call(bf16[1024,2048]{1,0:T(8,128)(2,1)} %bitcast.16.refs_0_, bf16[1024,2048]{1,0:T(8,128)(2,1)} %multiply_convert_fusion.1.refs_1_, bf16[3072,2048]{1,0:T(8,128)(2,1)} %copy-done.1), custom_call_target="tpu_custom_call" | custom-call | flops 12884901888 | bytes 33554432 | tf_op jit(solution)/shard_map/terms/pallas_call | solution.py:183
  203.0 13.8 %multiply_convert_fusion.refs_1_ = bf16[1024,2048]{1,0:T(8,128)(2,1)} fusion(f32[1024,2048]{1,0:T(8,128)} %fusion.4, bf16[1024,1536]{1,0:T(8,128)(2,1)S(1)} %bitcast.47, bf16[3072,2048]{1,0:T(8,128)(2,1)} %copy-done), kind=kOutput, calls=%fused_computation.2 | convolution fusion | flops 6461325312 | bytes 22020096 | tf_op jit(solution)/shard_map/dot_general | solution.py:35
  216.8 15.0 %all-to-all-done.1 = bf16[32,32,2048]{2,1,0:T(8,128)(2,1)} async-done(((bf16[32,32,2048]{2,1,0:T(8,128)(2,1)}), bf16[32,32,2048]{2,1,0:T(8,128)(2,1)}, u32[]{:S(2)}, u32[]{:S(2)}) %all-to-all-start.1) | async-done | bytes 4194336 | tf_op jit(solution)/shard_map/all_to_all | solution.py:22
  231.8 15.0 %terms.4 = bf16[1024,1536]{1,0:T(8,128)(2,1)} custom-call(bf16[1024,2048]{1,0:T(8,128)(2,1)} %bitcast.11.refs_0_, bf16[1024,2048]{1,0:T(8,128)(2,1)} %multiply_convert_fusion.refs_1_, bf16[3072,2048]{1,0:T(8,128)(2,1)} %copy-done, f32[1024,3072]{1,0:T(8,128)} %terms.3.refs_3_), custom_call_target="tpu_custom_call" | custom-call | flops 6442450944 | bytes 20971520 | tf_op jit(solution)/shard_map/terms/pallas_call | solution.py:183
  246.8 4.1 %all-to-all-start.3 = ((bf16[32,32,1536]{2,1,0:T(8,128)(2,1)}), bf16[32,32,1536]{2,1,0:T(8,128)(2,1)S(1)}, u32[]{:S(2)}, u32[]{:S(2)}) async-start(bf16[32,32,1536]{2,1,0:T(8,128)(2,1)} %bitcast.40), calls=%async_computation.3 | async-start | bytes 6291456 | tf_op jit(solution)/shard_map/all_to_all | solution.py:22
  250.9 15.0 %terms.5 = bf16[1024,1536]{1,0:T(8,128)(2,1)} custom-call(bf16[1024,2048]{1,0:T(8,128)(2,1)} %bitcast.11.refs_0_, bf16[1024,2048]{1,0:T(8,128)(2,1)} %multiply_convert_fusion.refs_1_, bf16[3072,2048]{1,0:T(8,128)(2,1)} %copy-done, f32[1024,3072]{1,0:T(8,128)} %terms.3.refs_3_), custom_call_target="tpu_custom_call" | custom-call | flops 6442450944 | bytes 20971520 | tf_op jit(solution)/shard_map/terms/pallas_call | solution.py:183
  265.9 26.7 %all-to-all-done.3 = bf16[32,32,1536]{2,1,0:T(8,128)(2,1)S(1)} async-done(((bf16[32,32,1536]{2,1,0:T(8,128)(2,1)}), bf16[32,32,1536]{2,1,0:T(8,128)(2,1)S(1)}, u32[]{:S(2)}, u32[]{:S(2)}) %all-to-all-start.3) | async-done | bytes 3145760 | tf_op jit(solution)/shard_map/all_to_all | solution.py:22
  292.7 5.1 %all-to-all-start.4 = ((bf16[32,32,1536]{2,1,0:T(8,128)(2,1)}), bf16[32,32,1536]{2,1,0:T(8,128)(2,1)}, u32[]{:S(2)}, u32[]{:S(2)}) async-start(bf16[32,32,1536]{2,1,0:T(8,128)(2,1)} %bitcast.39), calls=%async_computation.4 | async-start | bytes 6291456 | tf_op jit(solution)/shard_map/all_to_all | solution.py:22
  298.0 1.0 fusion.22
  299.1 0.9 collective-permute-start.3
  300.0 39.2 %all-to-all-done.4 = bf16[32,32,1536]{2,1,0:T(8,128)(2,1)} async-done(((bf16[32,32,1536]{2,1,0:T(8,128)(2,1)}), bf16[32,32,1536]{2,1,0:T(8,128)(2,1)}, u32[]{:S(2)}, u32[]{:S(2)}) %all-to-all-start.4) | async-done | bytes 3145760 | tf_op jit(solution)/shard_map/all_to_all | solution.py:22
  339.2 3.0 fusion.21
  342.3 0.9 collective-permute-start.4
  343.2 8.9 %collective-permute-done.4 = bf16[128,1536]{1,0:T(8,128)(2,1)S(1)} collective-permute-done((bf16[128,1536]{1,0:T(8,128)(2,1)S(1)}, bf16[128,1536]{1,0:T(8,128)(2,1)S(1)}, u32[]{:S(2)}, u32[]{:S(2)}) %collective-permute-start.4) | collective-permute-done | bytes 393248 | tf_op jit(solution)/shard_map/ppermute | solution.py:266
  352.1 1.0 maximum_bitcast_fusion
  (44 shorter events, 6.4 us)
Async XLA Ops:
  6.5 143.0 %all-gather.3.cloned.1.call-start = ((), (), s32[]{:S(2)}) async-start(), calls=%async_computation.5 | async-start | bytes 12976128 | tf_op jit(solution)/shard_map/all_gather | solution.py:212
  8.5 80.7 %collective-permute-start = (bf16[3072,2048]{1,0:T(8,128)(2,1)}, bf16[3072,2048]{1,0:T(8,128)(2,1)}, u32[]{:S(2)}, u32[]{:S(2)}) collective-permute-start(bf16[3072,2048]{1,0:T(8,128)(2,1)} %bitcast.43), channel_id=1, source_target_pairs={{0,1},{1,0},{2,3},{3,2},{4,5},{5,4},{6,7},{7,6},{8,9},{9,8},{10,11... | collective-permute-start | bytes 37748744 | tf_op jit(solution)/shard_map/ppermute | solution.py:237
  10.1 15.1 %copy-start.4 = (s32[128]{0:T(128)}, s32[128]{0:T(128)S(1)}, u32[]{:S(2)}) copy-start(s32[128]{0:T(128)S(1)} %get-tuple-element.16) | copy-start | bytes 1540
  13.1 67.2 %all-to-all-start = ((bf16[32,32,1664]{2,1,0:T(8,128)(2,1)}), bf16[32,32,1664]{2,1,0:T(8,128)(2,1)S(1)}, u32[]{:S(2)}, u32[]{:S(2)}) async-start(bf16[32,32,1664]{2,1,0:T(8,128)(2,1)} %bitcast.38), calls=%async_computation | async-start | bytes 6815744 | tf_op jit(solution)/shard_map/all_to_all | solution.py:22
  25.2 50.0 %collective-permute-start.2 = (bf16[128,2,4096]{2,1,0:T(2,128)(2,1)}, bf16[128,2,4096]{2,1,0:T(2,128)(2,1)}, u32[]{:S(2)}, u32[]{:S(2)}) collective-permute-start(bf16[128,2,4096]{2,1,0:T(2,128)(2,1)} %cut_grads.3), channel_id=1, source_target_pairs={{32,0},{64,32},{96,64},{0,96},{33,1},{65,33},{97,65},{1,97},{34,2}... | collective-permute-start | bytes 6291464 | tf_op jit(solution)/shard_map/ppermute | solution.py:236
  29.9 89.6 %collective-permute-start.1 = (bf16[128,2,4096]{2,1,0:T(2,128)(2,1)}, bf16[128,2,4096]{2,1,0:T(2,128)(2,1)}, u32[]{:S(2)}, u32[]{:S(2)}) collective-permute-start(bf16[128,2,4096]{2,1,0:T(2,128)(2,1)} %cut_grads.2), channel_id=1, source_target_pairs={{32,0},{64,32},{96,64},{0,96},{33,1},{65,33},{97,65},{1,97},{34,2}... | collective-permute-start | bytes 6291464 | tf_op jit(solution)/shard_map/ppermute | solution.py:236
  80.3 90.7 %all-to-all-start.2 = ((bf16[32,32,2048]{2,1,0:T(8,128)(2,1)}), bf16[32,32,2048]{2,1,0:T(8,128)(2,1)}, u32[]{:S(2)}, u32[]{:S(2)}) async-start(bf16[32,32,2048]{2,1,0:T(8,128)(2,1)} %bitcast.36), calls=%async_computation.2 | async-start | bytes 8388608 | tf_op jit(solution)/shard_map/all_to_all | solution.py:22
  99.0 9.8 %copy-start = (bf16[3072,2048]{1,0:T(8,128)(2,1)}, bf16[3072,2048]{1,0:T(8,128)(2,1)S(1)}, u32[]{:S(2)}) copy-start(bf16[3072,2048]{1,0:T(8,128)(2,1)S(1)} %get-tuple-element.17.refs_2_) | copy-start | bytes 37748740
  99.0 11.1 %copy-start.1 = (bf16[3072,2048]{1,0:T(8,128)(2,1)}, bf16[3072,2048]{1,0:T(8,128)(2,1)S(1)}, u32[]{:S(2)}) copy-start(bf16[3072,2048]{1,0:T(8,128)(2,1)S(1)} %get-tuple-element.18.refs_2_) | copy-start | bytes 37748740
  171.0 60.7 %all-to-all-start.1 = ((bf16[32,32,2048]{2,1,0:T(8,128)(2,1)}), bf16[32,32,2048]{2,1,0:T(8,128)(2,1)}, u32[]{:S(2)}, u32[]{:S(2)}) async-start(bf16[32,32,2048]{2,1,0:T(8,128)(2,1)} %bitcast.37), calls=%async_computation.1 | async-start | bytes 8388608 | tf_op jit(solution)/shard_map/all_to_all | solution.py:22
  178.5 24.4 %copy-start.2 = (bf16[32,32,1536]{2,1,0:T(8,128)(2,1)S(1)}, bf16[32,32,1536]{2,1,0:T(8,128)(2,1)}, u32[]{:S(2)}) copy-start(bf16[32,32,1536]{2,1,0:T(8,128)(2,1)} %pick_rows.1) | copy-start | bytes 9437188
  246.8 45.8 %all-to-all-start.3 = ((bf16[32,32,1536]{2,1,0:T(8,128)(2,1)}), bf16[32,32,1536]{2,1,0:T(8,128)(2,1)S(1)}, u32[]{:S(2)}, u32[]{:S(2)}) async-start(bf16[32,32,1536]{2,1,0:T(8,128)(2,1)} %bitcast.40), calls=%async_computation.3 | async-start | bytes 6291456 | tf_op jit(solution)/shard_map/all_to_all | solution.py:22
  265.9 31.8 %copy-start.6 = (f32[1,128,2]{1,2,0:T(2,128)S(1)}, f32[1,128,2]{1,2,0:T(2,128)}, u32[]{:S(2)}) copy-start(f32[1,128,2]{1,2,0:T(2,128)} %param.8) | copy-start | bytes 3076
  265.9 31.8 %copy-start.5 = (s32[128]{0:T(128)S(1)}, s32[128]{0:T(128)}, u32[]{:S(2)}) copy-start(s32[128]{0:T(128)} %copy-done.4) | copy-start | bytes 1540
  292.7 46.6 %all-to-all-start.4 = ((bf16[32,32,1536]{2,1,0:T(8,128)(2,1)}), bf16[32,32,1536]{2,1,0:T(8,128)(2,1)}, u32[]{:S(2)}, u32[]{:S(2)}) async-start(bf16[32,32,1536]{2,1,0:T(8,128)(2,1)} %bitcast.39), calls=%async_computation.4 | async-start | bytes 6291456 | tf_op jit(solution)/shard_map/all_to_all | solution.py:22
  298.0 1.1 copy-start.3
  299.1 44.1 %collective-permute-start.3 = (bf16[128,1536]{1,0:T(8,128)(2,1)S(1)}, bf16[128,1536]{1,0:T(8,128)(2,1)S(1)}, u32[]{:S(2)}, u32[]{:S(2)}) collective-permute-start(bf16[128,1536]{1,0:T(8,128)(2,1)S(1)} %fusion.13), channel_id=1, source_target_pairs={{32,0},{64,32},{96,64},{0,96},{33,1},{65,33},{97,65},{1,97},{34,2}... | collective-permute-start | bytes 1179656 | tf_op jit(solution)/shard_map/ppermute | solution.py:266
  342.3 9.8 %collective-permute-start.4 = (bf16[128,1536]{1,0:T(8,128)(2,1)S(1)}, bf16[128,1536]{1,0:T(8,128)(2,1)S(1)}, u32[]{:S(2)}, u32[]{:S(2)}) collective-permute-start(bf16[128,1536]{1,0:T(8,128)(2,1)S(1)} %fusion.12), channel_id=1, source_target_pairs={{32,0},{64,32},{96,64},{0,96},{33,1},{65,33},{97,65},{1,97},{34,2}... | collective-permute-start | bytes 1179656 | tf_op jit(solution)/shard_map/ppermute | solution.py:266
Sparse Core Ops, SparseCore 0:
  9.6 139.8 all-gather.2

commit v3 on v2

--- a/solution.py
+++ b/solution.py
@@ -1,5 +1,3 @@
-import functools
-
 import jax
 import jax.numpy as jnp
 from jax import lax
@@ -138,66 +136,8 @@
     )(grads)
 
 
-DEEP = 512
-WIDE = 768
-
-
-def term_kernel(n, based, *refs):
-    grads, slopes, weights = refs[:n], refs[n : 2 * n], refs[2 * n : 3 * n]
-    out_ref, gate, total = refs[-3:]
-    j, k = pl.program_id(0), pl.program_id(1)
-
-    @pl.when(j == 0)
-    def _():
-        for i in range(n):
-            product = grads[i][...].astype(jnp.float32) * slopes[i][...].astype(jnp.float32)
-            gate[n * k + i] = product.astype(jnp.bfloat16)
-
-    def step():
-        return sum(bf16_dot(gate[n * k + i], weights[i][...], ((1,), (1,))) for i in range(n))
-
-    last = pl.num_programs(1) - 1
-
-    @pl.when(k == 0)
-    def _():
-        total[...] = step() + refs[3 * n][...] if based else step()
-
-    @pl.when((k > 0) & (k < last))
-    def _():
-        total[...] += step()
-
-    @pl.when(k == last)
-    def _():
-        out_ref[...] = (total[...] + step()).astype(out_ref.dtype)
-
-
-def terms(grads, slopes, weights, first, columns, base=None, dtype=jnp.bfloat16):
-    n = len(grads)
-    rows, hidden = grads[0].shape
-    steps, offset, depth = columns // WIDE, first // WIDE, hidden // DEEP
-    side = pl.BlockSpec((rows, DEEP), lambda j, k: (0, jnp.where(j == 0, k, depth - 1)))
-    weight = pl.BlockSpec((WIDE, DEEP), lambda j, k: (offset + j, k))
-    column = pl.BlockSpec((rows, WIDE), lambda j, k: (0, j))
-    behind = pl.BlockSpec((rows, WIDE), lambda j, k: (0, offset + j))
-    based = base is not None
-    return pl.pallas_call(
-        functools.partial(term_kernel, n, based),
-        grid=(steps, depth),
-        in_specs=[side] * (2 * n) + [weight] * n + [behind] * based,
-        out_specs=column,
-        out_shape=jax.ShapeDtypeStruct((rows, columns), dtype),
-        scratch_shapes=[
-            pltpu.VMEM((n * depth, rows, DEEP), jnp.bfloat16),
-            pltpu.VMEM((rows, WIDE), jnp.float32),
-        ],
-        compiler_params=pltpu.CompilerParams(vmem_limit_bytes=VMEM),
-        cost_estimate=pl.CostEstimate(
-            flops=2 * n * rows * hidden * columns,
-            bytes_accessed=2 * n * hidden * (2 * rows + columns) + 4 * rows * columns,
-            transcendentals=0,
-        ),
-        name="terms",
-    )(*grads, *slopes, *weights, *([base] if based else []))
+def products(grads, slopes):
+    return (grads.astype(jnp.float32) * slopes.astype(jnp.float32)).astype(jnp.bfloat16)
 
 
 def local(acts, hid_grad, routes, probs, w_gate):
@@ -245,13 +185,17 @@
     target, below[0], below[1] = after(target, below[0], below[1])
     second = exchange(place(target, halves[1])).reshape(rows_here, hidden)
 
+    gathered, first = after(gathered, first)
     rows_1 = pick(numbers, gathered).reshape(rows_here, width - sent_width)
     slope_0 = after(derivative(below[0] + bf16_dot(rows_1, lower[sent_width:], ((1,), (0,)))))
-    early = terms([first], [slope_0], [lower], 0, width, dtype=jnp.float32)
-    rows_1, early = after(rows_1, early)
+    columns = width // COLUMN_PARTS
+    early = []
+    for j in range(COLUMN_PARTS):
+        part = lower[j * columns : (j + 1) * columns]
+        early.append(after(bf16_dot(products(*after(first, slope_0)), part, ((1,), (1,)))))
+    rows_1, early[0], early[1] = after(rows_1, *early)
     slope_1 = after(derivative(below[1] + bf16_dot(rows_1, upper[sent_width:], ((1,), (0,)))))
 
-    columns = width // COLUMN_PARTS
     hit = [by_token[:, k, None] == places[None, :] for k in range(TOP)]
     mix = sum(jnp.where(hit[k], probs[0][:, k, None], 0.0) for k in range(TOP))
     high = lax.reduce_precision(mix, 8, 7)
@@ -259,7 +203,9 @@
 
     parts = []
     for j in range(COLUMN_PARTS):
-        term = terms([second], [slope_1], [upper], j * columns, columns, base=early)
+        part = upper[j * columns : (j + 1) * columns]
+        late = bf16_dot(products(*after(second, slope_1)), part, ((1,), (1,)))
+        term = (early[j] + late).astype(jnp.bfloat16)
         returned = exchange(term.reshape(DEVICES, SHARE, columns)).reshape(-1, columns)
         both = bf16_dot(mix, returned, ((1,), (0,)))
         summed = (both[:n_tokens] + both[n_tokens:]).astype(jnp.bfloat16)

time: 361 us -> 347 us (0.961)
  Pallas kernels: 80.1 us -> 25.8 us
  matrix products: 53.1 us -> 99.7 us
  waiting for transfers between devices: 159 us -> 151 us
    pallas_call x3 -> x0, Pallas kernels: 54.5 us -> none  [terms(): pl.pallas_call(functools.partial(term_kernel, n, based), grid=(steps, dep...]
    dot_general x7 -> x11, matrix products: 53.1 us -> 99.7 us  [bf16_dot(): lax.dot_general(a, b, (dims, ((), ())), preferred_element_type=jnp.float32)]
    all_gather x1, waiting for transfers between devices: 24.9 us -> 0.02 us  [local(): gathered = lax.all_gather(tokens[:, sent_width:], PLANE, axis=0)]
    all_to_all x5, waiting for transfers between devices: 81 us -> 97.7 us  [exchange(): return lax.all_to_all(block, PLANE, split_axis=0, concat_axis=0, tiled=True)]
  transfers between devices with their start and end apart: 11 -> 11, of which waited for: 7 -> 6; matrix products, arithmetic and copies ran while one was open for 19% -> 29% of each run, Pallas kernels for 18% -> 7%
where the time goes in v3:
time: 347 us
  waiting for transfers between devices  151 us (44%)
  matrix products  99.7 us (29%)
  starting transfers between devices  35.9 us (10%)
  Pallas kernels  25.8 us (7%)
  between operations  13.7 us (4%)
  other arithmetic  12.4 us (4%)
  local copies, waits for them, and re-layouts  7.97 us (2%)
    dot_general x11, matrix products, bf16_dot(): lax.dot_general(a, b, (dims, ((), ())), preferred_element_type=jnp.float32)  99.7 us
    all_to_all x5, waiting for transfers between devices, exchange(): return lax.all_to_all(block, PLANE, split_axis=0, concat_axis=0, tiled=True)  97.7 us
    ppermute x2, waiting for transfers between devices, local(): halves = [lax.ppermute(piece, 'pipe', BACK) for piece in pieces]  44.4 us
    all_to_all x5, starting transfers between devices, exchange(): return lax.all_to_all(block, PLANE, split_axis=0, concat_axis=0, tiled=True)  32.8 us
    pallas_call x2, Pallas kernels, place(): pl.pallas_call(place_kernel, grid=(2, steps), in_specs=[pl.BlockSpec((1,...  10.1 us
    select_n x1, other arithmetic, local(): upper = jnp.where(core == 0, other, mine)  9.79 us
    ppermute x2, waiting for transfers between devices, local(): parts.append(lax.ppermute(summed, 'pipe', BACK))  9.05 us
    pallas_call x1, Pallas kernels, pick(): pl.pallas_call(pick_kernel, grid=(sources // SOURCES,), in_specs=[pl.Bloc...  7.92 us
  transfers between devices with their start and end apart: 11, of which 6 were waited for; matrix products, arithmetic and copies ran while one was open for 29% of the time, Pallas kernels for 7%

profile of v3, /device:TPU:24, one launch (start us, length us, event | category | flops | bytes accessed | tf_op | source)
XLA Modules:
  0.0 346.7 jit_solution(17342350988969197441)
XLA Ops:
  6.5 1.9 fusion.42
  10.2 2.8 convolution_convert_fusion
  13.1 8.3 %all-to-all-start = ((bf16[32,32,1664]{2,1,0:T(8,128)(2,1)}), bf16[32,32,1664]{2,1,0:T(8,128)(2,1)S(1)}, u32[]{:S(2)}, u32[]{:S(2)}) async-start(bf16[32,32,1664]{2,1,0:T(8,128)(2,1)} %bitcast.38), calls=%async_computation | async-start | bytes 6815744 | tf_op jit(solution)/shard_map/all_to_all | solution.py:20
  21.3 3.9 %cut_grads.2 = bf16[128,2,4096]{2,1,0:T(2,128)(2,1)} custom-call(bf16[128,2,8192]{2,1,0:T(2,128)(2,1)} %bitcast.34), custom_call_target="tpu_custom_call" | custom-call | bytes 4194304 | tf_op jit(solution)/shard_map/cut_grads/pallas_call | solution.py:123
  26.0 3.9 %cut_grads.3 = bf16[128,2,4096]{2,1,0:T(2,128)(2,1)} custom-call(bf16[128,2,8192]{2,1,0:T(2,128)(2,1)} %bitcast.35), custom_call_target="tpu_custom_call" | custom-call | bytes 4194304 | tf_op jit(solution)/shard_map/cut_grads/pallas_call | solution.py:123
  31.6 43.6 %collective-permute-done.grads_ref = bf16[128,2,4096]{2,1,0:T(2,128)(2,1)} collective-permute-done((bf16[128,2,4096]{2,1,0:T(2,128)(2,1)}, bf16[128,2,4096]{2,1,0:T(2,128)(2,1)}, u32[]{:S(2)}, u32[]{:S(2)}) %collective-permute-start) | collective-permute-done | bytes 2097184 | tf_op jit(solution)/shard_map/ppermute | solution.py:176
  75.2 5.1 %place_grads.2 = bf16[8,2,2,32,2048]{4,3,2,1,0:T(8,128)(2,1)} custom-call(s32[1,256]{1,0:T(1,128)} %add.71.target_ref, bf16[128,2,4096]{2,1,0:T(2,128)(2,1)} %collective-permute-done.grads_ref), custom_call_target="tpu_custom_call" | custom-call | flops 1073741824 | bytes 6291456 | tf_op jit(solution)/shard_map/place_grads/pallas_call | solution.py:50
  80.3 7.5 %all-to-all-start.1 = ((bf16[32,32,2048]{2,1,0:T(8,128)(2,1)}), bf16[32,32,2048]{2,1,0:T(8,128)(2,1)}, u32[]{:S(2)}, u32[]{:S(2)}) async-start(bf16[32,32,2048]{2,1,0:T(8,128)(2,1)} %bitcast.36), calls=%async_computation.1 | async-start | bytes 8388608 | tf_op jit(solution)/shard_map/all_to_all | solution.py:20
  89.0 9.8 %broadcast_select_fusion = (bf16[3072,2048]{1,0:T(8,128)(2,1)S(1)}, bf16[3072,2048]{1,0:T(8,128)(2,1)S(1)}) fusion(bf16[3072,2048]{1,0:T(8,128)(2,1)} %collective-permute-done.1, pred[]{:T(512)S(6)} %eq.100, bf16[1,1,3072,2048]{3,2,1,0:T(8,128)(2,1)} %param.9), kind=kLoop, calls=%fused_computation | loop fusion | flops 12582912 | bytes 50331648 | tf_op jit(solution)/shard_map/jit(_where)/select_n | solution.py:179
  98.8 9.8 %fusion.14 = f32[1024,2048]{1,0:T(8,128)} fusion(bf16[1024,1536]{1,0:T(8,128)(2,1)S(1)} %bitcast.47, bf16[3072,2048]{1,0:T(8,128)(2,1)S(1)} %get-tuple-element.32), kind=kOutput, calls=%fused_computation.22 | convolution fusion | flops 6442450944 | bytes 17825792 | tf_op jit(solution)/shard_map/dot_general | solution.py:33
  108.6 1.3 copy-done
  109.9 8.8 %fusion.10 = f32[1024,2048]{1,0:T(8,128)} fusion(bf16[1024,1536]{1,0:T(8,128)(2,1)S(1)} %bitcast.48, bf16[3072,2048]{1,0:T(8,128)(2,1)S(1)} %get-tuple-element.31), kind=kOutput, calls=%fused_computation.18 | convolution fusion | flops 6442450944 | bytes 17825792 | tf_op jit(solution)/shard_map/dot_general | solution.py:33
  119.5 5.0 %place_grads.3 = bf16[8,2,2,32,2048]{4,3,2,1,0:T(8,128)(2,1)} custom-call(s32[1,256]{1,0:T(1,128)} %bitcast.54, bf16[128,2,4096]{2,1,0:T(2,128)(2,1)} %collective-permute-done.2.grads_ref), custom_call_target="tpu_custom_call" | custom-call | flops 1073741824 | bytes 6291456 | tf_op jit(solution)/shard_map/place_grads/pallas_call | solution.py:50
  124.5 30.1 %all-to-all-done.1 = bf16[32,32,2048]{2,1,0:T(8,128)(2,1)} async-done(((bf16[32,32,2048]{2,1,0:T(8,128)(2,1)}), bf16[32,32,2048]{2,1,0:T(8,128)(2,1)}, u32[]{:S(2)}, u32[]{:S(2)}) %all-to-all-start.1) | async-done | bytes 4194336 | tf_op jit(solution)/shard_map/all_to_all | solution.py:20
  154.6 5.0 %all-to-all-start.2 = ((bf16[32,32,2048]{2,1,0:T(8,128)(2,1)}), bf16[32,32,2048]{2,1,0:T(8,128)(2,1)}, u32[]{:S(2)}, u32[]{:S(2)}) async-start(bf16[32,32,2048]{2,1,0:T(8,128)(2,1)} %bitcast.37), calls=%async_computation.2 | async-start | bytes 8388608 | tf_op jit(solution)/shard_map/all_to_all | solution.py:20
  159.7 7.9 %pick_rows.1 = bf16[32,32,1536]{2,1,0:T(8,128)(2,1)} custom-call(bf16[32,32,128]{2,1,0:T(8,128)(2,1)} %slice.73.number_ref, bf16[32,128,1536]{2,1,0:T(8,128)(2,1)} %bitcast.40), custom_call_target="tpu_custom_call" | custom-call | flops 402653184 | bytes 15728640 | tf_op jit(solution)/shard_map/pick_rows/pallas_call | solution.py:97
  167.6 12.6 %multiply_convert_fusion.3 = bf16[1024,2048]{1,0:T(8,128)(2,1)S(1)} fusion(f32[1024,2048]{1,0:T(8,128)} %fusion.14, bf16[1024,1536]{1,0:T(8,128)(2,1)} %bitcast.50, bf16[3072,2048]{1,0:T(8,128)(2,1)} %copy-done.1), kind=kOutput, calls=%fused_computation.5 | convolution fusion | flops 6461325312 | bytes 22020096 | tf_op jit(solution)/shard_map/dot_general | solution.py:33
  180.3 2.0 copy-done.10
  182.3 10.4 %fusion.12 = f32[1024,1536]{1,0:T(8,128)} fusion(bf16[3072,2048]{1,0:T(8,128)(2,1)S(1)} %bitcast.45, bf16[1024,2048]{1,0:T(8,128)(2,1)S(1)} %multiply_convert_fusion.3, bf16[1024,2048]{1,0:T(8,128)(2,1)} %bitcast.10), kind=kOutput, calls=%fused_computation.20 | convolution fusion | flops 6450839552 | bytes 20971520 | tf_op jit(solution)/shard_map/dot_general | solution.py:33
  192.6 11.0 %fusion.4 = f32[1024,1536]{1,0:T(8,128)} fusion(bf16[3072,2048]{1,0:T(8,128)(2,1)S(1)} %bitcast.45, bf16[1024,2048]{1,0:T(8,128)(2,1)} %copy-done.10, bf16[1024,2048]{1,0:T(8,128)(2,1)} %bitcast.10), kind=kOutput, calls=%fused_computation.12 | convolution fusion | flops 6450839552 | bytes 20971520 | tf_op jit(solution)/shard_map/dot_general | solution.py:33
  203.6 13.2 %multiply_convert_fusion.1 = bf16[1024,2048]{1,0:T(8,128)(2,1)} fusion(f32[1024,2048]{1,0:T(8,128)} %fusion.10, bf16[1024,1536]{1,0:T(8,128)(2,1)} %bitcast.51, bf16[3072,2048]{1,0:T(8,128)(2,1)S(1)} %bitcast.43), kind=kOutput, calls=%fused_computation.3 | convolution fusion | flops 6461325312 | bytes 22020096 | tf_op jit(solution)/shard_map/dot_general | solution.py:33
  216.8 13.6 %add_convert_fusion = bf16[1024,1536]{1,0:T(8,128)(2,1)} fusion(f32[1024,1536]{1,0:T(8,128)} %fusion.4, bf16[3072,2048]{1,0:T(8,128)(2,1)} %copy-done, bf16[1024,2048]{1,0:T(8,128)(2,1)} %multiply_convert_fusion.1, bf16[1024,2048]{1,0:T(8,128)(2,1)} %bitcast.16), kind=kOutput, calls=%fused_computation.6 | convolution fusion | flops 6453985280 | bytes 24117248 | tf_op jit(solution)/shard_map/dot_general | solution.py:33
  230.3 7.1 %all-to-all-start.4 = ((bf16[32,32,1536]{2,1,0:T(8,128)(2,1)}), bf16[32,32,1536]{2,1,0:T(8,128)(2,1)S(1)}, u32[]{:S(2)}, u32[]{:S(2)}) async-start(bf16[32,32,1536]{2,1,0:T(8,128)(2,1)} %bitcast.49), calls=%async_computation.4 | async-start | bytes 6291456 | tf_op jit(solution)/shard_map/all_to_all | solution.py:20
  237.5 13.7 %add_convert_fusion.1 = bf16[1024,1536]{1,0:T(8,128)(2,1)} fusion(f32[1024,1536]{1,0:T(8,128)} %fusion.12, bf16[3072,2048]{1,0:T(8,128)(2,1)} %copy-done, bf16[1024,2048]{1,0:T(8,128)(2,1)} %multiply_convert_fusion.1, bf16[1024,2048]{1,0:T(8,128)(2,1)} %bitcast.16), kind=kOutput, calls=%fused_computation.7 | convolution fusion | flops 6453985280 | bytes 24117248 | tf_op jit(solution)/shard_map/dot_general | solution.py:33
  251.2 28.1 %all-to-all-done.4 = bf16[32,32,1536]{2,1,0:T(8,128)(2,1)S(1)} async-done(((bf16[32,32,1536]{2,1,0:T(8,128)(2,1)}), bf16[32,32,1536]{2,1,0:T(8,128)(2,1)S(1)}, u32[]{:S(2)}, u32[]{:S(2)}) %all-to-all-start.4) | async-done | bytes 3145760 | tf_op jit(solution)/shard_map/all_to_all | solution.py:20
  279.3 4.8 %all-to-all-start.3 = ((bf16[32,32,1536]{2,1,0:T(8,128)(2,1)}), bf16[32,32,1536]{2,1,0:T(8,128)(2,1)}, u32[]{:S(2)}, u32[]{:S(2)}) async-start(bf16[32,32,1536]{2,1,0:T(8,128)(2,1)} %bitcast.46), calls=%async_computation.3 | async-start | bytes 6291456 | tf_op jit(solution)/shard_map/all_to_all | solution.py:20
  284.4 1.0 fusion.33
  285.4 0.9 collective-permute-start.4
  286.4 39.5 %all-to-all-done.3 = bf16[32,32,1536]{2,1,0:T(8,128)(2,1)} async-done(((bf16[32,32,1536]{2,1,0:T(8,128)(2,1)}), bf16[32,32,1536]{2,1,0:T(8,128)(2,1)}, u32[]{:S(2)}, u32[]{:S(2)}) %all-to-all-start.3) | async-done | bytes 3145760 | tf_op jit(solution)/shard_map/all_to_all | solution.py:20
  325.9 3.0 fusion.34
  329.8 9.0 %collective-permute-done.3 = bf16[128,1536]{1,0:T(8,128)(2,1)S(1)} collective-permute-done((bf16[128,1536]{1,0:T(8,128)(2,1)S(1)}, bf16[128,1536]{1,0:T(8,128)(2,1)S(1)}, u32[]{:S(2)}, u32[]{:S(2)}) %collective-permute-start.3) | collective-permute-done | bytes 393248 | tf_op jit(solution)/shard_map/ppermute | solution.py:212
  338.9 1.0 maximum_bitcast_fusion
  (67 shorter events, 7.4 us)
Async XLA Ops:
  6.5 153.2 %all-gather.3.cloned.1.call-start = ((), (), s32[]{:S(2)}) async-start(), calls=%async_computation.5 | async-start | bytes 12976128 | tf_op jit(solution)/shard_map/all_gather | solution.py:152
  8.5 80.5 %collective-permute-start.1 = (bf16[3072,2048]{1,0:T(8,128)(2,1)}, bf16[3072,2048]{1,0:T(8,128)(2,1)}, u32[]{:S(2)}, u32[]{:S(2)}) collective-permute-start(bf16[3072,2048]{1,0:T(8,128)(2,1)} %bitcast.41), channel_id=1, source_target_pairs={{0,1},{1,0},{2,3},{3,2},{4,5},{5,4},{6,7},{7,6},{8,9},{9,8},{10,11... | collective-permute-start | bytes 37748744 | tf_op jit(solution)/shard_map/ppermute | solution.py:177
  9.9 3.1 copy-start.3
  10.1 2.9 copy-start.5
  10.1 2.9 copy-start.7
  13.1 67.2 %all-to-all-start = ((bf16[32,32,1664]{2,1,0:T(8,128)(2,1)}), bf16[32,32,1664]{2,1,0:T(8,128)(2,1)S(1)}, u32[]{:S(2)}, u32[]{:S(2)}) async-start(bf16[32,32,1664]{2,1,0:T(8,128)(2,1)} %bitcast.38), calls=%async_computation | async-start | bytes 6815744 | tf_op jit(solution)/shard_map/all_to_all | solution.py:20
  25.2 50.0 %collective-permute-start = (bf16[128,2,4096]{2,1,0:T(2,128)(2,1)}, bf16[128,2,4096]{2,1,0:T(2,128)(2,1)}, u32[]{:S(2)}, u32[]{:S(2)}) collective-permute-start(bf16[128,2,4096]{2,1,0:T(2,128)(2,1)} %cut_grads.2), channel_id=1, source_target_pairs={{32,0},{64,32},{96,64},{0,96},{33,1},{65,33},{97,65},{1,97},{34,2}... | collective-permute-start | bytes 6291464 | tf_op jit(solution)/shard_map/ppermute | solution.py:176
  29.9 89.6 %collective-permute-start.2 = (bf16[128,2,4096]{2,1,0:T(2,128)(2,1)}, bf16[128,2,4096]{2,1,0:T(2,128)(2,1)}, u32[]{:S(2)}, u32[]{:S(2)}) collective-permute-start(bf16[128,2,4096]{2,1,0:T(2,128)(2,1)} %cut_grads.3), channel_id=1, source_target_pairs={{32,0},{64,32},{96,64},{0,96},{33,1},{65,33},{97,65},{1,97},{34,2}... | collective-permute-start | bytes 6291464 | tf_op jit(solution)/shard_map/ppermute | solution.py:176
  80.3 74.3 %all-to-all-start.1 = ((bf16[32,32,2048]{2,1,0:T(8,128)(2,1)}), bf16[32,32,2048]{2,1,0:T(8,128)(2,1)}, u32[]{:S(2)}, u32[]{:S(2)}) async-start(bf16[32,32,2048]{2,1,0:T(8,128)(2,1)} %bitcast.36), calls=%async_computation.1 | async-start | bytes 8388608 | tf_op jit(solution)/shard_map/all_to_all | solution.py:20
  98.8 9.8 %copy-start.1 = (bf16[3072,2048]{1,0:T(8,128)(2,1)}, bf16[3072,2048]{1,0:T(8,128)(2,1)S(1)}, u32[]{:S(2)}) copy-start(bf16[3072,2048]{1,0:T(8,128)(2,1)S(1)} %get-tuple-element.32) | copy-start | bytes 37748740
  98.8 11.1 %copy-start = (bf16[3072,2048]{1,0:T(8,128)(2,1)}, bf16[3072,2048]{1,0:T(8,128)(2,1)S(1)}, u32[]{:S(2)}) copy-start(bf16[3072,2048]{1,0:T(8,128)(2,1)S(1)} %get-tuple-element.31) | copy-start | bytes 37748740
  154.6 62.1 %all-to-all-start.2 = ((bf16[32,32,2048]{2,1,0:T(8,128)(2,1)}), bf16[32,32,2048]{2,1,0:T(8,128)(2,1)}, u32[]{:S(2)}, u32[]{:S(2)}) async-start(bf16[32,32,2048]{2,1,0:T(8,128)(2,1)} %bitcast.37), calls=%async_computation.2 | async-start | bytes 8388608 | tf_op jit(solution)/shard_map/all_to_all | solution.py:20
  159.7 22.5 %slice-start.3 = ((s8[12582912]{0:T(1024)(128)(4,1)}), s8[4194304]{0:T(1024)(128)(4,1)S(1)}, s32[]{:S(2)}) async-start(s8[12582912]{0:T(1024)(128)(4,1)} %bitcast.44), calls=%async_computation.9 | async-start | bytes 8388608
  167.6 14.6 %slice-start.4 = ((s8[12582912]{0:T(1024)(128)(4,1)}), s8[4194304]{0:T(1024)(128)(4,1)S(1)}, s32[]{:S(2)}) async-start(s8[12582912]{0:T(1024)(128)(4,1)} %bitcast.44), calls=%async_computation.10 | async-start | bytes 8388608
  167.6 14.6 %slice-start.5 = ((s8[12582912]{0:T(1024)(128)(4,1)}), s8[4194304]{0:T(1024)(128)(4,1)S(1)}, s32[]{:S(2)}) async-start(s8[12582912]{0:T(1024)(128)(4,1)} %bitcast.44), calls=%async_computation.11 | async-start | bytes 8388608
  180.2 2.0 copy-start.10
  182.2 21.3 %slice-start = ((s8[12582912]{0:T(1024)(128)(4,1)}), s8[4194304]{0:T(1024)(128)(4,1)S(1)}, s32[]{:S(2)}) async-start(s8[12582912]{0:T(1024)(128)(4,1)} %bitcast.42), calls=%async_computation.6 | async-start | bytes 8388608
  182.3 21.3 %slice-start.1 = ((s8[12582912]{0:T(1024)(128)(4,1)}), s8[4194304]{0:T(1024)(128)(4,1)S(1)}, s32[]{:S(2)}) async-start(s8[12582912]{0:T(1024)(128)(4,1)} %bitcast.42), calls=%async_computation.7 | async-start | bytes 8388608
  192.6 11.0 %slice-start.2 = ((s8[12582912]{0:T(1024)(128)(4,1)}), s8[4194304]{0:T(1024)(128)(4,1)S(1)}, s32[]{:S(2)}) async-start(s8[12582912]{0:T(1024)(128)(4,1)} %bitcast.42), calls=%async_computation.8 | async-start | bytes 8388608
  230.3 48.9 %all-to-all-start.4 = ((bf16[32,32,1536]{2,1,0:T(8,128)(2,1)}), bf16[32,32,1536]{2,1,0:T(8,128)(2,1)S(1)}, u32[]{:S(2)}, u32[]{:S(2)}) async-start(bf16[32,32,1536]{2,1,0:T(8,128)(2,1)} %bitcast.49), calls=%async_computation.4 | async-start | bytes 6291456 | tf_op jit(solution)/shard_map/all_to_all | solution.py:20
  251.2 32.9 %copy-start.9 = (f32[1,128,2]{1,2,0:T(2,128)S(1)}, f32[1,128,2]{1,2,0:T(2,128)}, u32[]{:S(2)}) copy-start(f32[1,128,2]{1,2,0:T(2,128)} %param.8) | copy-start | bytes 3076
  251.2 33.0 %copy-start.4 = (s32[1024]{0:T(1024)S(1)}, s32[1024]{0:T(1024)}, u32[]{:S(2)}) copy-start(s32[1024]{0:T(1024)} %copy-done.3) | copy-start | bytes 12292
  251.2 33.0 %copy-start.6 = (s32[128]{0:T(128)S(1)}, s32[128]{0:T(128)}, u32[]{:S(2)}) copy-start(s32[128]{0:T(128)} %copy-done.5) | copy-start | bytes 1540
  251.2 33.0 %copy-start.8 = (s32[128]{0:T(128)S(1)}, s32[128]{0:T(128)}, u32[]{:S(2)}) copy-start(s32[128]{0:T(128)} %copy-done.7) | copy-start | bytes 1540
  279.3 46.6 %all-to-all-start.3 = ((bf16[32,32,1536]{2,1,0:T(8,128)(2,1)}), bf16[32,32,1536]{2,1,0:T(8,128)(2,1)}, u32[]{:S(2)}, u32[]{:S(2)}) async-start(bf16[32,32,1536]{2,1,0:T(8,128)(2,1)} %bitcast.46), calls=%async_computation.3 | async-start | bytes 6291456 | tf_op jit(solution)/shard_map/all_to_all | solution.py:20
  284.4 1.1 copy-start.2
  285.4 44.4 %collective-permute-start.4 = (bf16[128,1536]{1,0:T(8,128)(2,1)S(1)}, bf16[128,1536]{1,0:T(8,128)(2,1)S(1)}, u32[]{:S(2)}, u32[]{:S(2)}) collective-permute-start(bf16[128,1536]{1,0:T(8,128)(2,1)S(1)} %fusion.24), channel_id=1, source_target_pairs={{32,0},{64,32},{96,64},{0,96},{33,1},{65,33},{97,65},{1,97},{34,2}... | collective-permute-start | bytes 1179656 | tf_op jit(solution)/shard_map/ppermute | solution.py:212
  328.9 10.0 %collective-permute-start.3 = (bf16[128,1536]{1,0:T(8,128)(2,1)S(1)}, bf16[128,1536]{1,0:T(8,128)(2,1)S(1)}, u32[]{:S(2)}, u32[]{:S(2)}) collective-permute-start(bf16[128,1536]{1,0:T(8,128)(2,1)S(1)} %fusion.25), channel_id=1, source_target_pairs={{32,0},{64,32},{96,64},{0,96},{33,1},{65,33},{97,65},{1,97},{34,2}... | collective-permute-start | bytes 1179656 | tf_op jit(solution)/shard_map/ppermute | solution.py:212
Sparse Core Ops, SparseCore 0:
  9.6 139.9 all-gather.2

commit v4 on v3

v4 whole, which is shorter than its diff:
```python
import functools

import jax
import jax.numpy as jnp
from jax import lax
from jax.experimental import pallas as pl
from jax.experimental.pallas import tpu as pltpu
from jax.sharding import Mesh, PartitionSpec as P

EXPERTS = 8
TOP = 2
SLOTS = 64
PLANE = ("z", "xp", "p", "core")
DEVICES = 32
SHARE = SLOTS // 2
BACK = [((i + 1) % 4, i) for i in range(4)]
COLUMN_PARTS = 2
SHARDS = 4
FIRST = 1536
VMEM = 56 * 1024 * 1024


def exchange(block):
    return lax.all_to_all(block, PLANE, split_axis=0, concat_axis=0, tiled=True)


def after(*values):
    return lax.optimization_barrier(values if len(values) > 1 else values[0])


def derivative(gate_pre):
    squash = jax.nn.sigmoid(gate_pre)
    return (squash * (1.0 + gate_pre * (1.0 - squash))).astype(jnp.bfloat16)


def bf16_dot(a, b, dims):
    return lax.dot_general(a, b, (dims, ((), ())), preferred_element_type=jnp.float32)


def place_kernel(target_ref, grads_ref, out_ref):
    tokens, top, columns = grads_ref.shape
    places = lax.broadcasted_iota(jnp.int32, (EXPERTS * SLOTS, tokens * top), 0)
    hit = jnp.where(places == target_ref[...], 1.0, 0.0).astype(jnp.bfloat16)
    grads = grads_ref[...].reshape(tokens * top, columns)
    placed = jnp.dot(hit, grads, preferred_element_type=jnp.float32).astype(jnp.bfloat16)
    out_ref[:, 0] = placed.reshape(EXPERTS, 2, SHARE, columns)


def place(target, grads):
    tokens, top, width = grads.shape
    pairs, hidden = tokens * top, width // 2
    columns = 1024
    steps = hidden // columns
    out = pl.pallas_call(
        place_kernel,
        grid=(2, steps),
        in_specs=[
            pl.BlockSpec((1, pairs), lambda p, j: (0, 0)),
            pl.BlockSpec((tokens, top, columns), lambda p, j: (0, 0, p * steps + j)),
        ],
        out_specs=pl.BlockSpec((EXPERTS, 1, 2, SHARE, columns), lambda p, j: (0, p, 0, 0, j)),
        out_shape=jax.ShapeDtypeStruct((EXPERTS, 2, 2, SHARE, hidden), jnp.bfloat16),
        compiler_params=pltpu.CompilerParams(vmem_limit_bytes=VMEM),
        cost_estimate=pl.CostEstimate(
            flops=4 * EXPERTS * SLOTS * pairs * hidden,
            bytes_accessed=4 * (EXPERTS * SLOTS + pairs) * hidden,
            transcendentals=0,
        ),
        name="place_grads",
    )(target.reshape(1, pairs), grads)
    return out.reshape(DEVICES, SHARE, hidden)


def cut_kernel(shards, start, size, in_ref, out_ref, sems):
    hidden = in_ref.shape[2] // shards
    copies = [
        pltpu.make_async_copy(
            in_ref.at[:, :, pl.ds(f * hidden + start, size)],
            out_ref.at[:, :, pl.ds(f * size, size)],
            sems.at[f],
        )
        for f in range(shards)
    ]
    for copy in copies:
        copy.start()
    for copy in copies:
        copy.wait()


def cut(grads, shards, start, size):
    tokens, top, _ = grads.shape
    return pl.pallas_call(
        functools.partial(cut_kernel, shards, start, size),
        in_specs=[pl.BlockSpec(memory_space=pl.ANY)],
        out_specs=pl.BlockSpec(memory_space=pl.ANY),
        out_shape=jax.ShapeDtypeStruct((tokens, top, shards * size), grads.dtype),
        scratch_shapes=[pltpu.SemaphoreType.DMA((shards,))],
        cost_estimate=pl.CostEstimate(
            flops=0, bytes_accessed=4 * tokens * top * shards * size, transcendentals=0
        ),
        name="cut_grads",
    )(grads)


def products(grads, slopes):
    return (grads.astype(jnp.float32) * slopes.astype(jnp.float32)).astype(jnp.bfloat16)


def local(acts, hid_grad, routes, probs, w_gate):
    tokens = acts[0]
    n_tokens, width = tokens.shape
    mine = w_gate[0, 0]
    hidden = mine.shape[1]
    core = lax.axis_index("core")
    rows_here = DEVICES * SHARE

    flat_expert = routes[0].reshape(-1)
    pairs = flat_expert.shape[0]
    number = jnp.arange(pairs, dtype=jnp.int32)
    earlier = (flat_expert[:, None] == flat_expert[None, :]) & (number[None, :] < number[:, None])
    slot = jnp.sum(earlier.astype(jnp.int32), axis=1)
    target = flat_expert * SLOTS + slot
    by_token = target.reshape(n_tokens, TOP)

    places = jnp.arange(EXPERTS * SLOTS, dtype=jnp.int32).reshape(EXPERTS, 1, SLOTS)
    places = jnp.broadcast_to(places, (EXPERTS, 2, SLOTS)).reshape(-1)
    row_hit = [places[:, None] == by_token[None, :, k] for k in range(TOP)]
    place_token = (row_hit[0] | row_hit[1]).astype(jnp.bfloat16)
    sent = bf16_dot(place_token, tokens, ((1,), (0,))).astype(jnp.bfloat16)
    rows = exchange(sent.reshape(DEVICES, SHARE, width)).reshape(rows_here, width)

    shares = ((0, FIRST), (FIRST, hidden - FIRST))
    pieces = [cut(hid_grad[0], SHARDS, *share) for share in shares]
    parts = [lax.ppermute(piece, "pipe", BACK) for piece in pieces]
    other = lax.ppermute(mine, "core", [(0, 1), (1, 0)])
    shard = (jnp.where(core == 0, mine, other), jnp.where(core == 0, other, mine))
    weights = [
        jnp.concatenate([w[:, start : start + size] for w in shard], axis=1)
        for start, size in shares
    ]
    weights = list(after(*weights))

    placed = place(target, parts[0])
    first = exchange(placed).reshape(rows_here, 2 * FIRST)
    slopes = [after(derivative(bf16_dot(rows, w, ((1,), (0,))))) for w in weights]
    target, *slopes = after(target, *slopes)
    second = exchange(place(target, parts[1])).reshape(rows_here, 2 * (hidden - FIRST))

    columns = width // COLUMN_PARTS
    early = []
    for j in range(COLUMN_PARTS):
        part = weights[0][j * columns : (j + 1) * columns]
        early.append(after(bf16_dot(products(*after(first, slopes[0])), part, ((1,), (1,)))))
    hit = [by_token[:, k, None] == places[None, :] for k in range(TOP)]
    mix = sum(jnp.where(hit[k], probs[0][:, k, None], 0.0) for k in range(TOP))
    high = lax.reduce_precision(mix, 8, 7)
    mix = jnp.concatenate([high, mix - high]).astype(jnp.bfloat16)

    outs = []
    for j in range(COLUMN_PARTS):
        part = weights[1][j * columns : (j + 1) * columns]
        late = bf16_dot(products(*after(second, slopes[1])), part, ((1,), (1,)))
        term = (early[j] + late).astype(jnp.bfloat16)
        returned = exchange(term.reshape(DEVICES, SHARE, columns)).reshape(-1, columns)
        both = bf16_dot(mix, returned, ((1,), (0,)))
        summed = (both[:n_tokens] + both[n_tokens:]).astype(jnp.bfloat16)
        outs.append(lax.ppermute(summed, "pipe", BACK))
    return jnp.concatenate(outs, axis=1)[None]


def solution(mesh):
    fine = Mesh(mesh.devices.reshape(4, 4, 2, 2, 2), ("pipe",) + PLANE)
    placed = (
        P("pipe", PLANE, None),
        P("pipe", PLANE, None, None),
        P("pipe", PLANE, None),
        P("pipe", PLANE, None),
        P("pipe", PLANE, None, None),
    )
    return jax.shard_map(
        local, mesh=fine, in_specs=placed, out_specs=P("pipe", PLANE, None), check_vma=False
    )
```

time: 347 us -> 475 us (1.37)
  Pallas kernels: 25.8 us -> 139 us
  other arithmetic: 12.4 us -> 34.6 us
  local copies, waits for them, and re-layouts: 7.97 us -> 27.4 us
  between operations: 13.7 us -> 0.29 us
  waiting for transfers between devices: 151 us -> 139 us
    pallas_call x3 -> x2, Pallas kernels: 15.7 us -> 129 us  [cut(): pl.pallas_call(functools.partial(cut_kernel, shards, start, size), in_spe...]
    ppermute x4, waiting for transfers between devices: 53.4 us -> 33 us  [the longest x2 23.2 us: local(): parts = [lax.ppermute(piece, 'pipe', BACK) for piece in pieces]]
    concatenate x0 -> x2, other arithmetic: none -> 18.7 us  [local(): jnp.concatenate([w[:, start:start + size] for w in shard], axis=1)]
    slice x3 -> x4, local copies, waits for them, and re-layouts: 3.05 us -> 21.6 us  [local(): w[:, start:start + size]]
    all_to_all x5, waiting for transfers between devices: 97.7 us -> 106 us  [exchange(): return lax.all_to_all(block, PLANE, split_axis=0, concat_axis=0, tiled=True)]
    dot_general x11 -> x9, matrix products: 99.7 us -> 101 us  [bf16_dot(): lax.dot_general(a, b, (dims, ((), ())), preferred_element_type=jnp.float32)]
  transfers between devices with their start and end apart: 11 -> 10, of which waited for: 6 -> 6; matrix products, arithmetic and copies ran while one was open for 29% -> 31% of each run, Pallas kernels for 7% -> 29%
where the time goes in v4:
time: 475 us; the launch traced here: 474 us
  Pallas kernels  139 us (29%)
  waiting for transfers between devices  139 us (29%)
  matrix products  101 us (21%)
  other arithmetic  34.6 us (7%)
  starting transfers between devices  32.5 us (7%)
  local copies, waits for them, and re-layouts  27.4 us (6%)
    pallas_call x2, Pallas kernels, cut(): pl.pallas_call(functools.partial(cut_kernel, shards, start, size), in_spe...  129 us
    all_to_all x5, waiting for transfers between devices, exchange(): return lax.all_to_all(block, PLANE, split_axis=0, concat_axis=0, tiled=True)  106 us
    dot_general x9, matrix products, bf16_dot(): lax.dot_general(a, b, (dims, ((), ())), preferred_element_type=jnp.float32)  101 us
    all_to_all x5, starting transfers between devices, exchange(): return lax.all_to_all(block, PLANE, split_axis=0, concat_axis=0, tiled=True)  31 us
    ppermute x2, waiting for transfers between devices, local(): parts = [lax.ppermute(piece, 'pipe', BACK) for piece in pieces]  23.2 us
    slice x4, local copies, waits for them, and re-layouts, local(): w[:, start:start + size]  21.6 us
    concatenate x2, other arithmetic, local(): jnp.concatenate([w[:, start:start + size] for w in shard], axis=1)  18.7 us
    select_n x1, other arithmetic, local(): jnp.where(core == 0, mine, other)  13.3 us
  transfers between devices with their start and end apart: 10, of which 6 were waited for; matrix products, arithmetic and copies ran while one was open for 31% of the time, Pallas kernels for 29%

profile of v4, /device:TPU:24, one launch (start us, length us, event | category | flops | bytes accessed | tf_op | source)
XLA Modules:
  0.0 474.5 jit_solution(11838136718131628011)
XLA Ops:
  0.0 96.4 %cut_grads.2 = bf16[128,2,6144]{2,1,0:T(2,128)(2,1)} custom-call(bf16[128,2,8192]{2,1,0:T(2,128)(2,1)} %bitcast.36), custom_call_target="tpu_custom_call" | custom-call | bytes 6291456 | tf_op jit(solution)/shard_map/cut_grads/pallas_call | solution.py:92
  98.2 4.6 convolution_convert_fusion
  102.7 8.3 %all-to-all-start.1 = ((bf16[32,32,3072]{2,1,0:T(8,128)(2,1)}), bf16[32,32,3072]{2,1,0:T(8,128)(2,1)}, u32[]{:S(2)}, u32[]{:S(2)}) async-start(bf16[32,32,3072]{2,1,0:T(8,128)(2,1)} %bitcast.34), calls=%async_computation.1 | async-start | bytes 12582912 | tf_op jit(solution)/shard_map/all_to_all | solution.py:24
  111.0 32.9 %cut_grads.3 = bf16[128,2,2048]{2,1,0:T(2,128)(2,1)} custom-call(bf16[128,2,8192]{2,1,0:T(2,128)(2,1)} %bitcast.37), custom_call_target="tpu_custom_call" | custom-call | bytes 2097152 | tf_op jit(solution)/shard_map/cut_grads/pallas_call | solution.py:92
  145.8 23.2 %collective-permute-done.grads_ref = bf16[128,2,6144]{2,1,0:T(2,128)(2,1)} collective-permute-done((bf16[128,2,6144]{2,1,0:T(2,128)(2,1)}, bf16[128,2,6144]{2,1,0:T(2,128)(2,1)}, u32[]{:S(2)}, u32[]{:S(2)}) %collective-permute-start) | collective-permute-done | bytes 3145760 | tf_op jit(solution)/shard_map/ppermute | solution.py:134
  168.9 7.1 %place_grads.2 = bf16[8,2,2,32,3072]{4,3,2,1,0:T(8,128)(2,1)} custom-call(s32[1,256]{1,0:T(1,128)} %add.53.target_ref, bf16[128,2,6144]{2,1,0:T(2,128)(2,1)} %collective-permute-done.grads_ref), custom_call_target="tpu_custom_call" | custom-call | flops 1610612736 | bytes 9437184 | tf_op jit(solution)/shard_map/place_grads/pallas_call | solution.py:54
  176.0 13.3 %broadcast_select_fusion.1 = (bf16[3072,2048]{1,0:T(8,128)(2,1)S(1)}, bf16[3072,2048]{1,0:T(8,128)(2,1)}) fusion(bf16[3072,2048]{1,0:T(8,128)(2,1)} %collective-permute-done.1, pred[]{:T(512)S(6)} %eq.100, bf16[1,1,3072,2048]{3,2,1,0:T(8,128)(2,1)} %param.9), kind=kLoop, calls=%fused_computation.4 | loop fusion | flops 12582912 | bytes 50331648 | tf_op jit(solution)/shard_map/jit(_where)/select_n | solution.py:136
  189.3 4.5 copy-done.2
  193.8 2.0 slice.70
  195.9 7.9 %slice.68 = bf16[3072,1536]{1,0:T(8,128)(2,1)} slice(bf16[3072,2048]{1,0:T(8,128)(2,1)} %copy-done.2), slice={[0:3072], [0:1536]} | slice | bytes 18874368 | tf_op jit(solution)/shard_map/slice | solution.py:138
  203.8 3.8 slice.71
  207.5 8.0 %slice.69 = bf16[3072,1536]{1,0:T(8,128)(2,1)} slice(bf16[3072,2048]{1,0:T(8,128)(2,1)} %get-tuple-element.26), slice={[0:3072], [0:1536]} | slice | bytes 18874368 | tf_op jit(solution)/shard_map/slice | solution.py:138
  215.5 6.8 %pad_maximum_fusion.1 = bf16[3072,1024]{1,0:T(8,128)(2,1)} fusion(bf16[3072,512]{1,0:T(8,128)(2,1)} %slice.71, bf16[3072,512]{1,0:T(8,128)(2,1)} %slice.70), kind=kLoop, calls=%fused_computation.9 | loop fusion | flops 12582912 | bytes 12582912 | tf_op jit(solution)/shard_map/concatenate | solution.py:138
  222.6 11.9 %pad_maximum_fusion = bf16[3072,3072]{1,0:T(8,128)(2,1)} fusion(bf16[3072,1536]{1,0:T(8,128)(2,1)S(1)} %copy-done.3, bf16[3072,1536]{1,0:T(8,128)(2,1)} %slice.68), kind=kLoop, calls=%fused_computation | loop fusion | flops 37748736 | bytes 37748736 | tf_op jit(solution)/shard_map/concatenate | solution.py:138
  234.5 8.6 %all-to-all-start = ((bf16[32,32,3072]{2,1,0:T(8,128)(2,1)}), bf16[32,32,3072]{2,1,0:T(8,128)(2,1)}, u32[]{:S(2)}, u32[]{:S(2)}) async-start(bf16[32,32,3072]{2,1,0:T(8,128)(2,1)} %bitcast.35), calls=%async_computation | async-start | bytes 12582912 | tf_op jit(solution)/shard_map/all_to_all | solution.py:24
  243.1 27.8 %multiply_convert_fusion.1 = bf16[1024,3072]{1,0:T(8,128)(2,1)} fusion(bf16[1024,3072]{1,0:T(8,128)(2,1)} %bitcast.10, bf16[3072,3072]{1,0:T(8,128)(2,1)} %pad_maximum_fusion), kind=kOutput, calls=%fused_computation.2 | convolution fusion | flops 19352518656 | bytes 31457280 | tf_op jit(solution)/shard_map/dot_general | solution.py:37
  270.9 10.5 %multiply_convert_fusion.3 = bf16[1024,1024]{1,0:T(8,128)(2,1)} fusion(bf16[1024,3072]{1,0:T(8,128)(2,1)} %bitcast.10, bf16[3072,1024]{1,0:T(8,128)(2,1)S(1)} %bitcast.41), kind=kOutput, calls=%fused_computation.14 | convolution fusion | flops 6450839552 | bytes 14680064 | tf_op jit(solution)/shard_map/dot_general | solution.py:37
  281.4 39.4 %all-to-all-done = bf16[32,32,3072]{2,1,0:T(8,128)(2,1)} async-done(((bf16[32,32,3072]{2,1,0:T(8,128)(2,1)}), bf16[32,32,3072]{2,1,0:T(8,128)(2,1)}, u32[]{:S(2)}, u32[]{:S(2)}) %all-to-all-start) | async-done | bytes 6291488 | tf_op jit(solution)/shard_map/all_to_all | solution.py:24
  320.8 2.9 place_grads.3
  323.8 4.2 all-to-all-start.2
  328.0 17.4 %fusion.2 = f32[1024,1536]{1,0:T(8,128)} fusion(bf16[3072,3072]{1,0:T(8,128)(2,1)} %pad_maximum_fusion, bf16[1024,3072]{1,0:T(8,128)(2,1)} %multiply_convert_fusion.1, bf16[1024,3072]{1,0:T(8,128)(2,1)} %bitcast.7), kind=kOutput, calls=%fused_computation.7 | convolution fusion | flops 9676259328 | bytes 28311552 | tf_op jit(solution)/shard_map/dot_general | solution.py:37
  345.4 12.3 %all-to-all-done.2 = bf16[32,32,1024]{2,1,0:T(8,128)(2,1)S(1)} async-done(((bf16[32,32,1024]{2,1,0:T(8,128)(2,1)}), bf16[32,32,1024]{2,1,0:T(8,128)(2,1)S(1)}, u32[]{:S(2)}, u32[]{:S(2)}) %all-to-all-start.2) | async-done | bytes 2097184 | tf_op jit(solution)/shard_map/all_to_all | solution.py:24
  357.8 9.7 %add_convert_fusion.1 = bf16[1024,1536]{1,0:T(8,128)(2,1)} fusion(f32[1024,1536]{1,0:T(8,128)} %fusion.2, bf16[3072,1024]{1,0:T(8,128)(2,1)} %pad_maximum_fusion.1, bf16[1024,1024]{1,0:T(8,128)(2,1)} %multiply_convert_fusion.3, bf16[1024,1024]{1,0:T(8,128)(2,1)S(1)} %bitcast.44), kind=kOutput, calls=%fused_computation.11 | convolution fusion | flops 3228565504 | bytes 16777216 | tf_op jit(solution)/shard_map/dot_general | solution.py:37
  367.4 5.1 %all-to-all-start.3 = ((bf16[32,32,1536]{2,1,0:T(8,128)(2,1)}), bf16[32,32,1536]{2,1,0:T(8,128)(2,1)}, u32[]{:S(2)}, u32[]{:S(2)}) async-start(bf16[32,32,1536]{2,1,0:T(8,128)(2,1)} %bitcast.43), calls=%async_computation.3 | async-start | bytes 6291456 | tf_op jit(solution)/shard_map/all_to_all | solution.py:24
  372.5 17.5 %fusion = f32[1024,1536]{1,0:T(8,128)} fusion(bf16[3072,3072]{1,0:T(8,128)(2,1)} %pad_maximum_fusion, bf16[1024,3072]{1,0:T(8,128)(2,1)} %multiply_convert_fusion.1, bf16[1024,3072]{1,0:T(8,128)(2,1)} %bitcast.7), kind=kOutput, calls=%fused_computation.5 | convolution fusion | flops 9676259328 | bytes 28311552 | tf_op jit(solution)/shard_map/dot_general | solution.py:37
  390.1 7.7 %add_convert_fusion = bf16[1024,1536]{1,0:T(8,128)(2,1)} fusion(f32[1024,1536]{1,0:T(8,128)} %fusion, bf16[3072,1024]{1,0:T(8,128)(2,1)} %pad_maximum_fusion.1, bf16[1024,1024]{1,0:T(8,128)(2,1)S(1)} %copy-done.12, bf16[1024,1024]{1,0:T(8,128)(2,1)S(1)} %bitcast.45), kind=kOutput, calls=%fused_computation.10 | convolution fusion | flops 3228565504 | bytes 16777216 | tf_op jit(solution)/shard_map/dot_general | solution.py:37
  397.8 16.2 %all-to-all-done.3 = bf16[32,32,1536]{2,1,0:T(8,128)(2,1)} async-done(((bf16[32,32,1536]{2,1,0:T(8,128)(2,1)}), bf16[32,32,1536]{2,1,0:T(8,128)(2,1)}, u32[]{:S(2)}, u32[]{:S(2)}) %all-to-all-start.3) | async-done | bytes 3145760 | tf_op jit(solution)/shard_map/all_to_all | solution.py:24
  414.0 4.8 %all-to-all-start.4 = ((bf16[32,32,1536]{2,1,0:T(8,128)(2,1)}), bf16[32,32,1536]{2,1,0:T(8,128)(2,1)}, u32[]{:S(2)}, u32[]{:S(2)}) async-start(bf16[32,32,1536]{2,1,0:T(8,128)(2,1)} %bitcast.42), calls=%async_computation.4 | async-start | bytes 6291456 | tf_op jit(solution)/shard_map/all_to_all | solution.py:24
  419.1 2.9 fusion.14
  422.2 38.4 %all-to-all-done.4 = bf16[32,32,1536]{2,1,0:T(8,128)(2,1)} async-done(((bf16[32,32,1536]{2,1,0:T(8,128)(2,1)}), bf16[32,32,1536]{2,1,0:T(8,128)(2,1)}, u32[]{:S(2)}, u32[]{:S(2)}) %all-to-all-start.4) | async-done | bytes 3145760 | tf_op jit(solution)/shard_map/all_to_all | solution.py:24
  460.6 2.9 fusion.13
  463.6 9.9 %collective-permute-done.4 = bf16[128,1536]{1,0:T(8,128)(2,1)S(1)} collective-permute-done((bf16[128,1536]{1,0:T(8,128)(2,1)S(1)}, bf16[128,1536]{1,0:T(8,128)(2,1)S(1)}, u32[]{:S(2)}, u32[]{:S(2)}) %collective-permute-start.4) | collective-permute-done | bytes 393248 | tf_op jit(solution)/shard_map/ppermute | solution.py:167
  (57 shorter events, 5.4 us)
Async XLA Ops:
  0.0 98.2 %copy-start = (bf16[1,128,3072]{2,1,0:T(8,128)(2,1)S(1)}, bf16[1,128,3072]{2,1,0:T(8,128)(2,1)}, u32[]{:S(2)}) copy-start(bf16[1,128,3072]{2,1,0:T(8,128)(2,1)} %param.5) | copy-start | bytes 2359300
  0.0 97.3 %copy-start.10 = (s32[1,128,2]{1,2,0:T(2,128)S(1)}, s32[1,128,2]{1,2,0:T(2,128)}, u32[]{:S(2)}) copy-start(s32[1,128,2]{1,2,0:T(2,128)} %param.7) | copy-start | bytes 3076
  0.0 176.0 %collective-permute-start.1 = (bf16[3072,2048]{1,0:T(8,128)(2,1)}, bf16[3072,2048]{1,0:T(8,128)(2,1)}, u32[]{:S(2)}, u32[]{:S(2)}) collective-permute-start(bf16[3072,2048]{1,0:T(8,128)(2,1)} %bitcast.38), channel_id=1, source_target_pairs={{0,1},{1,0},{2,3},{3,2},{4,5},{5,4},{6,7},{7,6},{8,9},{9,8},{10,11... | collective-permute-start | bytes 37748744 | tf_op jit(solution)/shard_map/ppermute | solution.py:135
  96.5 72.5 %collective-permute-start = (bf16[128,2,6144]{2,1,0:T(2,128)(2,1)}, bf16[128,2,6144]{2,1,0:T(2,128)(2,1)}, u32[]{:S(2)}, u32[]{:S(2)}) collective-permute-start(bf16[128,2,6144]{2,1,0:T(2,128)(2,1)} %cut_grads.2), channel_id=1, source_target_pairs={{32,0},{64,32},{96,64},{0,96},{33,1},{65,33},{97,65},{1,97},{34,2}... | collective-permute-start | bytes 9437192 | tf_op jit(solution)/shard_map/ppermute | solution.py:134
  98.0 4.8 %copy-start.4 = (s32[1024]{0:T(1024)}, s32[1024]{0:T(1024)S(1)}, u32[]{:S(2)}) copy-start(s32[1024]{0:T(1024)S(1)} %eq.89) | copy-start | bytes 12292
  98.2 4.6 copy-start.6
  98.2 4.6 copy-start.8
  102.7 131.8 %all-to-all-start.1 = ((bf16[32,32,3072]{2,1,0:T(8,128)(2,1)}), bf16[32,32,3072]{2,1,0:T(8,128)(2,1)}, u32[]{:S(2)}, u32[]{:S(2)}) async-start(bf16[32,32,3072]{2,1,0:T(8,128)(2,1)} %bitcast.34), calls=%async_computation.1 | async-start | bytes 12582912 | tf_op jit(solution)/shard_map/all_to_all | solution.py:24
  144.0 176.9 %collective-permute-start.2 = (bf16[128,2,2048]{2,1,0:T(2,128)(2,1)}, bf16[128,2,2048]{2,1,0:T(2,128)(2,1)}, u32[]{:S(2)}, u32[]{:S(2)}) collective-permute-start(bf16[128,2,2048]{2,1,0:T(2,128)(2,1)} %cut_grads.3), channel_id=1, source_target_pairs={{32,0},{64,32},{96,64},{0,96},{33,1},{65,33},{97,65},{1,97},{34,2}... | collective-permute-start | bytes 3145736 | tf_op jit(solution)/shard_map/ppermute | solution.py:134
  189.3 4.5 copy-start.2
  215.5 7.1 %copy-start.3 = (bf16[3072,1536]{1,0:T(8,128)(2,1)S(1)}, bf16[3072,1536]{1,0:T(8,128)(2,1)}, u32[]{:S(2)}) copy-start(bf16[3072,1536]{1,0:T(8,128)(2,1)} %slice.69) | copy-start | bytes 28311556
  234.5 36.4 %slice-start = ((s8[6291456]{0:T(1024)(128)(4,1)}), s8[2097152]{0:T(1024)(128)(4,1)S(1)}, s32[]{:S(2)}) async-start(s8[6291456]{0:T(1024)(128)(4,1)} %bitcast.40), calls=%async_computation.5 | async-start | bytes 4194304
  234.5 86.3 %all-to-all-start = ((bf16[32,32,3072]{2,1,0:T(8,128)(2,1)}), bf16[32,32,3072]{2,1,0:T(8,128)(2,1)}, u32[]{:S(2)}, u32[]{:S(2)}) async-start(bf16[32,32,3072]{2,1,0:T(8,128)(2,1)} %bitcast.35), calls=%async_computation | async-start | bytes 12582912 | tf_op jit(solution)/shard_map/all_to_all | solution.py:24
  243.1 27.8 %slice-start.1 = ((s8[6291456]{0:T(1024)(128)(4,1)}), s8[4194304]{0:T(1024)(128)(4,1)S(1)}, s32[]{:S(2)}) async-start(s8[6291456]{0:T(1024)(128)(4,1)} %bitcast.40), calls=%async_computation.6 | async-start | bytes 8388608
  323.8 34.0 %all-to-all-start.2 = ((bf16[32,32,1024]{2,1,0:T(8,128)(2,1)}), bf16[32,32,1024]{2,1,0:T(8,128)(2,1)S(1)}, u32[]{:S(2)}, u32[]{:S(2)}) async-start(bf16[32,32,1024]{2,1,0:T(8,128)(2,1)} %bitcast.39), calls=%async_computation.2 | async-start | bytes 4194304 | tf_op jit(solution)/shard_map/all_to_all | solution.py:24
  367.4 46.6 %all-to-all-start.3 = ((bf16[32,32,1536]{2,1,0:T(8,128)(2,1)}), bf16[32,32,1536]{2,1,0:T(8,128)(2,1)}, u32[]{:S(2)}, u32[]{:S(2)}) async-start(bf16[32,32,1536]{2,1,0:T(8,128)(2,1)} %bitcast.43), calls=%async_computation.3 | async-start | bytes 6291456 | tf_op jit(solution)/shard_map/all_to_all | solution.py:24
  372.5 17.6 %copy-start.12 = (bf16[1024,1024]{1,0:T(8,128)(2,1)S(1)}, bf16[1024,1024]{1,0:T(8,128)(2,1)}, u32[]{:S(2)}) copy-start(bf16[1024,1024]{1,0:T(8,128)(2,1)} %multiply_convert_fusion.3) | copy-start | bytes 6291460
  397.8 21.1 %copy-start.11 = (f32[1,128,2]{1,2,0:T(2,128)S(1)}, f32[1,128,2]{1,2,0:T(2,128)}, u32[]{:S(2)}) copy-start(f32[1,128,2]{1,2,0:T(2,128)} %param.8) | copy-start | bytes 3076
  397.8 21.1 %copy-start.5 = (s32[1024]{0:T(1024)S(1)}, s32[1024]{0:T(1024)}, u32[]{:S(2)}) copy-start(s32[1024]{0:T(1024)} %copy-done.4) | copy-start | bytes 12292
  397.8 21.1 %copy-start.7 = (s32[128]{0:T(128)S(1)}, s32[128]{0:T(128)}, u32[]{:S(2)}) copy-start(s32[128]{0:T(128)} %copy-done.6) | copy-start | bytes 1540
  397.8 21.1 %copy-start.9 = (s32[128]{0:T(128)S(1)}, s32[128]{0:T(128)}, u32[]{:S(2)}) copy-start(s32[128]{0:T(128)} %copy-done.8) | copy-start | bytes 1540
  414.0 46.6 %all-to-all-start.4 = ((bf16[32,32,1536]{2,1,0:T(8,128)(2,1)}), bf16[32,32,1536]{2,1,0:T(8,128)(2,1)}, u32[]{:S(2)}, u32[]{:S(2)}) async-start(bf16[32,32,1536]{2,1,0:T(8,128)(2,1)} %bitcast.42), calls=%async_computation.4 | async-start | bytes 6291456 | tf_op jit(solution)/shard_map/all_to_all | solution.py:24
  419.1 55.4 %copy-start.1 = (bf16[1,128,3072]{2,1,0:T(8,128)(2,1)S(1)}, bf16[1,128,3072]{2,1,0:T(8,128)(2,1)}, u32[]{:S(2)}) copy-start(bf16[1,128,3072]{2,1,0:T(8,128)(2,1)} %param.5) | copy-start | bytes 2359300
  422.1 41.5 %collective-permute-start.3 = (bf16[128,1536]{1,0:T(8,128)(2,1)S(1)}, bf16[128,1536]{1,0:T(8,128)(2,1)S(1)}, u32[]{:S(2)}, u32[]{:S(2)}) collective-permute-start(bf16[128,1536]{1,0:T(8,128)(2,1)S(1)} %fusion.7), channel_id=1, source_target_pairs={{32,0},{64,32},{96,64},{0,96},{33,1},{65,33},{97,65},{1,97},{34,2}... | collective-permute-start | bytes 1179656 | tf_op jit(solution)/shard_map/ppermute | solution.py:167
  463.6 10.0 %collective-permute-start.4 = (bf16[128,1536]{1,0:T(8,128)(2,1)S(1)}, bf16[128,1536]{1,0:T(8,128)(2,1)S(1)}, u32[]{:S(2)}, u32[]{:S(2)}) collective-permute-start(bf16[128,1536]{1,0:T(8,128)(2,1)S(1)} %fusion.6), channel_id=1, source_target_pairs={{32,0},{64,32},{96,64},{0,96},{33,1},{65,33},{97,65},{1,97},{34,2}... | collective-permute-start | bytes 1179656 | tf_op jit(solution)/shard_map/ppermute | solution.py:167

commit v5 on v3

--- a/solution.py
+++ b/solution.py
@@ -45,8 +45,8 @@
 def place(target, grads):
     tokens, top, width = grads.shape
     pairs, hidden = tokens * top, width // 2
-    columns = 1024
-    steps = hidden // columns
+    columns = hidden
+    steps = 1
     out = pl.pallas_call(
         place_kernel,
         grid=(2, steps),
@@ -119,14 +119,12 @@
 
 def cut(grads, h):
     tokens, top, width = grads.shape
-    columns = width // 8
+    columns = width // 4
     return pl.pallas_call(
         copy_kernel,
-        grid=(2, 2),
-        in_specs=[
-            pl.BlockSpec((tokens, top, columns), lambda p, j: (0, 0, (2 * p + h) * 2 + j)),
-        ],
-        out_specs=pl.BlockSpec((tokens, top, columns), lambda p, j: (0, 0, 2 * p + j)),
+        grid=(2,),
+        in_specs=[pl.BlockSpec((tokens, top, columns), lambda p: (0, 0, 2 * p + h))],
+        out_specs=pl.BlockSpec((tokens, top, columns), lambda p: (0, 0, p)),
         out_shape=jax.ShapeDtypeStruct((tokens, top, width // 2), grads.dtype),
         compiler_params=pltpu.CompilerParams(vmem_limit_bytes=VMEM),
         cost_estimate=pl.CostEstimate(
@@ -192,7 +190,8 @@
     early = []
     for j in range(COLUMN_PARTS):
         part = lower[j * columns : (j + 1) * columns]
-        early.append(after(bf16_dot(products(*after(first, slope_0)), part, ((1,), (1,)))))
+        term = bf16_dot(products(*after(first, slope_0)), part, ((1,), (1,)))
+        early.append(after(term.astype(jnp.bfloat16)))
     rows_1, early[0], early[1] = after(rows_1, *early)
     slope_1 = after(derivative(below[1] + bf16_dot(rows_1, upper[sent_width:], ((1,), (0,)))))
 
@@ -205,7 +204,7 @@
     for j in range(COLUMN_PARTS):
         part = upper[j * columns : (j + 1) * columns]
         late = bf16_dot(products(*after(second, slope_1)), part, ((1,), (1,)))
-        term = (early[j] + late).astype(jnp.bfloat16)
+        term = (early[j].astype(jnp.float32) + late).astype(jnp.bfloat16)
         returned = exchange(term.reshape(DEVICES, SHARE, columns)).reshape(-1, columns)
         both = bf16_dot(mix, returned, ((1,), (0,)))
         summed = (both[:n_tokens] + both[n_tokens:]).astype(jnp.bfloat16)

time: 347 us -> 345 us (level)
  waiting for transfers between devices: 151 us -> 156 us
  Pallas kernels: 25.8 us -> 21.5 us
  transfers between devices with their start and end apart: 11 -> 11, of which waited for: 6 -> 6; matrix products, arithmetic and copies ran while one was open for 29% -> 29% of each run, Pallas kernels for 7% -> 6%
where the time goes in v5:
time: 345 us
  waiting for transfers between devices  156 us (45%)
  matrix products  97.5 us (28%)
  starting transfers between devices  35.9 us (10%)
  Pallas kernels  21.5 us (6%)
  between operations  13.7 us (4%)
  other arithmetic  12.4 us (4%)
  local copies, waits for them, and re-layouts  7.91 us (2%)
    all_to_all x5, waiting for transfers between devices, exchange(): return lax.all_to_all(block, PLANE, split_axis=0, concat_axis=0, tiled=True)  100 us
    dot_general x11, matrix products, bf16_dot(): lax.dot_general(a, b, (dims, ((), ())), preferred_element_type=jnp.float32)  97.5 us
    ppermute x2, waiting for transfers between devices, local(): halves = [lax.ppermute(piece, 'pipe', BACK) for piece in pieces]  46.5 us
    all_to_all x5, starting transfers between devices, exchange(): return lax.all_to_all(block, PLANE, split_axis=0, concat_axis=0, tiled=True)  32.8 us
    select_n x1, other arithmetic, local(): upper = jnp.where(core == 0, other, mine)  9.77 us
    ppermute x2, waiting for transfers between devices, local(): parts.append(lax.ppermute(summed, 'pipe', BACK))  9.04 us
    pallas_call x2, Pallas kernels, place(): pl.pallas_call(place_kernel, grid=(2, steps), in_specs=[pl.BlockSpec((1,...  8.08 us
    pallas_call x1, Pallas kernels, pick(): pl.pallas_call(pick_kernel, grid=(sources // SOURCES,), in_specs=[pl.Bloc...  7.93 us
  transfers between devices with their start and end apart: 11, of which 6 were waited for; matrix products, arithmetic and copies ran while one was open for 29% of the time, Pallas kernels for 6%

profile of v5, /device:TPU:24, one launch (start us, length us, event | category | flops | bytes accessed | tf_op | source)
XLA Modules:
  0.0 344.8 jit_solution(9851676123112127064)
XLA Ops:
  6.5 1.9 fusion.48
  10.2 2.8 convolution_convert_fusion
  13.1 8.3 %all-to-all-start = ((bf16[32,32,1664]{2,1,0:T(8,128)(2,1)}), bf16[32,32,1664]{2,1,0:T(8,128)(2,1)S(1)}, u32[]{:S(2)}, u32[]{:S(2)}) async-start(bf16[32,32,1664]{2,1,0:T(8,128)(2,1)} %bitcast.38), calls=%async_computation | async-start | bytes 6815744 | tf_op jit(solution)/shard_map/all_to_all | solution.py:20
  21.3 2.8 cut_grads.2
  24.9 2.7 cut_grads.3
  29.3 44.8 %collective-permute-done.grads_ref = bf16[128,2,4096]{2,1,0:T(2,128)(2,1)} collective-permute-done((bf16[128,2,4096]{2,1,0:T(2,128)(2,1)}, bf16[128,2,4096]{2,1,0:T(2,128)(2,1)}, u32[]{:S(2)}, u32[]{:S(2)}) %collective-permute-start) | collective-permute-done | bytes 2097184 | tf_op jit(solution)/shard_map/ppermute | solution.py:174
  74.1 4.1 %place_grads.2 = bf16[8,2,2,32,2048]{4,3,2,1,0:T(8,128)(2,1)} custom-call(s32[1,256]{1,0:T(1,128)} %add.71.target_ref, bf16[128,2,4096]{2,1,0:T(2,128)(2,1)} %collective-permute-done.grads_ref), custom_call_target="tpu_custom_call" | custom-call | flops 1073741824 | bytes 6291456 | tf_op jit(solution)/shard_map/place_grads/pallas_call | solution.py:50
  78.2 7.5 %all-to-all-start.1 = ((bf16[32,32,2048]{2,1,0:T(8,128)(2,1)}), bf16[32,32,2048]{2,1,0:T(8,128)(2,1)}, u32[]{:S(2)}, u32[]{:S(2)}) async-start(bf16[32,32,2048]{2,1,0:T(8,128)(2,1)} %bitcast.36), calls=%async_computation.1 | async-start | bytes 8388608 | tf_op jit(solution)/shard_map/all_to_all | solution.py:20
  86.9 9.8 %broadcast_select_fusion = (bf16[3072,2048]{1,0:T(8,128)(2,1)S(1)}, bf16[3072,2048]{1,0:T(8,128)(2,1)S(1)}) fusion(bf16[3072,2048]{1,0:T(8,128)(2,1)} %collective-permute-done.1, pred[]{:T(512)S(6)} %eq.100, bf16[1,1,3072,2048]{3,2,1,0:T(8,128)(2,1)} %param.9), kind=kLoop, calls=%fused_computation | loop fusion | flops 12582912 | bytes 50331648 | tf_op jit(solution)/shard_map/jit(_where)/select_n | solution.py:177
  96.6 9.9 %fusion.14 = f32[1024,2048]{1,0:T(8,128)} fusion(bf16[1024,1536]{1,0:T(8,128)(2,1)S(1)} %bitcast.47, bf16[3072,2048]{1,0:T(8,128)(2,1)S(1)} %get-tuple-element.32), kind=kOutput, calls=%fused_computation.22 | convolution fusion | flops 6442450944 | bytes 17825792 | tf_op jit(solution)/shard_map/dot_general | solution.py:33
  106.5 1.3 copy-done
  107.8 8.9 %fusion.10 = f32[1024,2048]{1,0:T(8,128)} fusion(bf16[1024,1536]{1,0:T(8,128)(2,1)S(1)} %bitcast.48, bf16[3072,2048]{1,0:T(8,128)(2,1)S(1)} %get-tuple-element.31), kind=kOutput, calls=%fused_computation.18 | convolution fusion | flops 6442450944 | bytes 17825792 | tf_op jit(solution)/shard_map/dot_general | solution.py:33
  116.7 1.7 collective-permute-done.2.grads_ref
  118.4 4.0 %place_grads.3 = bf16[8,2,2,32,2048]{4,3,2,1,0:T(8,128)(2,1)} custom-call(s32[1,256]{1,0:T(1,128)} %bitcast.54, bf16[128,2,4096]{2,1,0:T(2,128)(2,1)} %collective-permute-done.2.grads_ref), custom_call_target="tpu_custom_call" | custom-call | flops 1073741824 | bytes 6291456 | tf_op jit(solution)/shard_map/place_grads/pallas_call | solution.py:50
  122.4 32.2 %all-to-all-done.1 = bf16[32,32,2048]{2,1,0:T(8,128)(2,1)} async-done(((bf16[32,32,2048]{2,1,0:T(8,128)(2,1)}), bf16[32,32,2048]{2,1,0:T(8,128)(2,1)}, u32[]{:S(2)}, u32[]{:S(2)}) %all-to-all-start.1) | async-done | bytes 4194336 | tf_op jit(solution)/shard_map/all_to_all | solution.py:20
  154.6 5.1 %all-to-all-start.2 = ((bf16[32,32,2048]{2,1,0:T(8,128)(2,1)}), bf16[32,32,2048]{2,1,0:T(8,128)(2,1)}, u32[]{:S(2)}, u32[]{:S(2)}) async-start(bf16[32,32,2048]{2,1,0:T(8,128)(2,1)} %bitcast.37), calls=%async_computation.2 | async-start | bytes 8388608 | tf_op jit(solution)/shard_map/all_to_all | solution.py:20
  159.7 7.9 %pick_rows.1 = bf16[32,32,1536]{2,1,0:T(8,128)(2,1)} custom-call(bf16[32,32,128]{2,1,0:T(8,128)(2,1)} %slice.73.number_ref, bf16[32,128,1536]{2,1,0:T(8,128)(2,1)} %bitcast.40), custom_call_target="tpu_custom_call" | custom-call | flops 402653184 | bytes 15728640 | tf_op jit(solution)/shard_map/pick_rows/pallas_call | solution.py:97
  167.7 12.6 %multiply_convert_fusion.3 = bf16[1024,2048]{1,0:T(8,128)(2,1)S(1)} fusion(f32[1024,2048]{1,0:T(8,128)} %fusion.14, bf16[1024,1536]{1,0:T(8,128)(2,1)} %bitcast.50, bf16[3072,2048]{1,0:T(8,128)(2,1)} %copy-done.1), kind=kOutput, calls=%fused_computation.5 | convolution fusion | flops 6461325312 | bytes 22020096 | tf_op jit(solution)/shard_map/dot_general | solution.py:33
  180.3 2.0 copy-done.10
  182.3 9.8 %fusion.16 = bf16[1024,1536]{1,0:T(8,128)(2,1)} fusion(bf16[3072,2048]{1,0:T(8,128)(2,1)S(1)} %bitcast.45, bf16[1024,2048]{1,0:T(8,128)(2,1)S(1)} %multiply_convert_fusion.3, bf16[1024,2048]{1,0:T(8,128)(2,1)} %bitcast.10), kind=kOutput, calls=%fused_computation.24 | convolution fusion | flops 6452412416 | bytes 17825792 | tf_op jit(solution)/shard_map/dot_general | solution.py:33
  192.1 10.4 %fusion.19 = bf16[1024,1536]{1,0:T(8,128)(2,1)} fusion(bf16[3072,2048]{1,0:T(8,128)(2,1)S(1)} %bitcast.45, bf16[1024,2048]{1,0:T(8,128)(2,1)} %copy-done.10, bf16[1024,2048]{1,0:T(8,128)(2,1)} %bitcast.10), kind=kOutput, calls=%fused_computation.25 | convolution fusion | flops 6452412416 | bytes 17825792 | tf_op jit(solution)/shard_map/dot_general | solution.py:33
  202.6 13.3 %multiply_convert_fusion.1 = bf16[1024,2048]{1,0:T(8,128)(2,1)} fusion(f32[1024,2048]{1,0:T(8,128)} %fusion.10, bf16[1024,1536]{1,0:T(8,128)(2,1)} %bitcast.51, bf16[3072,2048]{1,0:T(8,128)(2,1)S(1)} %bitcast.43), kind=kOutput, calls=%fused_computation.3 | convolution fusion | flops 6461325312 | bytes 22020096 | tf_op jit(solution)/shard_map/dot_general | solution.py:33
  215.8 12.7 %add_convert_fusion = bf16[1024,1536]{1,0:T(8,128)(2,1)} fusion(bf16[1024,1536]{1,0:T(8,128)(2,1)S(1)} %copy-done.11, bf16[3072,2048]{1,0:T(8,128)(2,1)} %copy-done, bf16[1024,2048]{1,0:T(8,128)(2,1)} %multiply_convert_fusion.1, bf16[1024,2048]{1,0:T(8,128)(2,1)} %bitcast.16), kind=kOutput, calls=%fused_computation.6 | convolution fusion | flops 6455558144 | bytes 20971520 | tf_op jit(solution)/shard_map/dot_general | solution.py:33
  228.5 7.1 %all-to-all-start.4 = ((bf16[32,32,1536]{2,1,0:T(8,128)(2,1)}), bf16[32,32,1536]{2,1,0:T(8,128)(2,1)S(1)}, u32[]{:S(2)}, u32[]{:S(2)}) async-start(bf16[32,32,1536]{2,1,0:T(8,128)(2,1)} %bitcast.49), calls=%async_computation.4 | async-start | bytes 6291456 | tf_op jit(solution)/shard_map/all_to_all | solution.py:20
  235.6 13.3 %add_convert_fusion.1 = bf16[1024,1536]{1,0:T(8,128)(2,1)} fusion(bf16[1024,1536]{1,0:T(8,128)(2,1)} %fusion.16, bf16[3072,2048]{1,0:T(8,128)(2,1)} %copy-done, bf16[1024,2048]{1,0:T(8,128)(2,1)} %multiply_convert_fusion.1, bf16[1024,2048]{1,0:T(8,128)(2,1)} %bitcast.16), kind=kOutput, calls=%fused_computation.7 | convolution fusion | flops 6455558144 | bytes 20971520 | tf_op jit(solution)/shard_map/dot_general | solution.py:33
  248.9 28.5 %all-to-all-done.4 = bf16[32,32,1536]{2,1,0:T(8,128)(2,1)S(1)} async-done(((bf16[32,32,1536]{2,1,0:T(8,128)(2,1)}), bf16[32,32,1536]{2,1,0:T(8,128)(2,1)S(1)}, u32[]{:S(2)}, u32[]{:S(2)}) %all-to-all-start.4) | async-done | bytes 3145760 | tf_op jit(solution)/shard_map/all_to_all | solution.py:20
  277.4 4.8 %all-to-all-start.3 = ((bf16[32,32,1536]{2,1,0:T(8,128)(2,1)}), bf16[32,32,1536]{2,1,0:T(8,128)(2,1)}, u32[]{:S(2)}, u32[]{:S(2)}) async-start(bf16[32,32,1536]{2,1,0:T(8,128)(2,1)} %bitcast.46), calls=%async_computation.3 | async-start | bytes 6291456 | tf_op jit(solution)/shard_map/all_to_all | solution.py:20
  282.5 1.0 fusion.39
  284.5 39.5 %all-to-all-done.3 = bf16[32,32,1536]{2,1,0:T(8,128)(2,1)} async-done(((bf16[32,32,1536]{2,1,0:T(8,128)(2,1)}), bf16[32,32,1536]{2,1,0:T(8,128)(2,1)}, u32[]{:S(2)}, u32[]{:S(2)}) %all-to-all-start.3) | async-done | bytes 3145760 | tf_op jit(solution)/shard_map/all_to_all | solution.py:20
  324.0 3.0 fusion.40
  328.0 9.0 %collective-permute-done.3 = bf16[128,1536]{1,0:T(8,128)(2,1)S(1)} collective-permute-done((bf16[128,1536]{1,0:T(8,128)(2,1)S(1)}, bf16[128,1536]{1,0:T(8,128)(2,1)S(1)}, u32[]{:S(2)}, u32[]{:S(2)}) %collective-permute-start.3) | collective-permute-done | bytes 393248 | tf_op jit(solution)/shard_map/ppermute | solution.py:211
  337.0 1.0 maximum_bitcast_fusion
  (69 shorter events, 7.6 us)
Async XLA Ops:
  6.5 153.2 %all-gather.3.cloned.1.call-start = ((), (), s32[]{:S(2)}) async-start(), calls=%async_computation.5 | async-start | bytes 12976128 | tf_op jit(solution)/shard_map/all_gather | solution.py:150
  8.5 78.4 %collective-permute-start.1 = (bf16[3072,2048]{1,0:T(8,128)(2,1)}, bf16[3072,2048]{1,0:T(8,128)(2,1)}, u32[]{:S(2)}, u32[]{:S(2)}) collective-permute-start(bf16[3072,2048]{1,0:T(8,128)(2,1)} %bitcast.41), channel_id=1, source_target_pairs={{0,1},{1,0},{2,3},{3,2},{4,5},{5,4},{6,7},{7,6},{8,9},{9,8},{10,11... | collective-permute-start | bytes 37748744 | tf_op jit(solution)/shard_map/ppermute | solution.py:175
  9.9 3.1 copy-start.3
  10.1 2.9 copy-start.5
  10.1 2.9 copy-start.7
  13.1 65.1 %all-to-all-start = ((bf16[32,32,1664]{2,1,0:T(8,128)(2,1)}), bf16[32,32,1664]{2,1,0:T(8,128)(2,1)S(1)}, u32[]{:S(2)}, u32[]{:S(2)}) async-start(bf16[32,32,1664]{2,1,0:T(8,128)(2,1)} %bitcast.38), calls=%async_computation | async-start | bytes 6815744 | tf_op jit(solution)/shard_map/all_to_all | solution.py:20
  24.1 50.0 %collective-permute-start = (bf16[128,2,4096]{2,1,0:T(2,128)(2,1)}, bf16[128,2,4096]{2,1,0:T(2,128)(2,1)}, u32[]{:S(2)}, u32[]{:S(2)}) collective-permute-start(bf16[128,2,4096]{2,1,0:T(2,128)(2,1)} %cut_grads.2), channel_id=1, source_target_pairs={{32,0},{64,32},{96,64},{0,96},{33,1},{65,33},{97,65},{1,97},{34,2}... | collective-permute-start | bytes 6291464 | tf_op jit(solution)/shard_map/ppermute | solution.py:174
  27.6 90.8 %collective-permute-start.2 = (bf16[128,2,4096]{2,1,0:T(2,128)(2,1)}, bf16[128,2,4096]{2,1,0:T(2,128)(2,1)}, u32[]{:S(2)}, u32[]{:S(2)}) collective-permute-start(bf16[128,2,4096]{2,1,0:T(2,128)(2,1)} %cut_grads.3), channel_id=1, source_target_pairs={{32,0},{64,32},{96,64},{0,96},{33,1},{65,33},{97,65},{1,97},{34,2}... | collective-permute-start | bytes 6291464 | tf_op jit(solution)/shard_map/ppermute | solution.py:174
  78.2 76.5 %all-to-all-start.1 = ((bf16[32,32,2048]{2,1,0:T(8,128)(2,1)}), bf16[32,32,2048]{2,1,0:T(8,128)(2,1)}, u32[]{:S(2)}, u32[]{:S(2)}) async-start(bf16[32,32,2048]{2,1,0:T(8,128)(2,1)} %bitcast.36), calls=%async_computation.1 | async-start | bytes 8388608 | tf_op jit(solution)/shard_map/all_to_all | solution.py:20
  96.6 9.9 %copy-start.1 = (bf16[3072,2048]{1,0:T(8,128)(2,1)}, bf16[3072,2048]{1,0:T(8,128)(2,1)S(1)}, u32[]{:S(2)}) copy-start(bf16[3072,2048]{1,0:T(8,128)(2,1)S(1)} %get-tuple-element.32) | copy-start | bytes 37748740
  96.6 11.2 %copy-start = (bf16[3072,2048]{1,0:T(8,128)(2,1)}, bf16[3072,2048]{1,0:T(8,128)(2,1)S(1)}, u32[]{:S(2)}) copy-start(bf16[3072,2048]{1,0:T(8,128)(2,1)S(1)} %get-tuple-element.31) | copy-start | bytes 37748740
  154.6 61.2 %all-to-all-start.2 = ((bf16[32,32,2048]{2,1,0:T(8,128)(2,1)}), bf16[32,32,2048]{2,1,0:T(8,128)(2,1)}, u32[]{:S(2)}, u32[]{:S(2)}) async-start(bf16[32,32,2048]{2,1,0:T(8,128)(2,1)} %bitcast.37), calls=%async_computation.2 | async-start | bytes 8388608 | tf_op jit(solution)/shard_map/all_to_all | solution.py:20
  159.7 22.5 %slice-start.3 = ((s8[12582912]{0:T(1024)(128)(4,1)}), s8[4194304]{0:T(1024)(128)(4,1)S(1)}, s32[]{:S(2)}) async-start(s8[12582912]{0:T(1024)(128)(4,1)} %bitcast.44), calls=%async_computation.9 | async-start | bytes 8388608
  167.7 14.6 %slice-start.4 = ((s8[12582912]{0:T(1024)(128)(4,1)}), s8[4194304]{0:T(1024)(128)(4,1)S(1)}, s32[]{:S(2)}) async-start(s8[12582912]{0:T(1024)(128)(4,1)} %bitcast.44), calls=%async_computation.10 | async-start | bytes 8388608
  167.7 14.6 %slice-start.5 = ((s8[12582912]{0:T(1024)(128)(4,1)}), s8[4194304]{0:T(1024)(128)(4,1)S(1)}, s32[]{:S(2)}) async-start(s8[12582912]{0:T(1024)(128)(4,1)} %bitcast.44), calls=%async_computation.11 | async-start | bytes 8388608
  180.3 2.0 copy-start.10
  182.3 20.3 %slice-start = ((s8[12582912]{0:T(1024)(128)(4,1)}), s8[4194304]{0:T(1024)(128)(4,1)S(1)}, s32[]{:S(2)}) async-start(s8[12582912]{0:T(1024)(128)(4,1)} %bitcast.42), calls=%async_computation.6 | async-start | bytes 8388608
  182.3 20.3 %slice-start.1 = ((s8[12582912]{0:T(1024)(128)(4,1)}), s8[4194304]{0:T(1024)(128)(4,1)S(1)}, s32[]{:S(2)}) async-start(s8[12582912]{0:T(1024)(128)(4,1)} %bitcast.42), calls=%async_computation.7 | async-start | bytes 8388608
  192.1 10.4 %slice-start.2 = ((s8[12582912]{0:T(1024)(128)(4,1)}), s8[4194304]{0:T(1024)(128)(4,1)S(1)}, s32[]{:S(2)}) async-start(s8[12582912]{0:T(1024)(128)(4,1)} %bitcast.42), calls=%async_computation.8 | async-start | bytes 8388608
  202.6 13.3 %copy-start.11 = (bf16[1024,1536]{1,0:T(8,128)(2,1)S(1)}, bf16[1024,1536]{1,0:T(8,128)(2,1)}, u32[]{:S(2)}) copy-start(bf16[1024,1536]{1,0:T(8,128)(2,1)} %fusion.19) | copy-start | bytes 9437188
  228.5 48.9 %all-to-all-start.4 = ((bf16[32,32,1536]{2,1,0:T(8,128)(2,1)}), bf16[32,32,1536]{2,1,0:T(8,128)(2,1)S(1)}, u32[]{:S(2)}, u32[]{:S(2)}) async-start(bf16[32,32,1536]{2,1,0:T(8,128)(2,1)} %bitcast.49), calls=%async_computation.4 | async-start | bytes 6291456 | tf_op jit(solution)/shard_map/all_to_all | solution.py:20
  248.9 33.3 %copy-start.9 = (f32[1,128,2]{1,2,0:T(2,128)S(1)}, f32[1,128,2]{1,2,0:T(2,128)}, u32[]{:S(2)}) copy-start(f32[1,128,2]{1,2,0:T(2,128)} %param.8) | copy-start | bytes 3076
  248.9 33.3 %copy-start.4 = (s32[1024]{0:T(1024)S(1)}, s32[1024]{0:T(1024)}, u32[]{:S(2)}) copy-start(s32[1024]{0:T(1024)} %copy-done.3) | copy-start | bytes 12292
  248.9 33.3 %copy-start.6 = (s32[128]{0:T(128)S(1)}, s32[128]{0:T(128)}, u32[]{:S(2)}) copy-start(s32[128]{0:T(128)} %copy-done.5) | copy-start | bytes 1540
  248.9 33.4 %copy-start.8 = (s32[128]{0:T(128)S(1)}, s32[128]{0:T(128)}, u32[]{:S(2)}) copy-start(s32[128]{0:T(128)} %copy-done.7) | copy-start | bytes 1540
  277.4 46.6 %all-to-all-start.3 = ((bf16[32,32,1536]{2,1,0:T(8,128)(2,1)}), bf16[32,32,1536]{2,1,0:T(8,128)(2,1)}, u32[]{:S(2)}, u32[]{:S(2)}) async-start(bf16[32,32,1536]{2,1,0:T(8,128)(2,1)} %bitcast.46), calls=%async_computation.3 | async-start | bytes 6291456 | tf_op jit(solution)/shard_map/all_to_all | solution.py:20
  282.5 1.1 copy-start.2
  283.6 44.4 %collective-permute-start.4 = (bf16[128,1536]{1,0:T(8,128)(2,1)S(1)}, bf16[128,1536]{1,0:T(8,128)(2,1)S(1)}, u32[]{:S(2)}, u32[]{:S(2)}) collective-permute-start(bf16[128,1536]{1,0:T(8,128)(2,1)S(1)} %fusion.30), channel_id=1, source_target_pairs={{32,0},{64,32},{96,64},{0,96},{33,1},{65,33},{97,65},{1,97},{34,2}... | collective-permute-start | bytes 1179656 | tf_op jit(solution)/shard_map/ppermute | solution.py:211
  327.0 10.0 %collective-permute-start.3 = (bf16[128,1536]{1,0:T(8,128)(2,1)S(1)}, bf16[128,1536]{1,0:T(8,128)(2,1)S(1)}, u32[]{:S(2)}, u32[]{:S(2)}) collective-permute-start(bf16[128,1536]{1,0:T(8,128)(2,1)S(1)} %fusion.31), channel_id=1, source_target_pairs={{32,0},{64,32},{96,64},{0,96},{33,1},{65,33},{97,65},{1,97},{34,2}... | collective-permute-start | bytes 1179656 | tf_op jit(solution)/shard_map/ppermute | solution.py:211
Sparse Core Ops, SparseCore 0:
  9.6 139.9 all-gather.2

commit v6 on v5

--- a/solution.py
+++ b/solution.py
@@ -67,52 +67,6 @@
     return out.reshape(DEVICES, SHARE, hidden)
 
 
-SOURCES = 8
-
-
-def pick_kernel(number_ref, tokens_ref, out_ref):
-    n_tokens, width = tokens_ref.shape[1:]
-    token = lax.broadcasted_iota(jnp.int32, (SHARE, n_tokens), 1) + 1
-    nothing = jnp.zeros((SHARE, n_tokens), jnp.bfloat16)
-    for i in range(0, SOURCES, 2):
-        hits = [
-            jnp.where(number_ref[i + n].astype(jnp.float32) == token.astype(jnp.float32), 1.0, 0.0)
-            for n in range(2)
-        ]
-        hits = [hit.astype(jnp.bfloat16) for hit in hits]
-        pair = jnp.concatenate(
-            [
-                jnp.concatenate([hits[0], nothing], axis=1),
-                jnp.concatenate([nothing, hits[1]], axis=1),
-            ],
-            axis=0,
-        )
-        both = tokens_ref[i : i + 2].reshape(2 * n_tokens, width)
-        rows = jnp.dot(pair, both, preferred_element_type=jnp.float32)
-        out_ref[i : i + 2] = rows.astype(jnp.bfloat16).reshape(2, SHARE, width)
-
-
-def pick(numbers, tokens):
-    sources, n_tokens, width = tokens.shape
-    return pl.pallas_call(
-        pick_kernel,
-        grid=(sources // SOURCES,),
-        in_specs=[
-            pl.BlockSpec((SOURCES, SHARE, n_tokens), lambda i: (i, 0, 0)),
-            pl.BlockSpec((SOURCES, n_tokens, width), lambda i: (i, 0, 0)),
-        ],
-        out_specs=pl.BlockSpec((SOURCES, SHARE, width), lambda i: (i, 0, 0)),
-        out_shape=jax.ShapeDtypeStruct((sources, SHARE, width), jnp.bfloat16),
-        compiler_params=pltpu.CompilerParams(vmem_limit_bytes=VMEM),
-        cost_estimate=pl.CostEstimate(
-            flops=2 * sources * SHARE * n_tokens * width,
-            bytes_accessed=2 * sources * (SHARE + n_tokens) * width,
-            transcendentals=0,
-        ),
-        name="pick_rows",
-    )(numbers, tokens)
-
-
 def copy_kernel(in_ref, out_ref):
     out_ref[...] = in_ref[...]
 
@@ -146,9 +100,6 @@
     core = lax.axis_index("core")
     rows_here = DEVICES * SHARE
 
-    sent_width = width // 2
-    gathered = lax.all_gather(tokens[:, sent_width:], PLANE, axis=0)
-
     flat_expert = routes[0].reshape(-1)
     pairs = flat_expert.shape[0]
     number = jnp.arange(pairs, dtype=jnp.int32)
@@ -161,14 +112,8 @@
     places = jnp.broadcast_to(places, (EXPERTS, 2, SLOTS)).reshape(-1)
     row_hit = [places[:, None] == by_token[None, :, k] for k in range(TOP)]
     place_token = (row_hit[0] | row_hit[1]).astype(jnp.bfloat16)
-    numbered = jnp.broadcast_to(
-        jnp.arange(1, n_tokens + 1, dtype=jnp.int32)[:, None], (n_tokens, n_tokens)
-    ).astype(jnp.bfloat16)
-    sent = jnp.concatenate([tokens[:, :sent_width], numbered], axis=1)
-    sent = bf16_dot(place_token, sent, ((1,), (0,))).astype(jnp.bfloat16)
-    got = exchange(sent.reshape(DEVICES, SHARE, sent_width + n_tokens))
-    rows_0 = got[:, :, :sent_width].reshape(rows_here, sent_width)
-    numbers = got[:, :, sent_width:]
+    sent = bf16_dot(place_token, tokens, ((1,), (0,))).astype(jnp.bfloat16)
+    rows = exchange(sent.reshape(DEVICES, SHARE, width)).reshape(rows_here, width)
 
     pieces = [cut(hid_grad[0], h) for h in range(2)]
     halves = [lax.ppermute(piece, "pipe", BACK) for piece in pieces]
@@ -177,23 +122,18 @@
     upper = jnp.where(core == 0, other, mine)
 
     first = exchange(place(target, halves[0])).reshape(rows_here, hidden)
-    below = [
-        after(bf16_dot(rows_0, w[:sent_width], ((1,), (0,)))) for w in (lower, upper)
-    ]
-    target, below[0], below[1] = after(target, below[0], below[1])
-    second = exchange(place(target, halves[1])).reshape(rows_here, hidden)
+    slopes = [after(derivative(bf16_dot(rows, w, ((1,), (0,))))) for w in (lower, upper)]
+    target, *slopes = after(target, *slopes)
+    placed = place(target, halves[1])
+    first, placed = after(first, placed)
+    second = exchange(placed).reshape(rows_here, hidden)
 
-    gathered, first = after(gathered, first)
-    rows_1 = pick(numbers, gathered).reshape(rows_here, width - sent_width)
-    slope_0 = after(derivative(below[0] + bf16_dot(rows_1, lower[sent_width:], ((1,), (0,)))))
     columns = width // COLUMN_PARTS
     early = []
     for j in range(COLUMN_PARTS):
         part = lower[j * columns : (j + 1) * columns]
-        term = bf16_dot(products(*after(first, slope_0)), part, ((1,), (1,)))
+        term = bf16_dot(products(*after(first, slopes[0])), part, ((1,), (1,)))
         early.append(after(term.astype(jnp.bfloat16)))
-    rows_1, early[0], early[1] = after(rows_1, *early)
-    slope_1 = after(derivative(below[1] + bf16_dot(rows_1, upper[sent_width:], ((1,), (0,)))))
 
     hit = [by_token[:, k, None] == places[None, :] for k in range(TOP)]
     mix = sum(jnp.where(hit[k], probs[0][:, k, None], 0.0) for k in range(TOP))
@@ -203,7 +143,7 @@
     parts = []
     for j in range(COLUMN_PARTS):
         part = upper[j * columns : (j + 1) * columns]
-        late = bf16_dot(products(*after(second, slope_1)), part, ((1,), (1,)))
+        late = bf16_dot(products(*after(second, slopes[1])), part, ((1,), (1,)))
         term = (early[j].astype(jnp.float32) + late).astype(jnp.bfloat16)
         returned = exchange(term.reshape(DEVICES, SHARE, columns)).reshape(-1, columns)
         both = bf16_dot(mix, returned, ((1,), (0,)))

time: 345 us -> 330 us (0.957)
  between operations: 13.7 us -> 0.2 us
  Pallas kernels: 21.5 us -> 13.3 us
  waiting for transfers between devices: 156 us -> 164 us
  other arithmetic: 12.4 us -> 19.6 us
  local copies, waits for them, and re-layouts: 7.91 us -> 2.88 us
  starting transfers between devices: 35.9 us -> 31.2 us
    all_to_all x5, waiting for transfers between devices: 100 us -> 110 us  [exchange(): return lax.all_to_all(block, PLANE, split_axis=0, concat_axis=0, tiled=True)]
    pallas_call x1 -> x0, Pallas kernels: 7.93 us -> none  [pick(): pl.pallas_call(pick_kernel, grid=(sources // SOURCES,), in_specs=[pl.Bloc...]
    select_n x1, other arithmetic: 9.77 us -> 17 us  [local(): upper = jnp.where(core == 0, other, mine)]
    all_to_all x5, starting transfers between devices: 32.8 us -> 28.4 us  [exchange(): return lax.all_to_all(block, PLANE, split_axis=0, concat_axis=0, tiled=True)]
    dot_general x11 -> x9, matrix products: 97.5 us -> 97.6 us  [bf16_dot(): lax.dot_general(a, b, (dims, ((), ())), preferred_element_type=jnp.float32)]
  transfers between devices with their start and end apart: 11 -> 10, of which waited for: 6 -> 7; matrix products, arithmetic and copies ran while one was open for 29% -> 32% of each run, Pallas kernels for 6% -> 4%
where the time goes in v6:
time: 330 us; the launch traced here: 329 us
  waiting for transfers between devices  164 us (50%)
  matrix products  97.6 us (30%)
  starting transfers between devices  31.2 us (9%)
  other arithmetic  19.6 us (6%)
  Pallas kernels  13.3 us (4%)
    all_to_all x5, waiting for transfers between devices, exchange(): return lax.all_to_all(block, PLANE, split_axis=0, concat_axis=0, tiled=True)  110 us
    dot_general x9, matrix products, bf16_dot(): lax.dot_general(a, b, (dims, ((), ())), preferred_element_type=jnp.float32)  97.6 us
    ppermute x2, waiting for transfers between devices, local(): halves = [lax.ppermute(piece, 'pipe', BACK) for piece in pieces]  44.9 us
    all_to_all x5, starting transfers between devices, exchange(): return lax.all_to_all(block, PLANE, split_axis=0, concat_axis=0, tiled=True)  28.4 us
    select_n x1, other arithmetic, local(): upper = jnp.where(core == 0, other, mine)  17 us
    ppermute x2, waiting for transfers between devices, local(): parts.append(lax.ppermute(summed, 'pipe', BACK))  9.03 us
    pallas_call x2, Pallas kernels, place(): pl.pallas_call(place_kernel, grid=(2, steps), in_specs=[pl.BlockSpec((1,...  8.08 us
  transfers between devices with their start and end apart: 10, of which 7 were waited for; matrix products, arithmetic and copies ran while one was open for 32% of the time, Pallas kernels for 4%

profile of v6, /device:TPU:24, one launch (start us, length us, event | category | flops | bytes accessed | tf_op | source)
XLA Modules:
  0.0 329.1 jit_solution(14708443256964406436)
XLA Ops:
  0.0 0.9 copy.11
  1.6 4.4 %convolution_convert_fusion = bf16[1024,3072]{1,0:T(8,128)(2,1)} fusion(bf16[1,128,3072]{2,1,0:T(8,128)(2,1)S(1)} %copy-done, s32[128]{0:T(128)S(1)} %get-tuple-element.24, s32[128]{0:T(128)S(1)} %get-tuple-element.23, s32[1024]{0:T(1024)S(1)} %eq.89), kind=kOutput, calls=%fused_computation.16 | convolution fusion | flops 808845312 | bytes 7083008 | tf_op jit(solution)/shard_map/dot_general | solution.py:33
  6.1 8.3 %all-to-all-start.1 = ((bf16[32,32,3072]{2,1,0:T(8,128)(2,1)}), bf16[32,32,3072]{2,1,0:T(8,128)(2,1)}, u32[]{:S(2)}, u32[]{:S(2)}) async-start(bf16[32,32,3072]{2,1,0:T(8,128)(2,1)} %bitcast.34), calls=%async_computation.1 | async-start | bytes 12582912 | tf_op jit(solution)/shard_map/all_to_all | solution.py:20
  14.4 2.6 cut_grads.2
  17.0 0.7 collective-permute-start
  17.8 2.6 cut_grads.3
  22.1 44.9 %collective-permute-done.grads_ref = bf16[128,2,4096]{2,1,0:T(2,128)(2,1)} collective-permute-done((bf16[128,2,4096]{2,1,0:T(2,128)(2,1)}, bf16[128,2,4096]{2,1,0:T(2,128)(2,1)}, u32[]{:S(2)}, u32[]{:S(2)}) %collective-permute-start) | collective-permute-done | bytes 2097184 | tf_op jit(solution)/shard_map/ppermute | solution.py:119
  67.0 4.0 %place_grads.2 = bf16[8,2,2,32,2048]{4,3,2,1,0:T(8,128)(2,1)} custom-call(s32[1,256]{1,0:T(1,128)} %add.53.target_ref, bf16[128,2,4096]{2,1,0:T(2,128)(2,1)} %collective-permute-done.grads_ref), custom_call_target="tpu_custom_call" | custom-call | flops 1073741824 | bytes 6291456 | tf_op jit(solution)/shard_map/place_grads/pallas_call | solution.py:50
  71.1 17.0 %broadcast_select_fusion = (bf16[3072,2048]{1,0:T(8,128)(2,1)}, bf16[3072,2048]{1,0:T(8,128)(2,1)}) fusion(bf16[3072,2048]{1,0:T(8,128)(2,1)} %collective-permute-done.1, pred[]{:T(512)S(6)} %eq.100, bf16[1,1,3072,2048]{3,2,1,0:T(8,128)(2,1)} %param.9), kind=kLoop, calls=%fused_computation | loop fusion | flops 12582912 | bytes 50331648 | tf_op jit(solution)/shard_map/jit(_where)/select_n | solution.py:122
  88.0 4.2 %all-to-all-done.1 = bf16[32,32,3072]{2,1,0:T(8,128)(2,1)} async-done(((bf16[32,32,3072]{2,1,0:T(8,128)(2,1)}), bf16[32,32,3072]{2,1,0:T(8,128)(2,1)}, u32[]{:S(2)}, u32[]{:S(2)}) %all-to-all-start.1) | async-done | bytes 6291488 | tf_op jit(solution)/shard_map/all_to_all | solution.py:20
  92.3 5.0 %all-to-all-start = ((bf16[32,32,2048]{2,1,0:T(8,128)(2,1)}), bf16[32,32,2048]{2,1,0:T(8,128)(2,1)}, u32[]{:S(2)}, u32[]{:S(2)}) async-start(bf16[32,32,2048]{2,1,0:T(8,128)(2,1)} %bitcast.37), calls=%async_computation | async-start | bytes 8388608 | tf_op jit(solution)/shard_map/all_to_all | solution.py:20
  97.3 20.9 %multiply_convert_fusion.3 = bf16[1024,2048]{1,0:T(8,128)(2,1)} fusion(bf16[1024,3072]{1,0:T(8,128)(2,1)} %bitcast.10, bf16[3072,2048]{1,0:T(8,128)(2,1)} %get-tuple-element.26), kind=kOutput, calls=%fused_computation.5 | convolution fusion | flops 12901679104 | bytes 23068672 | tf_op jit(solution)/shard_map/dot_general | solution.py:33
  118.3 17.8 %multiply_convert_fusion.2 = bf16[1024,2048]{1,0:T(8,128)(2,1)} fusion(bf16[1024,3072]{1,0:T(8,128)(2,1)} %bitcast.10, bf16[3072,2048]{1,0:T(8,128)(2,1)S(1)} %copy-done.2), kind=kOutput, calls=%fused_computation.4 | convolution fusion | flops 12901679104 | bytes 23068672 | tf_op jit(solution)/shard_map/dot_general | solution.py:33
  136.0 1.3 copy-done.3
  137.3 4.0 %place_grads.3 = bf16[8,2,2,32,2048]{4,3,2,1,0:T(8,128)(2,1)} custom-call(s32[1,256]{1,0:T(1,128)} %bitcast.43, bf16[128,2,4096]{2,1,0:T(2,128)(2,1)} %copy-done.3), custom_call_target="tpu_custom_call" | custom-call | flops 1073741824 | bytes 6291456 | tf_op jit(solution)/shard_map/place_grads/pallas_call | solution.py:50
  141.4 9.2 %all-to-all-done = bf16[32,32,2048]{2,1,0:T(8,128)(2,1)} async-done(((bf16[32,32,2048]{2,1,0:T(8,128)(2,1)}), bf16[32,32,2048]{2,1,0:T(8,128)(2,1)}, u32[]{:S(2)}, u32[]{:S(2)}) %all-to-all-start) | async-done | bytes 4194336 | tf_op jit(solution)/shard_map/all_to_all | solution.py:20
  150.6 5.1 %all-to-all-start.2 = ((bf16[32,32,2048]{2,1,0:T(8,128)(2,1)}), bf16[32,32,2048]{2,1,0:T(8,128)(2,1)}, u32[]{:S(2)}, u32[]{:S(2)}) async-start(bf16[32,32,2048]{2,1,0:T(8,128)(2,1)} %bitcast.38), calls=%async_computation.2 | async-start | bytes 8388608 | tf_op jit(solution)/shard_map/all_to_all | solution.py:20
  155.7 12.5 %fusion.12 = bf16[1024,1536]{1,0:T(8,128)(2,1)} fusion(bf16[3072,2048]{1,0:T(8,128)(2,1)} %get-tuple-element.26, bf16[1024,2048]{1,0:T(8,128)(2,1)} %multiply_convert_fusion.3, bf16[1024,2048]{1,0:T(8,128)(2,1)} %bitcast.7), kind=kOutput, calls=%fused_computation.17 | convolution fusion | flops 6452412416 | bytes 17825792 | tf_op jit(solution)/shard_map/dot_general | solution.py:33
  168.3 40.7 %all-to-all-done.2 = bf16[32,32,2048]{2,1,0:T(8,128)(2,1)} async-done(((bf16[32,32,2048]{2,1,0:T(8,128)(2,1)}), bf16[32,32,2048]{2,1,0:T(8,128)(2,1)}, u32[]{:S(2)}, u32[]{:S(2)}) %all-to-all-start.2) | async-done | bytes 4194336 | tf_op jit(solution)/shard_map/all_to_all | solution.py:20
  209.0 13.2 %add_convert_fusion.1 = bf16[1024,1536]{1,0:T(8,128)(2,1)} fusion(bf16[1024,1536]{1,0:T(8,128)(2,1)} %fusion.12, bf16[3072,2048]{1,0:T(8,128)(2,1)} %get-tuple-element.25, bf16[1024,2048]{1,0:T(8,128)(2,1)} %multiply_convert_fusion.2, bf16[1024,2048]{1,0:T(8,128)(2,1)} %bitcast.14), kind=kOutput, calls=%fused_computation.15 | convolution fusion | flops 6455558144 | bytes 20971520 | tf_op jit(solution)/shard_map/dot_general | solution.py:33
  222.2 4.8 %all-to-all-start.3 = ((bf16[32,32,1536]{2,1,0:T(8,128)(2,1)}), bf16[32,32,1536]{2,1,0:T(8,128)(2,1)}, u32[]{:S(2)}, u32[]{:S(2)}) async-start(bf16[32,32,1536]{2,1,0:T(8,128)(2,1)} %bitcast.41), calls=%async_computation.3 | async-start | bytes 6291456 | tf_op jit(solution)/shard_map/all_to_all | solution.py:20
  227.0 11.5 %fusion.15 = bf16[1024,1536]{1,0:T(8,128)(2,1)S(1)} fusion(bf16[3072,2048]{1,0:T(8,128)(2,1)} %get-tuple-element.26, bf16[1024,2048]{1,0:T(8,128)(2,1)} %multiply_convert_fusion.3, bf16[1024,2048]{1,0:T(8,128)(2,1)} %bitcast.7), kind=kOutput, calls=%fused_computation.18 | convolution fusion | flops 6452412416 | bytes 17825792 | tf_op jit(solution)/shard_map/dot_general | solution.py:33
  238.5 11.5 %add_convert_fusion = bf16[1024,1536]{1,0:T(8,128)(2,1)} fusion(bf16[1024,1536]{1,0:T(8,128)(2,1)S(1)} %fusion.15, bf16[3072,2048]{1,0:T(8,128)(2,1)} %get-tuple-element.25, bf16[1024,2048]{1,0:T(8,128)(2,1)S(1)} %copy-done.5, bf16[1024,2048]{1,0:T(8,128)(2,1)} %bitcast.14), kind=kOutput, calls=%fused_computation.14 | convolution fusion | flops 6455558144 | bytes 20971520 | tf_op jit(solution)/shard_map/dot_general | solution.py:33
  250.1 18.7 %all-to-all-done.3 = bf16[32,32,1536]{2,1,0:T(8,128)(2,1)} async-done(((bf16[32,32,1536]{2,1,0:T(8,128)(2,1)}), bf16[32,32,1536]{2,1,0:T(8,128)(2,1)}, u32[]{:S(2)}, u32[]{:S(2)}) %all-to-all-start.3) | async-done | bytes 3145760 | tf_op jit(solution)/shard_map/all_to_all | solution.py:20
  268.8 5.1 %all-to-all-start.4 = ((bf16[32,32,1536]{2,1,0:T(8,128)(2,1)}), bf16[32,32,1536]{2,1,0:T(8,128)(2,1)}, u32[]{:S(2)}, u32[]{:S(2)}) async-start(bf16[32,32,1536]{2,1,0:T(8,128)(2,1)} %bitcast.40), calls=%async_computation.4 | async-start | bytes 6291456 | tf_op jit(solution)/shard_map/all_to_all | solution.py:20
  274.1 2.9 fusion.26
  277.1 0.8 collective-permute-start.3
  277.9 37.4 %all-to-all-done.4 = bf16[32,32,1536]{2,1,0:T(8,128)(2,1)} async-done(((bf16[32,32,1536]{2,1,0:T(8,128)(2,1)}), bf16[32,32,1536]{2,1,0:T(8,128)(2,1)}, u32[]{:S(2)}, u32[]{:S(2)}) %all-to-all-start.4) | async-done | bytes 3145760 | tf_op jit(solution)/shard_map/all_to_all | solution.py:20
  315.4 2.9 fusion.25
  318.3 0.8 collective-permute-start.4
  319.1 9.0 %collective-permute-done.4 = bf16[128,1536]{1,0:T(8,128)(2,1)S(1)} collective-permute-done((bf16[128,1536]{1,0:T(8,128)(2,1)S(1)}, bf16[128,1536]{1,0:T(8,128)(2,1)S(1)}, u32[]{:S(2)}, u32[]{:S(2)}) %collective-permute-start.4) | collective-permute-done | bytes 393248 | tf_op jit(solution)/shard_map/ppermute | solution.py:151
  328.1 1.0 maximum_bitcast_fusion
  (32 shorter events, 2.9 us)
Async XLA Ops:
  0.0 1.6 copy-start
  0.0 71.1 %collective-permute-start.1 = (bf16[3072,2048]{1,0:T(8,128)(2,1)}, bf16[3072,2048]{1,0:T(8,128)(2,1)}, u32[]{:S(2)}, u32[]{:S(2)}) collective-permute-start(bf16[3072,2048]{1,0:T(8,128)(2,1)} %bitcast.39), channel_id=1, source_target_pairs={{0,1},{1,0},{2,3},{3,2},{4,5},{5,4},{6,7},{7,6},{8,9},{9,8},{10,11... | collective-permute-start | bytes 37748744 | tf_op jit(solution)/shard_map/ppermute | solution.py:120
  6.1 86.2 %all-to-all-start.1 = ((bf16[32,32,3072]{2,1,0:T(8,128)(2,1)}), bf16[32,32,3072]{2,1,0:T(8,128)(2,1)}, u32[]{:S(2)}, u32[]{:S(2)}) async-start(bf16[32,32,3072]{2,1,0:T(8,128)(2,1)} %bitcast.34), calls=%async_computation.1 | async-start | bytes 12582912 | tf_op jit(solution)/shard_map/all_to_all | solution.py:20
  17.0 50.0 %collective-permute-start = (bf16[128,2,4096]{2,1,0:T(2,128)(2,1)}, bf16[128,2,4096]{2,1,0:T(2,128)(2,1)}, u32[]{:S(2)}, u32[]{:S(2)}) collective-permute-start(bf16[128,2,4096]{2,1,0:T(2,128)(2,1)} %cut_grads.2), channel_id=1, source_target_pairs={{32,0},{64,32},{96,64},{0,96},{33,1},{65,33},{97,65},{1,97},{34,2}... | collective-permute-start | bytes 6291464 | tf_op jit(solution)/shard_map/ppermute | solution.py:119
  20.4 115.6 %collective-permute-start.2 = (bf16[128,2,4096]{2,1,0:T(2,128)(2,1)}, bf16[128,2,4096]{2,1,0:T(2,128)(2,1)S(1)}, u32[]{:S(2)}, u32[]{:S(2)}) collective-permute-start(bf16[128,2,4096]{2,1,0:T(2,128)(2,1)} %cut_grads.3), channel_id=1, source_target_pairs={{32,0},{64,32},{96,64},{0,96},{33,1},{65,33},{97,65},{1,97},{34,2}... | collective-permute-start | bytes 6291464 | tf_op jit(solution)/shard_map/ppermute | solution.py:119
  92.3 58.3 %all-to-all-start = ((bf16[32,32,2048]{2,1,0:T(8,128)(2,1)}), bf16[32,32,2048]{2,1,0:T(8,128)(2,1)}, u32[]{:S(2)}, u32[]{:S(2)}) async-start(bf16[32,32,2048]{2,1,0:T(8,128)(2,1)} %bitcast.37), calls=%async_computation | async-start | bytes 8388608 | tf_op jit(solution)/shard_map/all_to_all | solution.py:20
  97.3 20.9 %copy-start.2 = (bf16[3072,2048]{1,0:T(8,128)(2,1)S(1)}, bf16[3072,2048]{1,0:T(8,128)(2,1)}, u32[]{:S(2)}) copy-start(bf16[3072,2048]{1,0:T(8,128)(2,1)} %get-tuple-element.25) | copy-start | bytes 37748740
  136.0 1.3 copy-start.3
  150.6 58.3 %all-to-all-start.2 = ((bf16[32,32,2048]{2,1,0:T(8,128)(2,1)}), bf16[32,32,2048]{2,1,0:T(8,128)(2,1)}, u32[]{:S(2)}, u32[]{:S(2)}) async-start(bf16[32,32,2048]{2,1,0:T(8,128)(2,1)} %bitcast.38), calls=%async_computation.2 | async-start | bytes 8388608 | tf_op jit(solution)/shard_map/all_to_all | solution.py:20
  222.2 46.6 %all-to-all-start.3 = ((bf16[32,32,1536]{2,1,0:T(8,128)(2,1)}), bf16[32,32,1536]{2,1,0:T(8,128)(2,1)}, u32[]{:S(2)}, u32[]{:S(2)}) async-start(bf16[32,32,1536]{2,1,0:T(8,128)(2,1)} %bitcast.41), calls=%async_computation.3 | async-start | bytes 6291456 | tf_op jit(solution)/shard_map/all_to_all | solution.py:20
  227.0 11.5 %copy-start.5 = (bf16[1024,2048]{1,0:T(8,128)(2,1)S(1)}, bf16[1024,2048]{1,0:T(8,128)(2,1)}, u32[]{:S(2)}) copy-start(bf16[1024,2048]{1,0:T(8,128)(2,1)} %multiply_convert_fusion.2) | copy-start | bytes 12582916
  250.1 23.8 %copy-start.4 = (f32[1,128,2]{1,2,0:T(2,128)S(1)}, f32[1,128,2]{1,2,0:T(2,128)}, u32[]{:S(2)}) copy-start(f32[1,128,2]{1,2,0:T(2,128)} %param.8) | copy-start | bytes 3076
  268.8 46.6 %all-to-all-start.4 = ((bf16[32,32,1536]{2,1,0:T(8,128)(2,1)}), bf16[32,32,1536]{2,1,0:T(8,128)(2,1)}, u32[]{:S(2)}, u32[]{:S(2)}) async-start(bf16[32,32,1536]{2,1,0:T(8,128)(2,1)} %bitcast.40), calls=%async_computation.4 | async-start | bytes 6291456 | tf_op jit(solution)/shard_map/all_to_all | solution.py:20
  274.1 55.0 %copy-start.1 = (bf16[1,128,3072]{2,1,0:T(8,128)(2,1)S(1)}, bf16[1,128,3072]{2,1,0:T(8,128)(2,1)}, u32[]{:S(2)}) copy-start(bf16[1,128,3072]{2,1,0:T(8,128)(2,1)} %param.5) | copy-start | bytes 2359300
  277.1 42.0 %collective-permute-start.3 = (bf16[128,1536]{1,0:T(8,128)(2,1)S(1)}, bf16[128,1536]{1,0:T(8,128)(2,1)S(1)}, u32[]{:S(2)}, u32[]{:S(2)}) collective-permute-start(bf16[128,1536]{1,0:T(8,128)(2,1)S(1)} %fusion.19), channel_id=1, source_target_pairs={{32,0},{64,32},{96,64},{0,96},{33,1},{65,33},{97,65},{1,97},{34,2}... | collective-permute-start | bytes 1179656 | tf_op jit(solution)/shard_map/ppermute | solution.py:151
  318.3 9.8 %collective-permute-start.4 = (bf16[128,1536]{1,0:T(8,128)(2,1)S(1)}, bf16[128,1536]{1,0:T(8,128)(2,1)S(1)}, u32[]{:S(2)}, u32[]{:S(2)}) collective-permute-start(bf16[128,1536]{1,0:T(8,128)(2,1)S(1)} %fusion.18), channel_id=1, source_target_pairs={{32,0},{64,32},{96,64},{0,96},{33,1},{65,33},{97,65},{1,97},{34,2}... | collective-permute-start | bytes 1179656 | tf_op jit(solution)/shard_map/ppermute | solution.py:151

commit v7 on v6

--- a/solution.py
+++ b/solution.py
@@ -1,3 +1,5 @@
+import functools
+
 import jax
 import jax.numpy as jnp
 from jax import lax
@@ -13,6 +15,8 @@
 SHARE = SLOTS // 2
 BACK = [((i + 1) % 4, i) for i in range(4)]
 COLUMN_PARTS = 2
+SHARDS = 4
+FIRST = 1408
 VMEM = 56 * 1024 * 1024
 
 
@@ -67,25 +71,75 @@
     return out.reshape(DEVICES, SHARE, hidden)
 
 
-def copy_kernel(in_ref, out_ref):
-    out_ref[...] = in_ref[...]
-
-
-def cut(grads, h):
-    tokens, top, width = grads.shape
-    columns = width // 4
+def cut_kernel(start, size, in_ref, out_ref, held, sems):
+    hidden = in_ref.shape[2] // SHARDS
+    arrive, leave = [], []
+    for f in range(SHARDS):
+        source = in_ref.at[:, :, pl.ds(f * hidden + start, size)]
+        target = out_ref.at[:, :, pl.ds(f * size, size)]
+        arrive.append(pltpu.make_async_copy(source, held.at[f], sems.at[f]))
+        leave.append(pltpu.make_async_copy(held.at[f], target, sems.at[SHARDS + f]))
+    for copy in arrive:
+        copy.start()
+    for f in range(SHARDS):
+        arrive[f].wait()
+        leave[f].start()
+    for copy in leave:
+        copy.wait()
+
+
+def cut(grads, start, size):
+    tokens, top, _ = grads.shape
     return pl.pallas_call(
-        copy_kernel,
-        grid=(2,),
-        in_specs=[pl.BlockSpec((tokens, top, columns), lambda p: (0, 0, 2 * p + h))],
-        out_specs=pl.BlockSpec((tokens, top, columns), lambda p: (0, 0, p)),
-        out_shape=jax.ShapeDtypeStruct((tokens, top, width // 2), grads.dtype),
+        functools.partial(cut_kernel, start, size),
+        in_specs=[pl.BlockSpec(memory_space=pl.ANY)],
+        out_specs=pl.BlockSpec(memory_space=pl.ANY),
+        out_shape=jax.ShapeDtypeStruct((tokens, top, SHARDS * size), grads.dtype),
+        scratch_shapes=[
+            pltpu.VMEM((SHARDS, tokens, top, size), grads.dtype),
+            pltpu.SemaphoreType.DMA((2 * SHARDS,)),
+        ],
         compiler_params=pltpu.CompilerParams(vmem_limit_bytes=VMEM),
         cost_estimate=pl.CostEstimate(
-            flops=0, bytes_accessed=2 * tokens * top * width, transcendentals=0
+            flops=0, bytes_accessed=4 * tokens * top * SHARDS * size, transcendentals=0
         ),
         name="cut_grads",
     )(grads)
+
+
+def lay_kernel(core_ref, mine_ref, other_ref, wide_ref, narrow_ref):
+    def lay(lower, upper):
+        for n, w in enumerate((lower, upper)):
+            wide, narrow = FIRST, w.shape[1] - FIRST
+            wide_ref[:, n * wide : (n + 1) * wide] = w[:, :wide]
+            narrow_ref[:, n * narrow : (n + 1) * narrow] = w[:, wide:]
+
+    @pl.when(core_ref[0] == 0)
+    def _():
+        lay(mine_ref, other_ref)
+
+    @pl.when(core_ref[0] != 0)
+    def _():
+        lay(other_ref, mine_ref)
+
+
+def lay_weights(core, mine, other):
+    width, hidden = mine.shape
+    block = 256
+    sizes = (2 * FIRST, 2 * (hidden - FIRST))
+    return pl.pallas_call(
+        lay_kernel,
+        grid=(width // block,),
+        in_specs=[pl.BlockSpec(memory_space=pltpu.SMEM)]
+        + [pl.BlockSpec((block, hidden), lambda i: (i, 0))] * 2,
+        out_specs=[pl.BlockSpec((block, size), lambda i: (i, 0)) for size in sizes],
+        out_shape=[jax.ShapeDtypeStruct((width, size), mine.dtype) for size in sizes],
+        compiler_params=pltpu.CompilerParams(vmem_limit_bytes=VMEM),
+        cost_estimate=pl.CostEstimate(
+            flops=0, bytes_accessed=8 * width * hidden, transcendentals=0
+        ),
+        name="lay_weights",
+    )(core.reshape(1), mine, other)
 
 
 def products(grads, slopes):
@@ -115,23 +169,23 @@
     sent = bf16_dot(place_token, tokens, ((1,), (0,))).astype(jnp.bfloat16)
     rows = exchange(sent.reshape(DEVICES, SHARE, width)).reshape(rows_here, width)
 
-    pieces = [cut(hid_grad[0], h) for h in range(2)]
+    pieces = [cut(hid_grad[0], 0, FIRST), cut(hid_grad[0], FIRST, hidden - FIRST)]
     halves = [lax.ppermute(piece, "pipe", BACK) for piece in pieces]
     other = lax.ppermute(mine, "core", [(0, 1), (1, 0)])
-    lower = jnp.where(core == 0, mine, other)
-    upper = jnp.where(core == 0, other, mine)
-
-    first = exchange(place(target, halves[0])).reshape(rows_here, hidden)
-    slopes = [after(derivative(bf16_dot(rows, w, ((1,), (0,))))) for w in (lower, upper)]
+    weights = lay_weights(core, mine, other)
+
+    target, *weights = after(target, *weights)
+    first = exchange(place(target, halves[0])).reshape(rows_here, 2 * FIRST)
+    slopes = [after(derivative(bf16_dot(rows, w, ((1,), (0,))))) for w in weights]
     target, *slopes = after(target, *slopes)
     placed = place(target, halves[1])
     first, placed = after(first, placed)
-    second = exchange(placed).reshape(rows_here, hidden)
+    second = exchange(placed).reshape(rows_here, 2 * (hidden - FIRST))
 
     columns = width // COLUMN_PARTS
     early = []
     for j in range(COLUMN_PARTS):
-        part = lower[j * columns : (j + 1) * columns]
+        part = weights[0][j * columns : (j + 1) * columns]
         term = bf16_dot(products(*after(first, slopes[0])), part, ((1,), (1,)))
         early.append(after(term.astype(jnp.bfloat16)))
 
@@ -142,7 +196,7 @@
 
     parts = []
     for j in range(COLUMN_PARTS):
-        part = upper[j * columns : (j + 1) * columns]
+        part = weights[1][j * columns : (j + 1) * columns]
         late = bf16_dot(products(*after(second, slopes[1])), part, ((1,), (1,)))
         term = (early[j].astype(jnp.float32) + late).astype(jnp.bfloat16)
         returned = exchange(term.reshape(DEVICES, SHARE, columns)).reshape(-1, columns)

time: 330 us -> 327 us (level)
  Pallas kernels: 13.3 us -> 33.5 us
  other arithmetic: 19.6 us -> 2.1 us
  waiting for transfers between devices: 164 us -> 157 us
    pallas_call x2 -> x3, Pallas kernels: 5.26 us -> 25.4 us  [the longest x1 20.4 us: lay_weights(): pl.pallas_call(lay_kernel, grid=(width // block,), in_specs=[pl.BlockSpec...]
    select_n x1 -> x0, other arithmetic: 17 us -> none  [local(): upper = jnp.where(core == 0, other, mine)]
    all_to_all x5, waiting for transfers between devices: 110 us -> 105 us  [exchange(): return lax.all_to_all(block, PLANE, split_axis=0, concat_axis=0, tiled=True)]
  transfers between devices with their start and end apart: 10 -> 10, of which waited for: 7 -> 7; matrix products, arithmetic and copies ran while one was open for 32% -> 29% of each run, Pallas kernels for 4% -> 10%
where the time goes in v7:
time: 327 us; the launch traced here: 326 us
  waiting for transfers between devices  157 us (48%)
  matrix products  100 us (31%)
  Pallas kernels  33.5 us (10%)
  starting transfers between devices  30.5 us (9%)
    all_to_all x5, waiting for transfers between devices, exchange(): return lax.all_to_all(block, PLANE, split_axis=0, concat_axis=0, tiled=True)  105 us
    dot_general x9, matrix products, bf16_dot(): lax.dot_general(a, b, (dims, ((), ())), preferred_element_type=jnp.float32)  100 us
    ppermute x2, waiting for transfers between devices, local(): halves = [lax.ppermute(piece, 'pipe', BACK) for piece in pieces]  42.4 us
    all_to_all x5, starting transfers between devices, exchange(): return lax.all_to_all(block, PLANE, split_axis=0, concat_axis=0, tiled=True)  27.6 us
    pallas_call x1, Pallas kernels, lay_weights(): pl.pallas_call(lay_kernel, grid=(width // block,), in_specs=[pl.BlockSpec...  20.4 us
    ppermute x2, waiting for transfers between devices, local(): parts.append(lax.ppermute(summed, 'pipe', BACK))  9.14 us
    pallas_call x2, Pallas kernels, place(): pl.pallas_call(place_kernel, grid=(2, steps), in_specs=[pl.BlockSpec((1,...  8.14 us
  transfers between devices with their start and end apart: 10, of which 7 were waited for; matrix products, arithmetic and copies ran while one was open for 29% of the time, Pallas kernels for 10%

profile of v7, /device:TPU:24, one launch (start us, length us, event | category | flops | bytes accessed | tf_op | source)
XLA Modules:
  0.0 326.2 jit_solution(14941932878420336715)
XLA Ops:
  0.0 0.9 copy.10
  1.6 4.6 %convolution_convert_fusion = bf16[1024,3072]{1,0:T(8,128)(2,1)} fusion(bf16[1,128,3072]{2,1,0:T(8,128)(2,1)S(1)} %copy-done, s32[128]{0:T(128)S(1)} %get-tuple-element.34, s32[128]{0:T(128)S(1)} %get-tuple-element.33, s32[1024]{0:T(1024)S(1)} %eq.85), kind=kOutput, calls=%fused_computation.8 | convolution fusion | flops 808845312 | bytes 7083008 | tf_op jit(solution)/shard_map/dot_general | solution.py:37
  6.2 8.3 %all-to-all-start.1 = ((bf16[32,32,3072]{2,1,0:T(8,128)(2,1)}), bf16[32,32,3072]{2,1,0:T(8,128)(2,1)}, u32[]{:S(2)}, u32[]{:S(2)}) async-start(bf16[32,32,3072]{2,1,0:T(8,128)(2,1)} %bitcast.33), calls=%async_computation.1 | async-start | bytes 12582912 | tf_op jit(solution)/shard_map/all_to_all | solution.py:24
  14.5 2.8 cut_grads.2
  17.3 0.8 collective-permute-start.1
  18.2 2.2 cut_grads.3
  21.4 20.4 %lay_weights.1 = (bf16[3072,2816]{1,0:T(8,128)(2,1)}, bf16[3072,1280]{1,0:T(8,128)(2,1)}) custom-call(s32[1]{0:T(128)} %bitcast.4.core_ref, bf16[3072,2048]{1,0:T(8,128)(2,1)} %bitcast.38, bf16[3072,2048]{1,0:T(8,128)(2,1)} %collective-permute-done.other_ref), custom_call_target="tpu_custom_call" | custom-call | bytes 50331648 | tf_op jit(solution)/shard_map/lay_weights/pallas_call | solution.py:130
  41.8 42.4 %collective-permute-done.1.grads_ref = bf16[128,2,5632]{2,1,0:T(2,128)(2,1)} collective-permute-done((bf16[128,2,5632]{2,1,0:T(2,128)(2,1)}, bf16[128,2,5632]{2,1,0:T(2,128)(2,1)}, u32[]{:S(2)}, u32[]{:S(2)}) %collective-permute-start.1) | collective-permute-done | bytes 2883616 | tf_op jit(solution)/shard_map/ppermute | solution.py:173
  84.3 4.9 %place_grads.2 = bf16[8,2,2,32,2816]{4,3,2,1,0:T(8,128)(2,1)} custom-call(s32[1,256]{1,0:T(1,128)} %bitcast.44, bf16[128,2,5632]{2,1,0:T(2,128)(2,1)} %collective-permute-done.1.grads_ref), custom_call_target="tpu_custom_call" | custom-call | flops 1476395008 | bytes 8650752 | tf_op jit(solution)/shard_map/place_grads/pallas_call | solution.py:54
  89.1 3.3 %all-to-all-done.1 = bf16[32,32,3072]{2,1,0:T(8,128)(2,1)} async-done(((bf16[32,32,3072]{2,1,0:T(8,128)(2,1)}), bf16[32,32,3072]{2,1,0:T(8,128)(2,1)}, u32[]{:S(2)}, u32[]{:S(2)}) %all-to-all-start.1) | async-done | bytes 6291488 | tf_op jit(solution)/shard_map/all_to_all | solution.py:24
  92.4 5.1 %all-to-all-start = ((bf16[32,32,2816]{2,1,0:T(8,128)(2,1)}), bf16[32,32,2816]{2,1,0:T(8,128)(2,1)}, u32[]{:S(2)}, u32[]{:S(2)}) async-start(bf16[32,32,2816]{2,1,0:T(8,128)(2,1)} %bitcast.34), calls=%async_computation | async-start | bytes 11534336 | tf_op jit(solution)/shard_map/all_to_all | solution.py:24
  97.5 27.5 %multiply_convert_fusion.1 = bf16[1024,2816]{1,0:T(8,128)(2,1)} fusion(bf16[1024,3072]{1,0:T(8,128)(2,1)} %bitcast.12, bf16[3072,2816]{1,0:T(8,128)(2,1)} %get-tuple-element.22), kind=kOutput, calls=%fused_computation.1 | convolution fusion | flops 17739808768 | bytes 29360128 | tf_op jit(solution)/shard_map/dot_general | solution.py:37
  125.0 14.5 %multiply_convert_fusion.3 = bf16[1024,1280]{1,0:T(8,128)(2,1)} fusion(bf16[1024,3072]{1,0:T(8,128)(2,1)} %bitcast.12, bf16[3072,1280]{1,0:T(8,128)(2,1)} %get-tuple-element.23), kind=kOutput, calls=%fused_computation.10 | convolution fusion | flops 8063549440 | bytes 16777216 | tf_op jit(solution)/shard_map/dot_general | solution.py:37
  139.5 1.1 copy-done.2
  140.6 3.3 %place_grads.3 = bf16[8,2,2,32,1280]{4,3,2,1,0:T(8,128)(2,1)} custom-call(s32[1,256]{1,0:T(1,128)} %bitcast.45, bf16[128,2,2560]{2,1,0:T(2,128)(2,1)} %copy-done.2), custom_call_target="tpu_custom_call" | custom-call | flops 671088640 | bytes 3932160 | tf_op jit(solution)/shard_map/place_grads/pallas_call | solution.py:54
  143.8 25.1 %all-to-all-done = bf16[32,32,2816]{2,1,0:T(8,128)(2,1)} async-done(((bf16[32,32,2816]{2,1,0:T(8,128)(2,1)}), bf16[32,32,2816]{2,1,0:T(8,128)(2,1)}, u32[]{:S(2)}, u32[]{:S(2)}) %all-to-all-start) | async-done | bytes 5767200 | tf_op jit(solution)/shard_map/all_to_all | solution.py:24
  169.0 4.3 %all-to-all-start.2 = ((bf16[32,32,1280]{2,1,0:T(8,128)(2,1)}), bf16[32,32,1280]{2,1,0:T(8,128)(2,1)S(1)}, u32[]{:S(2)}, u32[]{:S(2)}) async-start(bf16[32,32,1280]{2,1,0:T(8,128)(2,1)} %bitcast.39), calls=%async_computation.2 | async-start | bytes 5242880 | tf_op jit(solution)/shard_map/all_to_all | solution.py:24
  173.2 15.7 %fusion.6 = bf16[1024,1536]{1,0:T(8,128)(2,1)} fusion(bf16[3072,2816]{1,0:T(8,128)(2,1)} %get-tuple-element.22, bf16[1024,2816]{1,0:T(8,128)(2,1)} %multiply_convert_fusion.1, bf16[1024,2816]{1,0:T(8,128)(2,1)} %bitcast.9), kind=kOutput, calls=%fused_computation.13 | convolution fusion | flops 8871477248 | bytes 23330816 | tf_op jit(solution)/shard_map/dot_general | solution.py:37
  188.9 20.1 %all-to-all-done.2 = bf16[32,32,1280]{2,1,0:T(8,128)(2,1)S(1)} async-done(((bf16[32,32,1280]{2,1,0:T(8,128)(2,1)}), bf16[32,32,1280]{2,1,0:T(8,128)(2,1)S(1)}, u32[]{:S(2)}, u32[]{:S(2)}) %all-to-all-start.2) | async-done | bytes 2621472 | tf_op jit(solution)/shard_map/all_to_all | solution.py:24
  209.1 9.8 %add_convert_fusion.1 = bf16[1024,1536]{1,0:T(8,128)(2,1)} fusion(bf16[1024,1536]{1,0:T(8,128)(2,1)} %fusion.6, bf16[3072,1280]{1,0:T(8,128)(2,1)} %get-tuple-element.23, bf16[1024,1280]{1,0:T(8,128)(2,1)} %multiply_convert_fusion.3, bf16[1024,1280]{1,0:T(8,128)(2,1)S(1)} %bitcast.42), kind=kOutput, calls=%fused_computation.7 | convolution fusion | flops 4036493312 | bytes 15466496 | tf_op jit(solution)/shard_map/dot_general | solution.py:37
  218.9 4.8 %all-to-all-start.3 = ((bf16[32,32,1536]{2,1,0:T(8,128)(2,1)}), bf16[32,32,1536]{2,1,0:T(8,128)(2,1)}, u32[]{:S(2)}, u32[]{:S(2)}) async-start(bf16[32,32,1536]{2,1,0:T(8,128)(2,1)} %bitcast.41), calls=%async_computation.3 | async-start | bytes 6291456 | tf_op jit(solution)/shard_map/all_to_all | solution.py:24
  223.7 14.7 %fusion.9 = bf16[1024,1536]{1,0:T(8,128)(2,1)S(1)} fusion(bf16[3072,2816]{1,0:T(8,128)(2,1)} %get-tuple-element.22, bf16[1024,2816]{1,0:T(8,128)(2,1)} %multiply_convert_fusion.1, bf16[1024,2816]{1,0:T(8,128)(2,1)} %bitcast.9), kind=kOutput, calls=%fused_computation.14 | convolution fusion | flops 8871477248 | bytes 23330816 | tf_op jit(solution)/shard_map/dot_general | solution.py:37
  238.4 7.8 %add_convert_fusion = bf16[1024,1536]{1,0:T(8,128)(2,1)} fusion(bf16[1024,1536]{1,0:T(8,128)(2,1)S(1)} %fusion.9, bf16[3072,1280]{1,0:T(8,128)(2,1)} %get-tuple-element.23, bf16[1024,1280]{1,0:T(8,128)(2,1)S(1)} %copy-done.4, bf16[1024,1280]{1,0:T(8,128)(2,1)S(1)} %bitcast.43), kind=kOutput, calls=%fused_computation.6 | convolution fusion | flops 4036493312 | bytes 15466496 | tf_op jit(solution)/shard_map/dot_general | solution.py:37
  246.3 19.2 %all-to-all-done.3 = bf16[32,32,1536]{2,1,0:T(8,128)(2,1)} async-done(((bf16[32,32,1536]{2,1,0:T(8,128)(2,1)}), bf16[32,32,1536]{2,1,0:T(8,128)(2,1)}, u32[]{:S(2)}, u32[]{:S(2)}) %all-to-all-start.3) | async-done | bytes 3145760 | tf_op jit(solution)/shard_map/all_to_all | solution.py:24
  265.5 5.1 %all-to-all-start.4 = ((bf16[32,32,1536]{2,1,0:T(8,128)(2,1)}), bf16[32,32,1536]{2,1,0:T(8,128)(2,1)}, u32[]{:S(2)}, u32[]{:S(2)}) async-start(bf16[32,32,1536]{2,1,0:T(8,128)(2,1)} %bitcast.40), calls=%async_computation.4 | async-start | bytes 6291456 | tf_op jit(solution)/shard_map/all_to_all | solution.py:24
  270.8 2.9 fusion.20
  273.8 0.8 collective-permute-start.3
  274.7 37.7 %all-to-all-done.4 = bf16[32,32,1536]{2,1,0:T(8,128)(2,1)} async-done(((bf16[32,32,1536]{2,1,0:T(8,128)(2,1)}), bf16[32,32,1536]{2,1,0:T(8,128)(2,1)}, u32[]{:S(2)}, u32[]{:S(2)}) %all-to-all-start.4) | async-done | bytes 3145760 | tf_op jit(solution)/shard_map/all_to_all | solution.py:24
  312.3 2.9 fusion.19
  315.3 0.8 collective-permute-start.4
  316.1 9.1 %collective-permute-done.4 = bf16[128,1536]{1,0:T(8,128)(2,1)S(1)} collective-permute-done((bf16[128,1536]{1,0:T(8,128)(2,1)S(1)}, bf16[128,1536]{1,0:T(8,128)(2,1)S(1)}, u32[]{:S(2)}, u32[]{:S(2)}) %collective-permute-start.4) | collective-permute-done | bytes 393248 | tf_op jit(solution)/shard_map/ppermute | solution.py:205
  325.2 1.0 maximum_bitcast_fusion
  (27 shorter events, 2.2 us)
Async XLA Ops:
  0.0 1.6 copy-start
  0.0 21.4 %collective-permute-start = (bf16[3072,2048]{1,0:T(8,128)(2,1)}, bf16[3072,2048]{1,0:T(8,128)(2,1)}, u32[]{:S(2)}, u32[]{:S(2)}) collective-permute-start(bf16[3072,2048]{1,0:T(8,128)(2,1)} %bitcast.37), channel_id=1, source_target_pairs={{0,1},{1,0},{2,3},{3,2},{4,5},{5,4},{6,7},{7,6},{8,9},{9,8},{10,11... | collective-permute-start | bytes 37748744 | tf_op jit(solution)/shard_map/ppermute | solution.py:174
  6.2 86.2 %all-to-all-start.1 = ((bf16[32,32,3072]{2,1,0:T(8,128)(2,1)}), bf16[32,32,3072]{2,1,0:T(8,128)(2,1)}, u32[]{:S(2)}, u32[]{:S(2)}) async-start(bf16[32,32,3072]{2,1,0:T(8,128)(2,1)} %bitcast.33), calls=%async_computation.1 | async-start | bytes 12582912 | tf_op jit(solution)/shard_map/all_to_all | solution.py:24
  17.3 66.9 %collective-permute-start.1 = (bf16[128,2,5632]{2,1,0:T(2,128)(2,1)}, bf16[128,2,5632]{2,1,0:T(2,128)(2,1)}, u32[]{:S(2)}, u32[]{:S(2)}) collective-permute-start(bf16[128,2,5632]{2,1,0:T(2,128)(2,1)} %cut_grads.2), channel_id=1, source_target_pairs={{32,0},{64,32},{96,64},{0,96},{33,1},{65,33},{97,65},{1,97},{34,2}... | collective-permute-start | bytes 8650760 | tf_op jit(solution)/shard_map/ppermute | solution.py:173
  20.3 119.1 %collective-permute-start.2 = (bf16[128,2,2560]{2,1,0:T(2,128)(2,1)}, bf16[128,2,2560]{2,1,0:T(2,128)(2,1)S(1)}, u32[]{:S(2)}, u32[]{:S(2)}) collective-permute-start(bf16[128,2,2560]{2,1,0:T(2,128)(2,1)} %cut_grads.3), channel_id=1, source_target_pairs={{32,0},{64,32},{96,64},{0,96},{33,1},{65,33},{97,65},{1,97},{34,2}... | collective-permute-start | bytes 3932168 | tf_op jit(solution)/shard_map/ppermute | solution.py:173
  92.4 76.5 %all-to-all-start = ((bf16[32,32,2816]{2,1,0:T(8,128)(2,1)}), bf16[32,32,2816]{2,1,0:T(8,128)(2,1)}, u32[]{:S(2)}, u32[]{:S(2)}) async-start(bf16[32,32,2816]{2,1,0:T(8,128)(2,1)} %bitcast.34), calls=%async_computation | async-start | bytes 11534336 | tf_op jit(solution)/shard_map/all_to_all | solution.py:24
  139.5 1.1 copy-start.2
  169.0 40.1 %all-to-all-start.2 = ((bf16[32,32,1280]{2,1,0:T(8,128)(2,1)}), bf16[32,32,1280]{2,1,0:T(8,128)(2,1)S(1)}, u32[]{:S(2)}, u32[]{:S(2)}) async-start(bf16[32,32,1280]{2,1,0:T(8,128)(2,1)} %bitcast.39), calls=%async_computation.2 | async-start | bytes 5242880 | tf_op jit(solution)/shard_map/all_to_all | solution.py:24
  218.9 46.6 %all-to-all-start.3 = ((bf16[32,32,1536]{2,1,0:T(8,128)(2,1)}), bf16[32,32,1536]{2,1,0:T(8,128)(2,1)}, u32[]{:S(2)}, u32[]{:S(2)}) async-start(bf16[32,32,1536]{2,1,0:T(8,128)(2,1)} %bitcast.41), calls=%async_computation.3 | async-start | bytes 6291456 | tf_op jit(solution)/shard_map/all_to_all | solution.py:24
  223.7 14.7 %copy-start.4 = (bf16[1024,1280]{1,0:T(8,128)(2,1)S(1)}, bf16[1024,1280]{1,0:T(8,128)(2,1)}, u32[]{:S(2)}) copy-start(bf16[1024,1280]{1,0:T(8,128)(2,1)} %multiply_convert_fusion.3) | copy-start | bytes 7864324
  246.3 24.3 %copy-start.3 = (f32[1,128,2]{1,2,0:T(2,128)S(1)}, f32[1,128,2]{1,2,0:T(2,128)}, u32[]{:S(2)}) copy-start(f32[1,128,2]{1,2,0:T(2,128)} %param.8) | copy-start | bytes 3076
  265.5 46.9 %all-to-all-start.4 = ((bf16[32,32,1536]{2,1,0:T(8,128)(2,1)}), bf16[32,32,1536]{2,1,0:T(8,128)(2,1)}, u32[]{:S(2)}, u32[]{:S(2)}) async-start(bf16[32,32,1536]{2,1,0:T(8,128)(2,1)} %bitcast.40), calls=%async_computation.4 | async-start | bytes 6291456 | tf_op jit(solution)/shard_map/all_to_all | solution.py:24
  270.8 55.4 %copy-start.1 = (bf16[1,128,3072]{2,1,0:T(8,128)(2,1)S(1)}, bf16[1,128,3072]{2,1,0:T(8,128)(2,1)}, u32[]{:S(2)}) copy-start(bf16[1,128,3072]{2,1,0:T(8,128)(2,1)} %param.5) | copy-start | bytes 2359300
  273.8 42.3 %collective-permute-start.3 = (bf16[128,1536]{1,0:T(8,128)(2,1)S(1)}, bf16[128,1536]{1,0:T(8,128)(2,1)S(1)}, u32[]{:S(2)}, u32[]{:S(2)}) collective-permute-start(bf16[128,1536]{1,0:T(8,128)(2,1)S(1)} %fusion.13), channel_id=1, source_target_pairs={{32,0},{64,32},{96,64},{0,96},{33,1},{65,33},{97,65},{1,97},{34,2}... | collective-permute-start | bytes 1179656 | tf_op jit(solution)/shard_map/ppermute | solution.py:205
  315.3 10.0 %collective-permute-start.4 = (bf16[128,1536]{1,0:T(8,128)(2,1)S(1)}, bf16[128,1536]{1,0:T(8,128)(2,1)S(1)}, u32[]{:S(2)}, u32[]{:S(2)}) collective-permute-start(bf16[128,1536]{1,0:T(8,128)(2,1)S(1)} %fusion.12), channel_id=1, source_target_pairs={{32,0},{64,32},{96,64},{0,96},{33,1},{65,33},{97,65},{1,97},{34,2}... | collective-permute-start | bytes 1179656 | tf_op jit(solution)/shard_map/ppermute | solution.py:205

commit v8 on v7

--- a/solution.py
+++ b/solution.py
@@ -154,17 +154,17 @@
     core = lax.axis_index("core")
     rows_here = DEVICES * SHARE
 
-    flat_expert = routes[0].reshape(-1)
+    flat_expert = routes[0].T.reshape(-1)
     pairs = flat_expert.shape[0]
     number = jnp.arange(pairs, dtype=jnp.int32)
     earlier = (flat_expert[:, None] == flat_expert[None, :]) & (number[None, :] < number[:, None])
     slot = jnp.sum(earlier.astype(jnp.int32), axis=1)
-    target = flat_expert * SLOTS + slot
-    by_token = target.reshape(n_tokens, TOP)
+    by_route = (flat_expert * SLOTS + slot).reshape(TOP, n_tokens)
+    target = by_route.T.reshape(-1)
 
     places = jnp.arange(EXPERTS * SLOTS, dtype=jnp.int32).reshape(EXPERTS, 1, SLOTS)
     places = jnp.broadcast_to(places, (EXPERTS, 2, SLOTS)).reshape(-1)
-    row_hit = [places[:, None] == by_token[None, :, k] for k in range(TOP)]
+    row_hit = [places[:, None] == by_route[None, k] for k in range(TOP)]
     place_token = (row_hit[0] | row_hit[1]).astype(jnp.bfloat16)
     sent = bf16_dot(place_token, tokens, ((1,), (0,))).astype(jnp.bfloat16)
     rows = exchange(sent.reshape(DEVICES, SHARE, width)).reshape(rows_here, width)
@@ -189,7 +189,7 @@
         term = bf16_dot(products(*after(first, slopes[0])), part, ((1,), (1,)))
         early.append(after(term.astype(jnp.bfloat16)))
 
-    hit = [by_token[:, k, None] == places[None, :] for k in range(TOP)]
+    hit = [by_route[k, :, None] == places[None, :] for k in range(TOP)]
     mix = sum(jnp.where(hit[k], probs[0][:, k, None], 0.0) for k in range(TOP))
     high = lax.reduce_precision(mix, 8, 7)
     mix = jnp.concatenate([high, mix - high]).astype(jnp.bfloat16)

time: 327 us -> 327 us (level)
  no operation moved by 1% of the time
where the time goes in v8:
time: 327 us; the launch traced here: 326 us
  waiting for transfers between devices  157 us (48%)
  matrix products  100 us (31%)
  Pallas kernels  33.6 us (10%)
  starting transfers between devices  30.6 us (9%)
    all_to_all x5, waiting for transfers between devices, exchange(): return lax.all_to_all(block, PLANE, split_axis=0, concat_axis=0, tiled=True)  105 us
    dot_general x9, matrix products, bf16_dot(): lax.dot_general(a, b, (dims, ((), ())), preferred_element_type=jnp.float32)  100 us
    ppermute x2, waiting for transfers between devices, local(): halves = [lax.ppermute(piece, 'pipe', BACK) for piece in pieces]  42.2 us
    all_to_all x5, starting transfers between devices, exchange(): return lax.all_to_all(block, PLANE, split_axis=0, concat_axis=0, tiled=True)  27.6 us
    pallas_call x1, Pallas kernels, lay_weights(): pl.pallas_call(lay_kernel, grid=(width // block,), in_specs=[pl.BlockSpec...  20.4 us
    ppermute x2, waiting for transfers between devices, local(): parts.append(lax.ppermute(summed, 'pipe', BACK))  9.14 us
    pallas_call x2, Pallas kernels, place(): pl.pallas_call(place_kernel, grid=(2, steps), in_specs=[pl.BlockSpec((1,...  8.19 us
  transfers between devices with their start and end apart: 10, of which 7 were waited for; matrix products, arithmetic and copies ran while one was open for 29% of the time, Pallas kernels for 10%

profile of v8, /device:TPU:24, one launch (start us, length us, event | category | flops | bytes accessed | tf_op | source)
XLA Modules:
  0.0 326.4 jit_solution(15353018858838542938)
XLA Ops:
  0.1 0.9 convert_reduce_fusion
  1.7 4.6 %convolution_convert_fusion = bf16[1024,3072]{1,0:T(8,128)(2,1)} fusion(bf16[1,128,3072]{2,1,0:T(8,128)(2,1)S(1)} %copy-done, s32[128]{0:T(128)S(1)} %get-tuple-element.38, s32[128]{0:T(128)S(1)} %get-tuple-element.37, s32[1024]{0:T(1024)S(1)} %eq.77), kind=kOutput, calls=%fused_computation.8 | convolution fusion | flops 808845312 | bytes 7083008 | tf_op jit(solution)/shard_map/dot_general | solution.py:37
  6.3 8.4 %all-to-all-start.1 = ((bf16[32,32,3072]{2,1,0:T(8,128)(2,1)}), bf16[32,32,3072]{2,1,0:T(8,128)(2,1)}, u32[]{:S(2)}, u32[]{:S(2)}) async-start(bf16[32,32,3072]{2,1,0:T(8,128)(2,1)} %bitcast.46), calls=%async_computation.1 | async-start | bytes 12582912 | tf_op jit(solution)/shard_map/all_to_all | solution.py:24
  14.7 2.8 cut_grads.2
  17.5 0.8 collective-permute-start.1
  18.4 2.1 cut_grads.3
  21.8 20.4 %lay_weights.1 = (bf16[3072,2816]{1,0:T(8,128)(2,1)}, bf16[3072,1280]{1,0:T(8,128)(2,1)}) custom-call(s32[1]{0:T(128)} %bitcast.10.core_ref, bf16[3072,2048]{1,0:T(8,128)(2,1)} %bitcast.51, bf16[3072,2048]{1,0:T(8,128)(2,1)} %collective-permute-done.other_ref), custom_call_target="tpu_custom_call" | custom-call | bytes 50331648 | tf_op jit(solution)/shard_map/lay_weights/pallas_call | solution.py:130
  42.3 42.2 %collective-permute-done.1.grads_ref = bf16[128,2,5632]{2,1,0:T(2,128)(2,1)} collective-permute-done((bf16[128,2,5632]{2,1,0:T(2,128)(2,1)}, bf16[128,2,5632]{2,1,0:T(2,128)(2,1)}, u32[]{:S(2)}, u32[]{:S(2)}) %collective-permute-start.1) | collective-permute-done | bytes 2883616 | tf_op jit(solution)/shard_map/ppermute | solution.py:173
  84.5 4.9 %place_grads.2 = bf16[8,2,2,32,2816]{4,3,2,1,0:T(8,128)(2,1)} custom-call(s32[1,256]{1,0:T(1,128)} %bitcast.58, bf16[128,2,5632]{2,1,0:T(2,128)(2,1)} %collective-permute-done.1.grads_ref), custom_call_target="tpu_custom_call" | custom-call | flops 1476395008 | bytes 8650752 | tf_op jit(solution)/shard_map/place_grads/pallas_call | solution.py:54
  89.3 3.2 all-to-all-done.1
  92.6 5.1 %all-to-all-start = ((bf16[32,32,2816]{2,1,0:T(8,128)(2,1)}), bf16[32,32,2816]{2,1,0:T(8,128)(2,1)}, u32[]{:S(2)}, u32[]{:S(2)}) async-start(bf16[32,32,2816]{2,1,0:T(8,128)(2,1)} %bitcast.47), calls=%async_computation | async-start | bytes 11534336 | tf_op jit(solution)/shard_map/all_to_all | solution.py:24
  97.7 27.4 %multiply_convert_fusion.1 = bf16[1024,2816]{1,0:T(8,128)(2,1)} fusion(bf16[1024,3072]{1,0:T(8,128)(2,1)} %bitcast.18, bf16[3072,2816]{1,0:T(8,128)(2,1)} %get-tuple-element.22), kind=kOutput, calls=%fused_computation.1 | convolution fusion | flops 17739808768 | bytes 29360128 | tf_op jit(solution)/shard_map/dot_general | solution.py:37
  125.1 14.5 %multiply_convert_fusion.3 = bf16[1024,1280]{1,0:T(8,128)(2,1)} fusion(bf16[1024,3072]{1,0:T(8,128)(2,1)} %bitcast.18, bf16[3072,1280]{1,0:T(8,128)(2,1)} %get-tuple-element.23), kind=kOutput, calls=%fused_computation.10 | convolution fusion | flops 8063549440 | bytes 16777216 | tf_op jit(solution)/shard_map/dot_general | solution.py:37
  139.6 1.1 copy-done.2
  140.7 3.3 %place_grads.3 = bf16[8,2,2,32,1280]{4,3,2,1,0:T(8,128)(2,1)} custom-call(s32[1,256]{1,0:T(1,128)} %bitcast.59, bf16[128,2,2560]{2,1,0:T(2,128)(2,1)} %copy-done.2), custom_call_target="tpu_custom_call" | custom-call | flops 671088640 | bytes 3932160 | tf_op jit(solution)/shard_map/place_grads/pallas_call | solution.py:54
  144.0 25.2 %all-to-all-done = bf16[32,32,2816]{2,1,0:T(8,128)(2,1)} async-done(((bf16[32,32,2816]{2,1,0:T(8,128)(2,1)}), bf16[32,32,2816]{2,1,0:T(8,128)(2,1)}, u32[]{:S(2)}, u32[]{:S(2)}) %all-to-all-start) | async-done | bytes 5767200 | tf_op jit(solution)/shard_map/all_to_all | solution.py:24
  169.1 4.3 %all-to-all-start.2 = ((bf16[32,32,1280]{2,1,0:T(8,128)(2,1)}), bf16[32,32,1280]{2,1,0:T(8,128)(2,1)S(1)}, u32[]{:S(2)}, u32[]{:S(2)}) async-start(bf16[32,32,1280]{2,1,0:T(8,128)(2,1)} %bitcast.52), calls=%async_computation.2 | async-start | bytes 5242880 | tf_op jit(solution)/shard_map/all_to_all | solution.py:24
  173.4 15.7 %fusion.6 = bf16[1024,1536]{1,0:T(8,128)(2,1)} fusion(bf16[3072,2816]{1,0:T(8,128)(2,1)} %get-tuple-element.22, bf16[1024,2816]{1,0:T(8,128)(2,1)} %multiply_convert_fusion.1, bf16[1024,2816]{1,0:T(8,128)(2,1)} %bitcast.15), kind=kOutput, calls=%fused_computation.13 | convolution fusion | flops 8871477248 | bytes 23330816 | tf_op jit(solution)/shard_map/dot_general | solution.py:37
  189.1 20.2 %all-to-all-done.2 = bf16[32,32,1280]{2,1,0:T(8,128)(2,1)S(1)} async-done(((bf16[32,32,1280]{2,1,0:T(8,128)(2,1)}), bf16[32,32,1280]{2,1,0:T(8,128)(2,1)S(1)}, u32[]{:S(2)}, u32[]{:S(2)}) %all-to-all-start.2) | async-done | bytes 2621472 | tf_op jit(solution)/shard_map/all_to_all | solution.py:24
  209.3 9.8 %add_convert_fusion.1 = bf16[1024,1536]{1,0:T(8,128)(2,1)} fusion(bf16[1024,1536]{1,0:T(8,128)(2,1)} %fusion.6, bf16[3072,1280]{1,0:T(8,128)(2,1)} %get-tuple-element.23, bf16[1024,1280]{1,0:T(8,128)(2,1)} %multiply_convert_fusion.3, bf16[1024,1280]{1,0:T(8,128)(2,1)S(1)} %bitcast.55), kind=kOutput, calls=%fused_computation.7 | convolution fusion | flops 4036493312 | bytes 15466496 | tf_op jit(solution)/shard_map/dot_general | solution.py:37
  219.1 4.8 %all-to-all-start.3 = ((bf16[32,32,1536]{2,1,0:T(8,128)(2,1)}), bf16[32,32,1536]{2,1,0:T(8,128)(2,1)}, u32[]{:S(2)}, u32[]{:S(2)}) async-start(bf16[32,32,1536]{2,1,0:T(8,128)(2,1)} %bitcast.54), calls=%async_computation.3 | async-start | bytes 6291456 | tf_op jit(solution)/shard_map/all_to_all | solution.py:24
  223.9 14.7 %fusion.9 = bf16[1024,1536]{1,0:T(8,128)(2,1)S(1)} fusion(bf16[3072,2816]{1,0:T(8,128)(2,1)} %get-tuple-element.22, bf16[1024,2816]{1,0:T(8,128)(2,1)} %multiply_convert_fusion.1, bf16[1024,2816]{1,0:T(8,128)(2,1)} %bitcast.15), kind=kOutput, calls=%fused_computation.14 | convolution fusion | flops 8871477248 | bytes 23330816 | tf_op jit(solution)/shard_map/dot_general | solution.py:37
  238.6 7.8 %add_convert_fusion = bf16[1024,1536]{1,0:T(8,128)(2,1)} fusion(bf16[1024,1536]{1,0:T(8,128)(2,1)S(1)} %fusion.9, bf16[3072,1280]{1,0:T(8,128)(2,1)} %get-tuple-element.23, bf16[1024,1280]{1,0:T(8,128)(2,1)S(1)} %copy-done.5, bf16[1024,1280]{1,0:T(8,128)(2,1)S(1)} %bitcast.56), kind=kOutput, calls=%fused_computation.6 | convolution fusion | flops 4036493312 | bytes 15466496 | tf_op jit(solution)/shard_map/dot_general | solution.py:37
  246.4 19.2 %all-to-all-done.3 = bf16[32,32,1536]{2,1,0:T(8,128)(2,1)} async-done(((bf16[32,32,1536]{2,1,0:T(8,128)(2,1)}), bf16[32,32,1536]{2,1,0:T(8,128)(2,1)}, u32[]{:S(2)}, u32[]{:S(2)}) %all-to-all-start.3) | async-done | bytes 3145760 | tf_op jit(solution)/shard_map/all_to_all | solution.py:24
  265.6 5.1 %all-to-all-start.4 = ((bf16[32,32,1536]{2,1,0:T(8,128)(2,1)}), bf16[32,32,1536]{2,1,0:T(8,128)(2,1)}, u32[]{:S(2)}, u32[]{:S(2)}) async-start(bf16[32,32,1536]{2,1,0:T(8,128)(2,1)} %bitcast.53), calls=%async_computation.4 | async-start | bytes 6291456 | tf_op jit(solution)/shard_map/all_to_all | solution.py:24
  271.0 2.9 fusion.20
  274.0 0.8 collective-permute-start.3
  274.8 37.7 %all-to-all-done.4 = bf16[32,32,1536]{2,1,0:T(8,128)(2,1)} async-done(((bf16[32,32,1536]{2,1,0:T(8,128)(2,1)}), bf16[32,32,1536]{2,1,0:T(8,128)(2,1)}, u32[]{:S(2)}, u32[]{:S(2)}) %all-to-all-start.4) | async-done | bytes 3145760 | tf_op jit(solution)/shard_map/all_to_all | solution.py:24
  312.5 2.9 fusion.19
  315.5 0.8 collective-permute-start.4
  316.3 9.1 %collective-permute-done.4 = bf16[128,1536]{1,0:T(8,128)(2,1)S(1)} collective-permute-done((bf16[128,1536]{1,0:T(8,128)(2,1)S(1)}, bf16[128,1536]{1,0:T(8,128)(2,1)S(1)}, u32[]{:S(2)}, u32[]{:S(2)}) %collective-permute-start.4) | collective-permute-done | bytes 393248 | tf_op jit(solution)/shard_map/ppermute | solution.py:205
  325.4 1.0 maximum_bitcast_fusion
  (28 shorter events, 2.5 us)
Async XLA Ops:
  0.0 1.7 copy-start
  0.0 21.8 %collective-permute-start = (bf16[3072,2048]{1,0:T(8,128)(2,1)}, bf16[3072,2048]{1,0:T(8,128)(2,1)}, u32[]{:S(2)}, u32[]{:S(2)}) collective-permute-start(bf16[3072,2048]{1,0:T(8,128)(2,1)} %bitcast.50), channel_id=1, source_target_pairs={{0,1},{1,0},{2,3},{3,2},{4,5},{5,4},{6,7},{7,6},{8,9},{9,8},{10,11... | collective-permute-start | bytes 37748744 | tf_op jit(solution)/shard_map/ppermute | solution.py:174
  6.3 86.3 %all-to-all-start.1 = ((bf16[32,32,3072]{2,1,0:T(8,128)(2,1)}), bf16[32,32,3072]{2,1,0:T(8,128)(2,1)}, u32[]{:S(2)}, u32[]{:S(2)}) async-start(bf16[32,32,3072]{2,1,0:T(8,128)(2,1)} %bitcast.46), calls=%async_computation.1 | async-start | bytes 12582912 | tf_op jit(solution)/shard_map/all_to_all | solution.py:24
  14.7 6.3 %copy-start.3 = (s32[1,128,2]{1,2,0:T(2,128)S(1)}, s32[1,128,2]{1,2,0:T(2,128)}, u32[]{:S(2)}) copy-start(s32[1,128,2]{1,2,0:T(2,128)} %param.7) | copy-start | bytes 3076
  17.5 66.9 %collective-permute-start.1 = (bf16[128,2,5632]{2,1,0:T(2,128)(2,1)}, bf16[128,2,5632]{2,1,0:T(2,128)(2,1)}, u32[]{:S(2)}, u32[]{:S(2)}) collective-permute-start(bf16[128,2,5632]{2,1,0:T(2,128)(2,1)} %cut_grads.2), channel_id=1, source_target_pairs={{32,0},{64,32},{96,64},{0,96},{33,1},{65,33},{97,65},{1,97},{34,2}... | collective-permute-start | bytes 8650760 | tf_op jit(solution)/shard_map/ppermute | solution.py:173
  20.5 119.1 %collective-permute-start.2 = (bf16[128,2,2560]{2,1,0:T(2,128)(2,1)}, bf16[128,2,2560]{2,1,0:T(2,128)(2,1)S(1)}, u32[]{:S(2)}, u32[]{:S(2)}) collective-permute-start(bf16[128,2,2560]{2,1,0:T(2,128)(2,1)} %cut_grads.3), channel_id=1, source_target_pairs={{32,0},{64,32},{96,64},{0,96},{33,1},{65,33},{97,65},{1,97},{34,2}... | collective-permute-start | bytes 3932168 | tf_op jit(solution)/shard_map/ppermute | solution.py:173
  92.6 76.5 %all-to-all-start = ((bf16[32,32,2816]{2,1,0:T(8,128)(2,1)}), bf16[32,32,2816]{2,1,0:T(8,128)(2,1)}, u32[]{:S(2)}, u32[]{:S(2)}) async-start(bf16[32,32,2816]{2,1,0:T(8,128)(2,1)} %bitcast.47), calls=%async_computation | async-start | bytes 11534336 | tf_op jit(solution)/shard_map/all_to_all | solution.py:24
  139.6 1.1 copy-start.2
  169.1 40.1 %all-to-all-start.2 = ((bf16[32,32,1280]{2,1,0:T(8,128)(2,1)}), bf16[32,32,1280]{2,1,0:T(8,128)(2,1)S(1)}, u32[]{:S(2)}, u32[]{:S(2)}) async-start(bf16[32,32,1280]{2,1,0:T(8,128)(2,1)} %bitcast.52), calls=%async_computation.2 | async-start | bytes 5242880 | tf_op jit(solution)/shard_map/all_to_all | solution.py:24
  219.1 46.6 %all-to-all-start.3 = ((bf16[32,32,1536]{2,1,0:T(8,128)(2,1)}), bf16[32,32,1536]{2,1,0:T(8,128)(2,1)}, u32[]{:S(2)}, u32[]{:S(2)}) async-start(bf16[32,32,1536]{2,1,0:T(8,128)(2,1)} %bitcast.54), calls=%async_computation.3 | async-start | bytes 6291456 | tf_op jit(solution)/shard_map/all_to_all | solution.py:24
  223.9 14.7 %copy-start.5 = (bf16[1024,1280]{1,0:T(8,128)(2,1)S(1)}, bf16[1024,1280]{1,0:T(8,128)(2,1)}, u32[]{:S(2)}) copy-start(bf16[1024,1280]{1,0:T(8,128)(2,1)} %multiply_convert_fusion.3) | copy-start | bytes 7864324
  246.4 24.3 %copy-start.4 = (f32[1,128,2]{1,2,0:T(2,128)S(1)}, f32[1,128,2]{1,2,0:T(2,128)}, u32[]{:S(2)}) copy-start(f32[1,128,2]{1,2,0:T(2,128)} %param.8) | copy-start | bytes 3076
  265.6 46.9 %all-to-all-start.4 = ((bf16[32,32,1536]{2,1,0:T(8,128)(2,1)}), bf16[32,32,1536]{2,1,0:T(8,128)(2,1)}, u32[]{:S(2)}, u32[]{:S(2)}) async-start(bf16[32,32,1536]{2,1,0:T(8,128)(2,1)} %bitcast.53), calls=%async_computation.4 | async-start | bytes 6291456 | tf_op jit(solution)/shard_map/all_to_all | solution.py:24
  271.0 55.4 %copy-start.1 = (bf16[1,128,3072]{2,1,0:T(8,128)(2,1)S(1)}, bf16[1,128,3072]{2,1,0:T(8,128)(2,1)}, u32[]{:S(2)}) copy-start(bf16[1,128,3072]{2,1,0:T(8,128)(2,1)} %param.5) | copy-start | bytes 2359300
  274.0 42.3 %collective-permute-start.3 = (bf16[128,1536]{1,0:T(8,128)(2,1)S(1)}, bf16[128,1536]{1,0:T(8,128)(2,1)S(1)}, u32[]{:S(2)}, u32[]{:S(2)}) collective-permute-start(bf16[128,1536]{1,0:T(8,128)(2,1)S(1)} %fusion.13), channel_id=1, source_target_pairs={{32,0},{64,32},{96,64},{0,96},{33,1},{65,33},{97,65},{1,97},{34,2}... | collective-permute-start | bytes 1179656 | tf_op jit(solution)/shard_map/ppermute | solution.py:205
  315.5 10.0 %collective-permute-start.4 = (bf16[128,1536]{1,0:T(8,128)(2,1)S(1)}, bf16[128,1536]{1,0:T(8,128)(2,1)S(1)}, u32[]{:S(2)}, u32[]{:S(2)}) collective-permute-start(bf16[128,1536]{1,0:T(8,128)(2,1)S(1)} %fusion.12), channel_id=1, source_target_pairs={{32,0},{64,32},{96,64},{0,96},{33,1},{65,33},{97,65},{1,97},{34,2}... | collective-permute-start | bytes 1179656 | tf_op jit(solution)/shard_map/ppermute | solution.py:205
